TPU v7x, 32 devices: a whole 2x2x4 slice. The times are simulated.
32 devices in a mesh: dp: 4 (over z), expert: 4 (over y, core), tensor: 2 (over x).
Axes of the slice: x: 2, y: 2, z: 4, core: 2. Of those that a mesh axis runs over, the one named last changes fastest.
Arguments:
- tokens: bfloat16 [1024, 3072], P('expert', 'dp'), may hold values from -6 to 6
- route_ids: int32 [1024, 2], P('expert'), may hold values from 0 to 3, all different within a row; in each aligned block of 256 rows (0 to 255, 256 to 511, ...) at most 128 rows name the same one
- gates: float32 [1024, 2], P('expert'), may hold values from 0.2 to 1
- w_gate: bfloat16 [4, 3072, 8192], P('expert', 'dp', 'tensor'), may hold values from -0.109375 to 0.109375
- w_up: bfloat16 [4, 3072, 8192], P('expert', 'dp', 'tensor'), may hold values from -0.109375 to 0.109375
- w_down: bfloat16 [4, 8192, 3072], P('expert', 'tensor', 'dp'), may hold values from -0.0625 to 0.0625
Outputs:
- mixed: bfloat16 [1024, 3072], P('expert', 'dp')
Inputs may be any that keep to these rules, and one draw needn't show every extreme that they name: `route_ids`: each token names two different experts. Among the 256 tokens of one index of expert, no expert is named by more than 128 tokens, a bound that some block reaches.
All inputs are finite; a program needn't handle non-finite values.
Results may differ from a plain program's by a relative error of at most 0.025.
Values may be sent and summed in bfloat16 or wider, within the bound.
No kernel may reach another device: no remote copies, remote signals or barrier semaphores. Data moves between devices by JAX's collectives and lax.ppermute only.
A program may use at most 64 MiB of HBM per device.

v0:
```python
import jax
import jax.numpy as jnp
from jax import lax
from jax.experimental import pallas as pl
from jax.experimental.pallas import tpu as pltpu
from jax.sharding import PartitionSpec as P

F32, BF16 = jnp.float32, jnp.bfloat16
CHUNK = 32


def places_of(ids, experts):
    n = ids.shape[1]
    hits = ids[:, None, :] == jnp.arange(experts, dtype=jnp.int32)[None, :, None]
    named = (hits[0] | hits[1]).astype(BF16)
    earlier = (jnp.arange(n)[:, None] < jnp.arange(n)[None, :]).astype(BF16)
    before = jnp.dot(named, earlier, preferred_element_type=F32)
    rank = jnp.sum(jnp.where(hits, before[None], 0.0), axis=1).astype(jnp.int32)
    return rank * experts + ids


def chunk_order(experts, per):
    head = max(1, per // 2)
    order = [(0, i) for i in range(head)]
    order += [(j, i) for j in range(1, experts) for i in range(per)]
    return order + [(0, i) for i in range(head, per)]


def pick(options, index):
    out = options[-1]
    for k in range(len(options) - 2, -1, -1):
        out = jnp.where(index == k, options[k], out)
    return out


WHOLE = pl.BlockSpec(memory_space=pltpu.VMEM)
SCALAR = pl.BlockSpec(memory_space=pltpu.SMEM)
LIGHT = pl.CostEstimate(flops=0, bytes_accessed=0, transcendentals=0)


def call(body, name, shapes, *args):
    specs = [SCALAR if a.dtype == jnp.int32 else WHOLE for a in args]
    return pl.pallas_call(
        body,
        name=name,
        out_shape=shapes,
        in_specs=specs,
        out_specs=[WHOLE] * len(shapes),
        cost_estimate=LIGHT,
        compiler_params=pltpu.CompilerParams(vmem_limit_bytes=16 * 2**20),
    )(*args)


def width_of(columns):
    return 512 if columns % 512 == 0 else columns


def over_columns(columns, step):
    wide = width_of(columns)

    def body(i, carry):
        step(pl.ds(pl.multiple_of(i * wide, wide), wide))
        return carry

    lax.fori_loop(0, columns // wide, body, 0)


def combine(m, units, f, first, came, partial, act, summing, sending, fresh, owner):
    args, use = [], {}

    def take(key, value):
        if value is not None:
            use[key] = len(args)
            args.append(value)

    take("owner", owner if act is not None and came is not None else None)
    take("came", came)
    if summing:
        take("g", partial[0])
        take("u", partial[1])
    take("act", act)
    sums = 2 * m if summing and sending else 0
    hidden = act is not None or (came is not None and came.shape[0] % (2 * m) == m)
    rows = sums + (m if hidden else 0)
    shapes = []
    if rows:
        shapes.append(jax.ShapeDtypeStruct((rows, units), BF16))
    if fresh:
        shapes.append(jax.ShapeDtypeStruct((m, units), BF16))

    def body(*refs):
        ins, outs = refs[: len(args)], refs[len(args) :]
        message = outs[0] if rows else None

        def get(key):
            return ins[use[key]] if key in use else None

        came_ref, act_ref = get("came"), get("act")

        def step(cols):
            if summing:
                total = []
                for k, key in enumerate(("g", "u")):
                    value = get(key)[f * m : (f + 1) * m, cols].astype(F32)
                    if not first:
                        value = value + came_ref[k * m : (k + 1) * m, cols].astype(F32)
                    total.append(value)
                    if sending:
                        message[k * m : (k + 1) * m, cols] = value.astype(BF16)
                if fresh:
                    outs[-1][:, cols] = (total[0] / (1.0 + jnp.exp(-total[0])) * total[1]).astype(BF16)
            if hidden:
                if act_ref is None:
                    h = came_ref[came.shape[0] - m :, cols]
                elif "owner" in use:
                    h = jnp.where(get("owner")[0] != 0, act_ref[:, cols], came_ref[came.shape[0] - m :, cols])
                else:
                    h = act_ref[:, cols]
                message[sums:, cols] = h

        over_columns(units, step)

    return call(body, "combine", shapes, *args)


def project(block, wg, wu, tie):
    def body(*refs):
        x_ref, g_w, u_w = refs[:3]
        g_ref, u_ref = refs[-2:]

        def step(cols):
            x = x_ref[...]
            g_ref[:, cols] = jnp.dot(x, g_w[:, cols], preferred_element_type=F32).astype(BF16)
            u_ref[:, cols] = jnp.dot(x, u_w[:, cols], preferred_element_type=F32).astype(BF16)

        over_columns(wg.shape[1], step)

    shape = jax.ShapeDtypeStruct((block.shape[0], wg.shape[1]), BF16)
    return call(body, "project", [shape, shape], block, wg, wu, *tie)


def lower(m, one, two, wd):
    def body(one_ref, two_ref, w_ref, out_ref):
        def step(cols):
            h = jnp.concatenate([r[r.shape[0] - m :, :] for r in (one_ref, two_ref)])
            out_ref[:, cols] = jnp.dot(h, w_ref[:, cols], preferred_element_type=F32).astype(BF16)

        columns = wd.shape[1]
        wide = 256 if columns % 256 == 0 else columns

        def loop(i, carry):
            step(pl.ds(pl.multiple_of(i * wide, wide), wide))
            return carry

        lax.fori_loop(0, columns // wide, loop, 0)

    shape = jax.ShapeDtypeStruct((2 * m, wd.shape[1]), BF16)
    return call(body, "lower", [shape], one, two, wd)[0]


def local(tokens, route_ids, gates, w_gate, w_up, w_down):
    experts = lax.axis_size("expert")
    depth = lax.axis_size("dp")
    tensors = lax.axis_size("tensor")
    z = lax.axis_index("dp")
    e = lax.axis_index("expert")
    n, width = tokens.shape
    units = w_gate.shape[2]
    capacity = max(3 * n // 8, 2 * n // experts)
    capacity = (capacity + 15) // 16 * 16
    half = capacity // 2
    m = CHUNK if half % CHUNK == 0 else 16
    per = half // m
    order = chunk_order(experts, per)
    chunks = len(order)
    last = depth - 1

    even = e % 2 == 0
    spot = [jnp.where(even, z, last - z), jnp.where(even, last - z, z)]
    climb = [(a * experts + b, (a + 1) * experts + b) for a in range(last) for b in range(experts)]
    flows = [
        [(a, c) if a % experts % 2 == f else (c, a) for a, c in climb] for f in range(2)
    ]

    places = places_of(route_ids.T, experts)

    def rows_for(j, tie=None):
        lines = jnp.arange(capacity, dtype=jnp.int32) * experts + (e ^ j)
        chosen = (lines[:, None] == places[0][None, :]) | (lines[:, None] == places[1][None, :])
        if tie is not None:
            chosen = chosen & ~jnp.isnan(tie)
        picked = jnp.dot(chosen.astype(BF16), tokens, preferred_element_type=F32).astype(BF16)
        if j:
            picked = lax.ppermute(picked, "expert", [(a, a ^ j) for a in range(experts)])
        return picked

    rows = [rows_for(0)] + [None] * (experts - 1)
    nothing = jnp.zeros((m, width), BF16)

    def chunk_rows(index, f):
        if not 0 <= index < chunks:
            return nothing
        j, i = order[index]
        return lax.slice_in_dim(rows[j], f * half + i * m, f * half + (i + 1) * m)

    wg, wu, wd = w_gate[0], w_up[0], w_down[0]
    sums_end = chunks + last
    owners = [(spot[f] == 0).astype(jnp.int32).reshape(1) for f in range(2)]
    got = [None, None]
    act = [None, None]
    held = [{}, {}]
    outs = []
    partial = None

    def round_rows(s):
        return jnp.concatenate(
            [pick([chunk_rows(s - a, f) for a in range(depth)], spot[f]) for f in range(2)]
        )

    partial = project(round_rows(0), wg, wu, ())
    for s in range(chunks + 2 * last + 1):
        summing = s < sums_end
        for f in range(2):
            o = 1 - f
            first = last + 1 if f == 0 else last
            carries = first <= s < first + chunks + last
            came = got[f] if s else None
            if not (summing or carries):
                continue
            result = combine(
                m,
                units,
                f,
                s == 0,
                came,
                partial,
                act[o] if carries else None,
                summing,
                s < sums_end - 1,
                summing and s >= last,
                owners[f],
            )
            message = result[0]
            fresh = result[-1] if summing and s >= last else None
            act[f] = fresh
            if carries:
                held[o][s - first] = message
            if s < sums_end - 1 or (carries and s < first + chunks + last - 1):
                got[f] = lax.ppermute(message, ("dp", "expert"), flows[f])
            if f == 0:
                climbing = message
            else:
                for j in range(1, experts):
                    if max(0, order.index((j, 0)) - 2) == s:
                        rows[j] = rows_for(j, message[:1, :1])
            if f == 0 and carries:
                outs.append(lower(m, held[0][s - first], message, wd))
        if s + 1 < sums_end:
            partial = project(round_rows(s + 1), wg, wu, (climbing,))

    def across(part):
        if tensors == 2:
            other = lax.ppermute(part, "tensor", [(0, 1), (1, 0)])
            return (part.astype(F32) + other.astype(F32)).astype(BF16)
        return lax.psum(part, "tensor")

    def finished(start, stop):
        return [
            jnp.concatenate(
                [
                    pick([outs[c + a][f * m : (f + 1) * m] for a in range(depth)], spot[1 - f])
                    for c in range(start, stop)
                ]
            )
            for f in range(2)
        ]

    yields = [jnp.zeros((n, width), F32), jnp.zeros((n, width), F32)]
    spans = []
    for index, (j, i) in enumerate(order):
        if spans and spans[-1][0] == j:
            spans[-1][2] = index + 1
        else:
            spans.append([j, index, index + 1, i])
    for j, start, stop, i in spans:
        size = (stop - start) * m
        part = across(jnp.concatenate(finished(start, stop)))
        if j:
            part = lax.ppermute(part, "expert", [(a, a ^ j) for a in range(experts)])
        ranks = jnp.arange(size, dtype=jnp.int32) + i * m
        ranks = jnp.concatenate([ranks, ranks + half])
        label = ranks * experts + (e ^ j)
        for k in range(2):
            chosen = (label[:, None] == places[k][None, :]).astype(BF16)
            yields[k] += lax.dot_general(
                chosen, part, (((0,), (0,)), ((), ())), preferred_element_type=F32
            )
    mixed = gates[:, 0:1] * yields[0] + gates[:, 1:2] * yields[1]
    return mixed.astype(BF16)


def solution(mesh):
    return jax.shard_map(
        local,
        mesh=mesh,
        in_specs=(
            P("expert", "dp"),
            P("expert", None),
            P("expert", None),
            P("expert", "dp", "tensor"),
            P("expert", "dp", "tensor"),
            P("expert", "tensor", "dp"),
        ),
        out_specs=P("expert", "dp"),
        check_vma=False,
    )
```

profile of v0, /device:TPU:0, one launch (start us, length us, event | category | flops | bytes accessed | tf_op | source)
XLA Modules:
  0.0 275.0 jit_solution(7369581273101219010)
XLA Ops:
  3.3 2.8 %copy-done.2 = bf16[1,768,4096]{2,1,0:T(8,128)(2,1)S(1)} copy-done((bf16[1,768,4096]{2,1,0:T(8,128)(2,1)S(1)}, bf16[1,768,4096]{2,1,0:T(8,128)(2,1)}, u32[]{:S(2)}) %copy-start.2) | copy-done | bytes 6291480
  6.1 2.8 %copy-done.8 = bf16[1,768,4096]{2,1,0:T(8,128)(2,1)S(1)} copy-done((bf16[1,768,4096]{2,1,0:T(8,128)(2,1)S(1)}, bf16[1,768,4096]{2,1,0:T(8,128)(2,1)}, u32[]{:S(2)}) %copy-start.8) | copy-done | bytes 6291480
  8.9 3.2 %project.11 = (bf16[64,4096]{1,0:T(8,128)(2,1)S(1)}, bf16[64,4096]{1,0:T(8,128)(2,1)S(1)}) custom-call(bf16[64,768]{1,0:T(8,128)(2,1)S(1)} %pad_maximum_fusion.3.refs_0_, bf16[768,4096]{1,0:T(8,128)(2,1)S(1)} %bitcast.27, bf16[768,4096]{1,0:T(8,128)(2,1)S(1)} %bitcast.40), custom_call_target="tpu_custom_call" | custom-call | tf_op jit(solution)/shard_map/project/pallas_call | solution.py:43
  16.1 5.2 %collective-permute-start.3 = (bf16[64,4096]{1,0:T(8,128)(2,1)S(1)}, bf16[64,4096]{1,0:T(8,128)(2,1)S(1)}, u32[]{:S(2)}, u32[]{:S(2)}) collective-permute-start(bf16[64,4096]{1,0:T(8,128)(2,1)S(1)} %combine.30.refs_3_), channel_id=1, source_target_pairs={{0,8},{10,2},{4,12},{14,6},{8,16},{18,10},{12,20},{22,14},{16,24},... | collective-permute-start | bytes 1572872 | tf_op jit(solution)/shard_map/ppermute | solution.py:249
  21.3 2.8 %copy-done.3 = bf16[1,768,4096]{2,1,0:T(8,128)(2,1)S(1)} copy-done((bf16[1,768,4096]{2,1,0:T(8,128)(2,1)S(1)}, bf16[1,768,4096]{2,1,0:T(8,128)(2,1)}, u32[]{:S(2)}) %copy-start.3) | copy-done | bytes 6291480
  24.1 2.8 %copy-done.9 = bf16[1,768,4096]{2,1,0:T(8,128)(2,1)S(1)} copy-done((bf16[1,768,4096]{2,1,0:T(8,128)(2,1)S(1)}, bf16[1,768,4096]{2,1,0:T(8,128)(2,1)}, u32[]{:S(2)}) %copy-start.9) | copy-done | bytes 6291480
  26.9 3.2 %project.12 = (bf16[64,4096]{1,0:T(8,128)(2,1)S(1)}, bf16[64,4096]{1,0:T(8,128)(2,1)S(1)}) custom-call(bf16[64,768]{1,0:T(8,128)(2,1)S(1)} %pad_maximum_fusion.4.refs_0_, bf16[768,4096]{1,0:T(8,128)(2,1)S(1)} %bitcast.28, bf16[768,4096]{1,0:T(8,128)(2,1)S(1)} %bitcast.41, bf16[64,4096]{1,0:T(8,128)(2,1)S(1)} %combine.30.refs_3_), custom_call_target="tpu_custom_call" | custom-call | tf_op jit(solution)/shard_map/project/pallas_call | solution.py:43
  32.3 2.0 collective-permute-start.5
  34.5 3.5 %collective-permute-start.6 = (bf16[64,4096]{1,0:T(8,128)(2,1)S(1)}, bf16[64,4096]{1,0:T(8,128)(2,1)S(1)}, u32[]{:S(2)}, u32[]{:S(2)}) collective-permute-start(bf16[64,4096]{1,0:T(8,128)(2,1)S(1)} %combine.32.refs_3_), channel_id=1, source_target_pairs={{0,8},{10,2},{4,12},{14,6},{8,16},{18,10},{12,20},{22,14},{16,24},... | collective-permute-start | bytes 1572872 | tf_op jit(solution)/shard_map/ppermute | solution.py:249
  40.1 2.8 %copy-done.4 = bf16[1,768,4096]{2,1,0:T(8,128)(2,1)S(1)} copy-done((bf16[1,768,4096]{2,1,0:T(8,128)(2,1)S(1)}, bf16[1,768,4096]{2,1,0:T(8,128)(2,1)}, u32[]{:S(2)}) %copy-start.4) | copy-done | bytes 6291480
  42.8 3.2 %project.13 = (bf16[64,4096]{1,0:T(8,128)(2,1)S(1)}, bf16[64,4096]{1,0:T(8,128)(2,1)S(1)}) custom-call(bf16[64,768]{1,0:T(8,128)(2,1)S(1)} %pad_maximum_fusion.5.refs_0_, bf16[768,4096]{1,0:T(8,128)(2,1)S(1)} %bitcast.29, bf16[768,4096]{1,0:T(8,128)(2,1)S(1)} %bitcast.42, bf16[64,4096]{1,0:T(8,128)(2,1)S(1)} %combine.32.refs_3_), custom_call_target="tpu_custom_call" | custom-call | tf_op jit(solution)/shard_map/project/pallas_call | solution.py:43
  46.0 3.7 %collective-permute-done.6.refs_0_ = bf16[64,4096]{1,0:T(8,128)(2,1)S(1)} collective-permute-done((bf16[64,4096]{1,0:T(8,128)(2,1)S(1)}, bf16[64,4096]{1,0:T(8,128)(2,1)S(1)}, u32[]{:S(2)}, u32[]{:S(2)}) %collective-permute-start.6) | collective-permute-done | bytes 524320 | tf_op jit(solution)/shard_map/ppermute | solution.py:249
  49.9 4.4 %collective-permute-start.7 = (bf16[64,4096]{1,0:T(8,128)(2,1)S(1)}, bf16[64,4096]{1,0:T(8,128)(2,1)S(1)}, u32[]{:S(2)}, u32[]{:S(2)}) collective-permute-start(bf16[64,4096]{1,0:T(8,128)(2,1)S(1)} %combine.34.refs_3_), channel_id=1, source_target_pairs={{0,8},{10,2},{4,12},{14,6},{8,16},{18,10},{12,20},{22,14},{16,24},... | collective-permute-start | bytes 1572872 | tf_op jit(solution)/shard_map/ppermute | solution.py:249
  55.8 2.8 %copy-done.5 = bf16[1,768,4096]{2,1,0:T(8,128)(2,1)S(1)} copy-done((bf16[1,768,4096]{2,1,0:T(8,128)(2,1)S(1)}, bf16[1,768,4096]{2,1,0:T(8,128)(2,1)}, u32[]{:S(2)}) %copy-start.5) | copy-done | bytes 6291480
  58.6 3.2 %project.14 = (bf16[64,4096]{1,0:T(8,128)(2,1)S(1)}, bf16[64,4096]{1,0:T(8,128)(2,1)S(1)}) custom-call(bf16[64,768]{1,0:T(8,128)(2,1)S(1)} %pad_maximum_fusion.6.refs_0_, bf16[768,4096]{1,0:T(8,128)(2,1)S(1)} %bitcast.30, bf16[768,4096]{1,0:T(8,128)(2,1)S(1)} %bitcast.43, bf16[64,4096]{1,0:T(8,128)(2,1)S(1)} %combine.34.refs_3_), custom_call_target="tpu_custom_call" | custom-call | tf_op jit(solution)/shard_map/project/pallas_call | solution.py:43
  61.7 4.3 %collective-permute-done.7.refs_0_ = bf16[64,4096]{1,0:T(8,128)(2,1)S(1)} collective-permute-done((bf16[64,4096]{1,0:T(8,128)(2,1)S(1)}, bf16[64,4096]{1,0:T(8,128)(2,1)S(1)}, u32[]{:S(2)}, u32[]{:S(2)}) %collective-permute-start.7) | collective-permute-done | bytes 524320 | tf_op jit(solution)/shard_map/ppermute | solution.py:249
  67.0 4.4 %collective-permute-start.8 = (bf16[64,4096]{1,0:T(8,128)(2,1)S(1)}, bf16[64,4096]{1,0:T(8,128)(2,1)S(1)}, u32[]{:S(2)}, u32[]{:S(2)}) collective-permute-start(bf16[64,4096]{1,0:T(8,128)(2,1)S(1)} %get-tuple-element.69.refs_3_), channel_id=1, source_target_pairs={{0,8},{10,2},{4,12},{14,6},{8,16},{18,10},{12,20},{22,14},{16,24},... | collective-permute-start | bytes 1572872 | tf_op jit(solution)/shard_map/ppermute | solution.py:249
  75.1 2.8 %copy-done.6 = bf16[1,768,4096]{2,1,0:T(8,128)(2,1)S(1)} copy-done((bf16[1,768,4096]{2,1,0:T(8,128)(2,1)S(1)}, bf16[1,768,4096]{2,1,0:T(8,128)(2,1)}, u32[]{:S(2)}) %copy-start.6) | copy-done | bytes 6291480
  77.8 2.8 %copy-done.10 = bf16[1,768,4096]{2,1,0:T(8,128)(2,1)S(1)} copy-done((bf16[1,768,4096]{2,1,0:T(8,128)(2,1)S(1)}, bf16[1,768,4096]{2,1,0:T(8,128)(2,1)}, u32[]{:S(2)}) %copy-start.10) | copy-done | bytes 6291480
  80.6 3.2 %project.15 = (bf16[64,4096]{1,0:T(8,128)(2,1)S(1)}, bf16[64,4096]{1,0:T(8,128)(2,1)S(1)}) custom-call(bf16[64,768]{1,0:T(8,128)(2,1)S(1)} %pad_maximum_fusion.7.refs_0_, bf16[768,4096]{1,0:T(8,128)(2,1)S(1)} %bitcast.31, bf16[768,4096]{1,0:T(8,128)(2,1)S(1)} %bitcast.44, bf16[64,4096]{1,0:T(8,128)(2,1)S(1)} %get-tuple-element.69.refs_3_), custom_call_target="tpu_custom_call" | custom-call | tf_op jit(solution)/shard_map/project/pallas_call | solution.py:43
  84.1 4.6 %collective-permute-start.10 = (bf16[96,4096]{1,0:T(8,128)(2,1)S(1)}, bf16[96,4096]{1,0:T(8,128)(2,1)S(1)}, u32[]{:S(2)}, u32[]{:S(2)}) collective-permute-start(bf16[96,4096]{1,0:T(8,128)(2,1)S(1)} %get-tuple-element.73.two_ref.refs_3_), channel_id=1, source_target_pairs={{0,8},{10,2},{4,12},{14,6},{8,16},{18,10},{12,20},{22,14},{16,24},... | collective-permute-start | bytes 2359304 | tf_op jit(solution)/shard_map/ppermute | solution.py:249
  90.9 6.3 %collective-permute-done.11 = bf16[128,768]{1,0:T(8,128)(2,1)S(1)} collective-permute-done((bf16[128,768]{1,0:T(8,128)(2,1)S(1)}, bf16[128,768]{1,0:T(8,128)(2,1)S(1)}, u32[]{:S(2)}, u32[]{:S(2)}) %collective-permute-start.11) | collective-permute-done | bytes 196640 | tf_op jit(solution)/shard_map/ppermute | solution.py:194
  97.2 2.8 %copy-done.7 = bf16[1,768,4096]{2,1,0:T(8,128)(2,1)S(1)} copy-done((bf16[1,768,4096]{2,1,0:T(8,128)(2,1)S(1)}, bf16[1,768,4096]{2,1,0:T(8,128)(2,1)}, u32[]{:S(2)}) %copy-start.7) | copy-done | bytes 6291480
  100.0 3.2 %project.16 = (bf16[64,4096]{1,0:T(8,128)(2,1)S(1)}, bf16[64,4096]{1,0:T(8,128)(2,1)S(1)}) custom-call(bf16[64,768]{1,0:T(8,128)(2,1)S(1)} %pad_maximum_fusion.8.refs_0_, bf16[768,4096]{1,0:T(8,128)(2,1)S(1)} %bitcast.32, bf16[768,4096]{1,0:T(8,128)(2,1)S(1)} %bitcast.45, bf16[96,4096]{1,0:T(8,128)(2,1)S(1)} %get-tuple-element.73.two_ref.refs_3_), custom_call_target="tpu_custom_call" | custom-call | tf_op jit(solution)/shard_map/project/pallas_call | solution.py:43
  105.1 4.6 %collective-permute-start.13 = (bf16[96,4096]{1,0:T(8,128)(2,1)S(1)}, bf16[96,4096]{1,0:T(8,128)(2,1)S(1)}, u32[]{:S(2)}, u32[]{:S(2)}) collective-permute-start(bf16[96,4096]{1,0:T(8,128)(2,1)S(1)} %get-tuple-element.79.two_ref.refs_3_), channel_id=1, source_target_pairs={{0,8},{10,2},{4,12},{14,6},{8,16},{18,10},{12,20},{22,14},{16,24},... | collective-permute-start | bytes 2359304 | tf_op jit(solution)/shard_map/ppermute | solution.py:249
  109.8 3.2 %project.17 = (bf16[64,4096]{1,0:T(8,128)(2,1)S(1)}, bf16[64,4096]{1,0:T(8,128)(2,1)S(1)}) custom-call(bf16[64,768]{1,0:T(8,128)(2,1)S(1)} %pad_maximum_fusion.9.refs_0_, bf16[768,4096]{1,0:T(8,128)(2,1)S(1)} %bitcast.35, bf16[768,4096]{1,0:T(8,128)(2,1)S(1)} %bitcast.46, bf16[96,4096]{1,0:T(8,128)(2,1)S(1)} %get-tuple-element.79.two_ref.refs_3_), custom_call_target="tpu_custom_call" | custom-call | tf_op jit(solution)/shard_map/project/pallas_call | solution.py:43
  113.0 11.0 %collective-permute-done.12.refs_1_ = bf16[96,4096]{1,0:T(8,128)(2,1)S(1)} collective-permute-done((bf16[96,4096]{1,0:T(8,128)(2,1)S(1)}, bf16[96,4096]{1,0:T(8,128)(2,1)S(1)}, u32[]{:S(2)}, u32[]{:S(2)}) %collective-permute-start.12) | collective-permute-done | bytes 786464 | tf_op jit(solution)/shard_map/ppermute | solution.py:249
  125.9 5.4 %collective-permute-start.15 = (bf16[96,4096]{1,0:T(8,128)(2,1)S(1)}, bf16[96,4096]{1,0:T(8,128)(2,1)S(1)}, u32[]{:S(2)}, u32[]{:S(2)}) collective-permute-start(bf16[96,4096]{1,0:T(8,128)(2,1)S(1)} %get-tuple-element.85.two_ref.refs_3_), channel_id=1, source_target_pairs={{0,8},{10,2},{4,12},{14,6},{8,16},{18,10},{12,20},{22,14},{16,24},... | collective-permute-start | bytes 2359304 | tf_op jit(solution)/shard_map/ppermute | solution.py:249
  131.4 3.2 %project.18 = (bf16[64,4096]{1,0:T(8,128)(2,1)S(1)}, bf16[64,4096]{1,0:T(8,128)(2,1)S(1)}) custom-call(bf16[64,768]{1,0:T(8,128)(2,1)S(1)} %pad_maximum_fusion.10.refs_0_, bf16[768,4096]{1,0:T(8,128)(2,1)S(1)} %bitcast.36, bf16[768,4096]{1,0:T(8,128)(2,1)S(1)} %bitcast.47, bf16[96,4096]{1,0:T(8,128)(2,1)S(1)} %get-tuple-element.85.two_ref.refs_3_), custom_call_target="tpu_custom_call" | custom-call | tf_op jit(solution)/shard_map/project/pallas_call | solution.py:43
  134.6 12.7 %collective-permute-done.14.refs_1_ = bf16[96,4096]{1,0:T(8,128)(2,1)S(1)} collective-permute-done((bf16[96,4096]{1,0:T(8,128)(2,1)S(1)}, bf16[96,4096]{1,0:T(8,128)(2,1)S(1)}, u32[]{:S(2)}, u32[]{:S(2)}) %collective-permute-start.14) | collective-permute-done | bytes 786464 | tf_op jit(solution)/shard_map/ppermute | solution.py:249
  149.2 4.6 %collective-permute-start.18 = (bf16[96,4096]{1,0:T(8,128)(2,1)S(1)}, bf16[96,4096]{1,0:T(8,128)(2,1)S(1)}, u32[]{:S(2)}, u32[]{:S(2)}) collective-permute-start(bf16[96,4096]{1,0:T(8,128)(2,1)S(1)} %get-tuple-element.91.two_ref.refs_3_), channel_id=1, source_target_pairs={{0,8},{10,2},{4,12},{14,6},{8,16},{18,10},{12,20},{22,14},{16,24},... | collective-permute-start | bytes 2359304 | tf_op jit(solution)/shard_map/ppermute | solution.py:249
  154.0 3.2 %project.19 = (bf16[64,4096]{1,0:T(8,128)(2,1)S(1)}, bf16[64,4096]{1,0:T(8,128)(2,1)S(1)}) custom-call(bf16[64,768]{1,0:T(8,128)(2,1)S(1)} %pad_maximum_fusion.12.refs_0_, bf16[768,4096]{1,0:T(8,128)(2,1)S(1)} %bitcast.37, bf16[768,4096]{1,0:T(8,128)(2,1)S(1)} %bitcast.48, bf16[96,4096]{1,0:T(8,128)(2,1)S(1)} %get-tuple-element.91.two_ref.refs_3_), custom_call_target="tpu_custom_call" | custom-call | tf_op jit(solution)/shard_map/project/pallas_call | solution.py:43
  157.2 11.6 %collective-permute-done.17.refs_1_ = bf16[96,4096]{1,0:T(8,128)(2,1)S(1)} collective-permute-done((bf16[96,4096]{1,0:T(8,128)(2,1)S(1)}, bf16[96,4096]{1,0:T(8,128)(2,1)S(1)}, u32[]{:S(2)}, u32[]{:S(2)}) %collective-permute-start.17) | collective-permute-done | bytes 786464 | tf_op jit(solution)/shard_map/ppermute | solution.py:249
  170.8 4.6 %collective-permute-start.20 = (bf16[96,4096]{1,0:T(8,128)(2,1)S(1)}, bf16[96,4096]{1,0:T(8,128)(2,1)S(1)}, u32[]{:S(2)}, u32[]{:S(2)}) collective-permute-start(bf16[96,4096]{1,0:T(8,128)(2,1)S(1)} %get-tuple-element.97.two_ref.refs_3_), channel_id=1, source_target_pairs={{0,8},{10,2},{4,12},{14,6},{8,16},{18,10},{12,20},{22,14},{16,24},... | collective-permute-start | bytes 2359304 | tf_op jit(solution)/shard_map/ppermute | solution.py:249
  175.6 1.5 lower.12
  177.0 1.5 lower.13
  178.5 1.5 lower.14
  180.0 1.5 lower.15
  181.8 3.2 %project.20 = (bf16[64,4096]{1,0:T(8,128)(2,1)S(1)}, bf16[64,4096]{1,0:T(8,128)(2,1)S(1)}) custom-call(bf16[64,768]{1,0:T(8,128)(2,1)S(1)} %pad_maximum_fusion.13.refs_0_, bf16[768,4096]{1,0:T(8,128)(2,1)S(1)} %bitcast.38, bf16[768,4096]{1,0:T(8,128)(2,1)S(1)} %bitcast.51, bf16[96,4096]{1,0:T(8,128)(2,1)S(1)} %get-tuple-element.97.two_ref.refs_3_), custom_call_target="tpu_custom_call" | custom-call | tf_op jit(solution)/shard_map/project/pallas_call | solution.py:43
  185.0 4.6 %collective-permute-done.19.refs_1_ = bf16[96,4096]{1,0:T(8,128)(2,1)S(1)} collective-permute-done((bf16[96,4096]{1,0:T(8,128)(2,1)S(1)}, bf16[96,4096]{1,0:T(8,128)(2,1)S(1)}, u32[]{:S(2)}, u32[]{:S(2)}) %collective-permute-start.19) | collective-permute-done | bytes 786464 | tf_op jit(solution)/shard_map/ppermute | solution.py:249
  191.5 1.5 lower.16
  193.0 4.6 %collective-permute-start.24 = (bf16[96,4096]{1,0:T(8,128)(2,1)S(1)}, bf16[96,4096]{1,0:T(8,128)(2,1)S(1)}, u32[]{:S(2)}, u32[]{:S(2)}) collective-permute-start(bf16[96,4096]{1,0:T(8,128)(2,1)S(1)} %get-tuple-element.103.two_ref.refs_3_), channel_id=1, source_target_pairs={{0,8},{10,2},{4,12},{14,6},{8,16},{18,10},{12,20},{22,14},{16,24},... | collective-permute-start | bytes 2359304 | tf_op jit(solution)/shard_map/ppermute | solution.py:249
  197.6 1.6 collective-permute-start.21
  199.2 1.5 lower.11
  200.7 2.7 collective-permute-done.21
  203.5 7.3 %collective-permute-done.23.refs_1_ = bf16[96,4096]{1,0:T(8,128)(2,1)S(1)} collective-permute-done((bf16[96,4096]{1,0:T(8,128)(2,1)S(1)}, bf16[96,4096]{1,0:T(8,128)(2,1)S(1)}, u32[]{:S(2)}, u32[]{:S(2)}) %collective-permute-start.23) | collective-permute-done | bytes 786464 | tf_op jit(solution)/shard_map/ppermute | solution.py:249
  212.5 1.6 collective-permute-start.16
  214.1 3.2 %project.21 = (bf16[64,4096]{1,0:T(8,128)(2,1)S(1)}, bf16[64,4096]{1,0:T(8,128)(2,1)S(1)}) custom-call(bf16[64,768]{1,0:T(8,128)(2,1)S(1)} %pad_maximum_fusion.14.refs_0_, bf16[768,4096]{1,0:T(8,128)(2,1)S(1)} %bitcast.39, bf16[768,4096]{1,0:T(8,128)(2,1)S(1)} %bitcast.52, bf16[96,4096]{1,0:T(8,128)(2,1)S(1)} %get-tuple-element.103.two_ref.refs_3_), custom_call_target="tpu_custom_call" | custom-call | tf_op jit(solution)/shard_map/project/pallas_call | solution.py:43
  217.6 4.6 %collective-permute-start.26 = (bf16[32,4096]{1,0:T(8,128)(2,1)S(1)}, bf16[32,4096]{1,0:T(8,128)(2,1)S(1)}, u32[]{:S(2)}, u32[]{:S(2)}) collective-permute-start(bf16[32,4096]{1,0:T(8,128)(2,1)S(1)} %get-tuple-element.109.two_ref), channel_id=1, source_target_pairs={{0,8},{10,2},{4,12},{14,6},{8,16},{18,10},{12,20},{22,14},{16,24},... | collective-permute-start | bytes 786440 | tf_op jit(solution)/shard_map/ppermute | solution.py:249
  222.5 1.5 lower.17
  224.1 3.1 %collective-permute-done.25.refs_1_ = bf16[96,4096]{1,0:T(8,128)(2,1)S(1)} collective-permute-done((bf16[96,4096]{1,0:T(8,128)(2,1)S(1)}, bf16[96,4096]{1,0:T(8,128)(2,1)S(1)}, u32[]{:S(2)}, u32[]{:S(2)}) %collective-permute-start.25) | collective-permute-done | bytes 786464 | tf_op jit(solution)/shard_map/ppermute | solution.py:249
  229.0 1.5 lower.18
  230.4 4.6 %collective-permute-start.30 = (bf16[32,4096]{1,0:T(8,128)(2,1)S(1)}, bf16[32,4096]{1,0:T(8,128)(2,1)S(1)}, u32[]{:S(2)}, u32[]{:S(2)}) collective-permute-start(bf16[32,4096]{1,0:T(8,128)(2,1)S(1)} %combine.51.two_ref), channel_id=1, source_target_pairs={{0,8},{10,2},{4,12},{14,6},{8,16},{18,10},{12,20},{22,14},{16,24},... | collective-permute-start | bytes 786440 | tf_op jit(solution)/shard_map/ppermute | solution.py:249
  235.9 4.9 %collective-permute-done.27 = bf16[128,768]{1,0:T(8,128)(2,1)S(1)} collective-permute-done((bf16[128,768]{1,0:T(8,128)(2,1)S(1)}, bf16[128,768]{1,0:T(8,128)(2,1)S(1)}, u32[]{:S(2)}, u32[]{:S(2)}) %collective-permute-start.27) | collective-permute-done | bytes 196640 | tf_op jit(solution)/shard_map/ppermute | solution.py:263
  240.9 2.0 collective-permute-start.28
  242.9 1.5 collective-permute-start.31
  244.5 1.5 lower.19
  245.9 4.6 %collective-permute-start.32 = (bf16[32,4096]{1,0:T(8,128)(2,1)S(1)}, bf16[32,4096]{1,0:T(8,128)(2,1)S(1)}, u32[]{:S(2)}, u32[]{:S(2)}) collective-permute-start(bf16[32,4096]{1,0:T(8,128)(2,1)S(1)} %combine.53.two_ref), channel_id=1, source_target_pairs={{0,8},{10,2},{4,12},{14,6},{8,16},{18,10},{12,20},{22,14},{16,24},... | collective-permute-start | bytes 786440 | tf_op jit(solution)/shard_map/ppermute | solution.py:249
  254.4 1.5 lower.20
  255.9 4.4 %collective-permute-start.36 = (bf16[32,4096]{1,0:T(8,128)(2,1)S(1)}, bf16[32,4096]{1,0:T(8,128)(2,1)S(1)}, u32[]{:S(2)}, u32[]{:S(2)}) collective-permute-start(bf16[32,4096]{1,0:T(8,128)(2,1)S(1)} %combine.55.two_ref), channel_id=1, source_target_pairs={{0,8},{10,2},{4,12},{14,6},{8,16},{18,10},{12,20},{22,14},{16,24},... | collective-permute-start | bytes 786440 | tf_op jit(solution)/shard_map/ppermute | solution.py:249
  261.4 2.7 collective-permute-done.36.refs_0_
  264.2 1.5 lower.21
  266.9 3.5 %collective-permute-done.37 = bf16[64,768]{1,0:T(8,128)(2,1)S(1)} collective-permute-done((bf16[64,768]{1,0:T(8,128)(2,1)S(1)}, bf16[64,768]{1,0:T(8,128)(2,1)S(1)}, u32[]{:S(2)}, u32[]{:S(2)}) %collective-permute-start.37) | collective-permute-done | bytes 98336 | tf_op jit(solution)/shard_map/ppermute | solution.py:263
  271.2 1.5 collective-permute-done.34
  (192 shorter events, 41.2 us)
Async XLA Ops:
  0.0 2.3 copy-start
  2.6 36.8 %copy-start.13 = (bf16[128,768]{1,0:T(8,128)(2,1)}, bf16[128,768]{1,0:T(8,128)(2,1)S(1)}, u32[]{:S(2)}) copy-start(bf16[128,768]{1,0:T(8,128)(2,1)S(1)} %convolution_convert_fusion.3) | copy-start | bytes 589828
  3.3 2.8 %copy-start.2 = (bf16[1,768,4096]{2,1,0:T(8,128)(2,1)S(1)}, bf16[1,768,4096]{2,1,0:T(8,128)(2,1)}, u32[]{:S(2)}) copy-start(bf16[1,768,4096]{2,1,0:T(8,128)(2,1)} %param.9) | copy-start | bytes 18874372
  6.1 2.8 %copy-start.8 = (bf16[1,768,4096]{2,1,0:T(8,128)(2,1)S(1)}, bf16[1,768,4096]{2,1,0:T(8,128)(2,1)}, u32[]{:S(2)}) copy-start(bf16[1,768,4096]{2,1,0:T(8,128)(2,1)} %param.10) | copy-start | bytes 18874372
  14.2 7.1 %collective-permute-start.1 = (bf16[128,768]{1,0:T(8,128)(2,1)S(1)}, bf16[128,768]{1,0:T(8,128)(2,1)S(1)}, u32[]{:S(2)}, u32[]{:S(2)}) collective-permute-start(bf16[128,768]{1,0:T(8,128)(2,1)S(1)} %convolution_convert_fusion.2), channel_id=1, source_target_pairs={{0,2},{2,0},{4,6},{6,4},{1,3},{3,1},{5,7},{7,5},{8,10},{10,8},{12,... | collective-permute-start | bytes 589832 | tf_op jit(solution)/shard_map/ppermute | solution.py:194
  14.7 15.4 %collective-permute-start = (bf16[64,4096]{1,0:T(8,128)(2,1)S(1)}, bf16[64,4096]{1,0:T(8,128)(2,1)S(1)}, u32[]{:S(2)}, u32[]{:S(2)}) collective-permute-start(bf16[64,4096]{1,0:T(8,128)(2,1)S(1)} %combine.29), channel_id=1, source_target_pairs={{8,0},{2,10},{12,4},{6,14},{16,8},{10,18},{20,12},{14,22},{24,16},... | collective-permute-start | bytes 1572872 | tf_op jit(solution)/shard_map/ppermute | solution.py:249
  16.1 18.3 %collective-permute-start.3 = (bf16[64,4096]{1,0:T(8,128)(2,1)S(1)}, bf16[64,4096]{1,0:T(8,128)(2,1)S(1)}, u32[]{:S(2)}, u32[]{:S(2)}) collective-permute-start(bf16[64,4096]{1,0:T(8,128)(2,1)S(1)} %combine.30.refs_3_), channel_id=1, source_target_pairs={{0,8},{10,2},{4,12},{14,6},{8,16},{18,10},{12,20},{22,14},{16,24},... | collective-permute-start | bytes 1572872 | tf_op jit(solution)/shard_map/ppermute | solution.py:249
  21.3 18.1 %copy-start.15 = (bf16[128,768]{1,0:T(8,128)(2,1)}, bf16[128,768]{1,0:T(8,128)(2,1)S(1)}, u32[]{:S(2)}) copy-start(bf16[128,768]{1,0:T(8,128)(2,1)S(1)} %collective-permute-done.1) | copy-start | bytes 589828
  21.3 2.8 %copy-start.3 = (bf16[1,768,4096]{2,1,0:T(8,128)(2,1)S(1)}, bf16[1,768,4096]{2,1,0:T(8,128)(2,1)}, u32[]{:S(2)}) copy-start(bf16[1,768,4096]{2,1,0:T(8,128)(2,1)} %param.9) | copy-start | bytes 18874372
  24.1 2.8 %copy-start.9 = (bf16[1,768,4096]{2,1,0:T(8,128)(2,1)S(1)}, bf16[1,768,4096]{2,1,0:T(8,128)(2,1)}, u32[]{:S(2)}) copy-start(bf16[1,768,4096]{2,1,0:T(8,128)(2,1)} %param.10) | copy-start | bytes 18874372
  32.3 7.0 %collective-permute-start.5 = (bf16[128,768]{1,0:T(8,128)(2,1)S(1)}, bf16[128,768]{1,0:T(8,128)(2,1)S(1)}, u32[]{:S(2)}, u32[]{:S(2)}) collective-permute-start(bf16[128,768]{1,0:T(8,128)(2,1)S(1)} %convolution_convert_fusion.1), channel_id=1, source_target_pairs={{0,4},{2,6},{4,0},{6,2},{1,5},{3,7},{5,1},{7,3},{8,12},{10,14},{12... | collective-permute-start | bytes 589832 | tf_op jit(solution)/shard_map/ppermute | solution.py:194
  34.5 15.2 %collective-permute-start.6 = (bf16[64,4096]{1,0:T(8,128)(2,1)S(1)}, bf16[64,4096]{1,0:T(8,128)(2,1)S(1)}, u32[]{:S(2)}, u32[]{:S(2)}) collective-permute-start(bf16[64,4096]{1,0:T(8,128)(2,1)S(1)} %combine.32.refs_3_), channel_id=1, source_target_pairs={{0,8},{10,2},{4,12},{14,6},{8,16},{18,10},{12,20},{22,14},{16,24},... | collective-permute-start | bytes 1572872 | tf_op jit(solution)/shard_map/ppermute | solution.py:249
  38.0 16.3 %collective-permute-start.2 = (bf16[64,4096]{1,0:T(8,128)(2,1)S(1)}, bf16[64,4096]{1,0:T(8,128)(2,1)S(1)}, u32[]{:S(2)}, u32[]{:S(2)}) collective-permute-start(bf16[64,4096]{1,0:T(8,128)(2,1)S(1)} %combine.31), channel_id=1, source_target_pairs={{8,0},{2,10},{12,4},{6,14},{16,8},{10,18},{20,12},{14,22},{24,16},... | collective-permute-start | bytes 1572872 | tf_op jit(solution)/shard_map/ppermute | solution.py:249
  40.1 2.8 %copy-start.4 = (bf16[1,768,4096]{2,1,0:T(8,128)(2,1)S(1)}, bf16[1,768,4096]{2,1,0:T(8,128)(2,1)}, u32[]{:S(2)}) copy-start(bf16[1,768,4096]{2,1,0:T(8,128)(2,1)} %param.9) | copy-start | bytes 18874372
  49.9 16.2 %collective-permute-start.7 = (bf16[64,4096]{1,0:T(8,128)(2,1)S(1)}, bf16[64,4096]{1,0:T(8,128)(2,1)S(1)}, u32[]{:S(2)}, u32[]{:S(2)}) collective-permute-start(bf16[64,4096]{1,0:T(8,128)(2,1)S(1)} %combine.34.refs_3_), channel_id=1, source_target_pairs={{0,8},{10,2},{4,12},{14,6},{8,16},{18,10},{12,20},{22,14},{16,24},... | collective-permute-start | bytes 1572872 | tf_op jit(solution)/shard_map/ppermute | solution.py:249
  54.5 18.0 %collective-permute-start.4 = (bf16[64,4096]{1,0:T(8,128)(2,1)S(1)}, bf16[64,4096]{1,0:T(8,128)(2,1)S(1)}, u32[]{:S(2)}, u32[]{:S(2)}) collective-permute-start(bf16[64,4096]{1,0:T(8,128)(2,1)S(1)} %combine.33), channel_id=1, source_target_pairs={{8,0},{2,10},{12,4},{6,14},{16,8},{10,18},{20,12},{14,22},{24,16},... | collective-permute-start | bytes 1572872 | tf_op jit(solution)/shard_map/ppermute | solution.py:249
  55.8 2.8 %copy-start.5 = (bf16[1,768,4096]{2,1,0:T(8,128)(2,1)S(1)}, bf16[1,768,4096]{2,1,0:T(8,128)(2,1)}, u32[]{:S(2)}) copy-start(bf16[1,768,4096]{2,1,0:T(8,128)(2,1)} %param.9) | copy-start | bytes 18874372
  67.0 16.8 %collective-permute-start.8 = (bf16[64,4096]{1,0:T(8,128)(2,1)S(1)}, bf16[64,4096]{1,0:T(8,128)(2,1)S(1)}, u32[]{:S(2)}, u32[]{:S(2)}) collective-permute-start(bf16[64,4096]{1,0:T(8,128)(2,1)S(1)} %get-tuple-element.69.refs_3_), channel_id=1, source_target_pairs={{0,8},{10,2},{4,12},{14,6},{8,16},{18,10},{12,20},{22,14},{16,24},... | collective-permute-start | bytes 1572872 | tf_op jit(solution)/shard_map/ppermute | solution.py:249
  72.5 1.0 copy-start.12
  73.7 29.4 %collective-permute-start.9 = (bf16[96,4096]{1,0:T(8,128)(2,1)S(1)}, bf16[96,4096]{1,0:T(8,128)(2,1)S(1)}, u32[]{:S(2)}, u32[]{:S(2)}) collective-permute-start(bf16[96,4096]{1,0:T(8,128)(2,1)S(1)} %get-tuple-element.68.one_ref), channel_id=1, source_target_pairs={{8,0},{2,10},{12,4},{6,14},{16,8},{10,18},{20,12},{14,22},{24,16},... | collective-permute-start | bytes 2359304 | tf_op jit(solution)/shard_map/ppermute | solution.py:249
  75.0 2.8 %copy-start.6 = (bf16[1,768,4096]{2,1,0:T(8,128)(2,1)S(1)}, bf16[1,768,4096]{2,1,0:T(8,128)(2,1)}, u32[]{:S(2)}) copy-start(bf16[1,768,4096]{2,1,0:T(8,128)(2,1)} %param.9) | copy-start | bytes 18874372
  77.8 2.8 %copy-start.10 = (bf16[1,768,4096]{2,1,0:T(8,128)(2,1)S(1)}, bf16[1,768,4096]{2,1,0:T(8,128)(2,1)}, u32[]{:S(2)}) copy-start(bf16[1,768,4096]{2,1,0:T(8,128)(2,1)} %param.10) | copy-start | bytes 18874372
  80.6 16.5 %copy-start.16 = (bf16[128,768]{1,0:T(8,128)(2,1)S(1)}, bf16[128,768]{1,0:T(8,128)(2,1)}, u32[]{:S(2)}) copy-start(bf16[128,768]{1,0:T(8,128)(2,1)} %copy-done.15) | copy-start | bytes 589828
  80.6 16.5 %copy-start.18 = (bf16[128,768]{1,0:T(8,128)(2,1)S(1)}, bf16[128,768]{1,0:T(8,128)(2,1)}, u32[]{:S(2)}) copy-start(bf16[128,768]{1,0:T(8,128)(2,1)} %copy-done.17) | copy-start | bytes 589828
  80.6 29.2 %slice-start = ((s8[6291456]{0:T(1024)(128)(4,1)}), s8[4194304]{0:T(1024)(128)(4,1)S(1)}, s32[]{:S(2)}) async-start(s8[6291456]{0:T(1024)(128)(4,1)} %bitcast.33), calls=%async_computation | async-start | bytes 8388608
  84.1 20.7 %collective-permute-start.10 = (bf16[96,4096]{1,0:T(8,128)(2,1)S(1)}, bf16[96,4096]{1,0:T(8,128)(2,1)S(1)}, u32[]{:S(2)}, u32[]{:S(2)}) collective-permute-start(bf16[96,4096]{1,0:T(8,128)(2,1)S(1)} %get-tuple-element.73.two_ref.refs_3_), channel_id=1, source_target_pairs={{0,8},{10,2},{4,12},{14,6},{8,16},{18,10},{12,20},{22,14},{16,24},... | collective-permute-start | bytes 2359304 | tf_op jit(solution)/shard_map/ppermute | solution.py:249
  90.8 6.3 %collective-permute-start.11 = (bf16[128,768]{1,0:T(8,128)(2,1)S(1)}, bf16[128,768]{1,0:T(8,128)(2,1)S(1)}, u32[]{:S(2)}, u32[]{:S(2)}) collective-permute-start(bf16[128,768]{1,0:T(8,128)(2,1)S(1)} %convolution_convert_fusion), channel_id=1, source_target_pairs={{0,6},{2,4},{4,2},{6,0},{1,7},{3,5},{5,3},{7,1},{8,14},{10,12},{12... | collective-permute-start | bytes 589832 | tf_op jit(solution)/shard_map/ppermute | solution.py:194
  97.2 2.8 %copy-start.7 = (bf16[1,768,4096]{2,1,0:T(8,128)(2,1)S(1)}, bf16[1,768,4096]{2,1,0:T(8,128)(2,1)}, u32[]{:S(2)}) copy-start(bf16[1,768,4096]{2,1,0:T(8,128)(2,1)} %param.9) | copy-start | bytes 18874372
  100.0 9.7 %copy-start.14 = (bf16[128,768]{1,0:T(8,128)(2,1)S(1)}, bf16[128,768]{1,0:T(8,128)(2,1)}, u32[]{:S(2)}) copy-start(bf16[128,768]{1,0:T(8,128)(2,1)} %copy-done.13) | copy-start | bytes 589828
  100.0 9.8 %slice-start.1 = ((s8[6291456]{0:T(1024)(128)(4,1)}), s8[2097152]{0:T(1024)(128)(4,1)S(1)}, s32[]{:S(2)}) async-start(s8[6291456]{0:T(1024)(128)(4,1)} %bitcast.33), calls=%async_computation.1 | async-start | bytes 4194304
  103.5 20.5 %collective-permute-start.12 = (bf16[96,4096]{1,0:T(8,128)(2,1)S(1)}, bf16[96,4096]{1,0:T(8,128)(2,1)S(1)}, u32[]{:S(2)}, u32[]{:S(2)}) collective-permute-start(bf16[96,4096]{1,0:T(8,128)(2,1)S(1)} %get-tuple-element.75.one_ref), channel_id=1, source_target_pairs={{8,0},{2,10},{12,4},{6,14},{16,8},{10,18},{20,12},{14,22},{24,16},... | collective-permute-start | bytes 2359304 | tf_op jit(solution)/shard_map/ppermute | solution.py:249
  105.1 20.5 %collective-permute-start.13 = (bf16[96,4096]{1,0:T(8,128)(2,1)S(1)}, bf16[96,4096]{1,0:T(8,128)(2,1)S(1)}, u32[]{:S(2)}, u32[]{:S(2)}) collective-permute-start(bf16[96,4096]{1,0:T(8,128)(2,1)S(1)} %get-tuple-element.79.two_ref.refs_3_), channel_id=1, source_target_pairs={{0,8},{10,2},{4,12},{14,6},{8,16},{18,10},{12,20},{22,14},{16,24},... | collective-permute-start | bytes 2359304 | tf_op jit(solution)/shard_map/ppermute | solution.py:249
  124.3 23.0 %collective-permute-start.14 = (bf16[96,4096]{1,0:T(8,128)(2,1)S(1)}, bf16[96,4096]{1,0:T(8,128)(2,1)S(1)}, u32[]{:S(2)}, u32[]{:S(2)}) collective-permute-start(bf16[96,4096]{1,0:T(8,128)(2,1)S(1)} %get-tuple-element.81.one_ref), channel_id=1, source_target_pairs={{8,0},{2,10},{12,4},{6,14},{16,8},{10,18},{20,12},{14,22},{24,16},... | collective-permute-start | bytes 2359304 | tf_op jit(solution)/shard_map/ppermute | solution.py:249
  125.9 22.9 %collective-permute-start.15 = (bf16[96,4096]{1,0:T(8,128)(2,1)S(1)}, bf16[96,4096]{1,0:T(8,128)(2,1)S(1)}, u32[]{:S(2)}, u32[]{:S(2)}) collective-permute-start(bf16[96,4096]{1,0:T(8,128)(2,1)S(1)} %get-tuple-element.85.two_ref.refs_3_), channel_id=1, source_target_pairs={{0,8},{10,2},{4,12},{14,6},{8,16},{18,10},{12,20},{22,14},{16,24},... | collective-permute-start | bytes 2359304 | tf_op jit(solution)/shard_map/ppermute | solution.py:249
  147.6 21.3 %collective-permute-start.17 = (bf16[96,4096]{1,0:T(8,128)(2,1)S(1)}, bf16[96,4096]{1,0:T(8,128)(2,1)S(1)}, u32[]{:S(2)}, u32[]{:S(2)}) collective-permute-start(bf16[96,4096]{1,0:T(8,128)(2,1)S(1)} %get-tuple-element.87.one_ref), channel_id=1, source_target_pairs={{8,0},{2,10},{12,4},{6,14},{16,8},{10,18},{20,12},{14,22},{24,16},... | collective-permute-start | bytes 2359304 | tf_op jit(solution)/shard_map/ppermute | solution.py:249
  149.2 21.2 %collective-permute-start.18 = (bf16[96,4096]{1,0:T(8,128)(2,1)S(1)}, bf16[96,4096]{1,0:T(8,128)(2,1)S(1)}, u32[]{:S(2)}, u32[]{:S(2)}) collective-permute-start(bf16[96,4096]{1,0:T(8,128)(2,1)S(1)} %get-tuple-element.91.two_ref.refs_3_), channel_id=1, source_target_pairs={{0,8},{10,2},{4,12},{14,6},{8,16},{18,10},{12,20},{22,14},{16,24},... | collective-permute-start | bytes 2359304 | tf_op jit(solution)/shard_map/ppermute | solution.py:249
  154.0 21.6 %slice-start.4 = ((s8[6291456]{0:T(1024)(128)(4,1)}), s8[4194304]{0:T(1024)(128)(4,1)S(1)}, s32[]{:S(2)}) async-start(s8[6291456]{0:T(1024)(128)(4,1)} %bitcast.53), calls=%async_computation.4 | async-start | bytes 8388608
  154.0 21.5 %copy-start.19 = (bf16[32,768]{1,0:T(8,128)(2,1)S(1)}, bf16[32,768]{1,0:T(8,128)(2,1)}, u32[]{:S(2)}) copy-start(bf16[32,768]{1,0:T(8,128)(2,1)} %get-tuple-element.149) | copy-start | bytes 147460
  154.0 21.5 %copy-start.20 = (bf16[32,768]{1,0:T(8,128)(2,1)S(1)}, bf16[32,768]{1,0:T(8,128)(2,1)}, u32[]{:S(2)}) copy-start(bf16[32,768]{1,0:T(8,128)(2,1)} %get-tuple-element.150) | copy-start | bytes 147460
  154.0 21.5 %copy-start.21 = (f32[256,2]{0,1:T(2,128)S(1)}, f32[256,2]{0,1:T(2,128)}, u32[]{:S(2)}) copy-start(f32[256,2]{0,1:T(2,128)} %param.8) | copy-start | bytes 6148
  154.0 21.5 %slice-start.5 = ((s8[6291456]{0:T(1024)(128)(4,1)}), s8[2097152]{0:T(1024)(128)(4,1)S(1)}, s32[]{:S(2)}) async-start(s8[6291456]{0:T(1024)(128)(4,1)} %bitcast.53), calls=%async_computation.5 | async-start | bytes 4194304
  169.2 20.4 %collective-permute-start.19 = (bf16[96,4096]{1,0:T(8,128)(2,1)S(1)}, bf16[96,4096]{1,0:T(8,128)(2,1)S(1)}, u32[]{:S(2)}, u32[]{:S(2)}) collective-permute-start(bf16[96,4096]{1,0:T(8,128)(2,1)S(1)} %get-tuple-element.93.one_ref), channel_id=1, source_target_pairs={{8,0},{2,10},{12,4},{6,14},{16,8},{10,18},{20,12},{14,22},{24,16},... | collective-permute-start | bytes 2359304 | tf_op jit(solution)/shard_map/ppermute | solution.py:249
  170.8 20.4 %collective-permute-start.20 = (bf16[96,4096]{1,0:T(8,128)(2,1)S(1)}, bf16[96,4096]{1,0:T(8,128)(2,1)S(1)}, u32[]{:S(2)}, u32[]{:S(2)}) collective-permute-start(bf16[96,4096]{1,0:T(8,128)(2,1)S(1)} %get-tuple-element.97.two_ref.refs_3_), channel_id=1, source_target_pairs={{0,8},{10,2},{4,12},{14,6},{8,16},{18,10},{12,20},{22,14},{16,24},... | collective-permute-start | bytes 2359304 | tf_op jit(solution)/shard_map/ppermute | solution.py:249
  178.5 3.0 %slice-start.2 = ((s8[6291456]{0:T(1024)(128)(4,1)}), s8[4194304]{0:T(1024)(128)(4,1)S(1)}, s32[]{:S(2)}) async-start(s8[6291456]{0:T(1024)(128)(4,1)} %bitcast.49), calls=%async_computation.2 | async-start | bytes 8388608
  180.0 1.8 slice-start.3
  189.9 21.0 %collective-permute-start.23 = (bf16[96,4096]{1,0:T(8,128)(2,1)S(1)}, bf16[96,4096]{1,0:T(8,128)(2,1)S(1)}, u32[]{:S(2)}, u32[]{:S(2)}) collective-permute-start(bf16[96,4096]{1,0:T(8,128)(2,1)S(1)} %get-tuple-element.99.one_ref), channel_id=1, source_target_pairs={{8,0},{2,10},{12,4},{6,14},{16,8},{10,18},{20,12},{14,22},{24,16},... | collective-permute-start | bytes 2359304 | tf_op jit(solution)/shard_map/ppermute | solution.py:249
  193.0 24.2 %collective-permute-start.24 = (bf16[96,4096]{1,0:T(8,128)(2,1)S(1)}, bf16[96,4096]{1,0:T(8,128)(2,1)S(1)}, u32[]{:S(2)}, u32[]{:S(2)}) collective-permute-start(bf16[96,4096]{1,0:T(8,128)(2,1)S(1)} %get-tuple-element.103.two_ref.refs_3_), channel_id=1, source_target_pairs={{0,8},{10,2},{4,12},{14,6},{8,16},{18,10},{12,20},{22,14},{16,24},... | collective-permute-start | bytes 2359304 | tf_op jit(solution)/shard_map/ppermute | solution.py:249
  197.6 5.7 %collective-permute-start.21 = (bf16[128,768]{1,0:T(8,128)(2,1)S(1)}, bf16[128,768]{1,0:T(8,128)(2,1)S(1)}, u32[]{:S(2)}, u32[]{:S(2)}) collective-permute-start(bf16[128,768]{1,0:T(8,128)(2,1)S(1)} %pad_maximum_fusion), channel_id=1, source_target_pairs={{0,1},{1,0},{2,3},{3,2},{4,5},{5,4},{6,7},{7,6},{8,9},{9,8},{10,11... | collective-permute-start | bytes 589832 | tf_op jit(solution)/shard_map/ppermute | solution.py:263
  203.4 18.7 %collective-permute-start.22 = (bf16[128,768]{1,0:T(8,128)(2,1)S(1)}, bf16[128,768]{1,0:T(8,128)(2,1)S(1)}, u32[]{:S(2)}, u32[]{:S(2)}) collective-permute-start(bf16[128,768]{1,0:T(8,128)(2,1)S(1)} %add_convert_fusion.2), channel_id=1, source_target_pairs={{0,2},{2,0},{4,6},{6,4},{1,3},{3,1},{5,7},{7,5},{8,10},{10,8},{12,... | collective-permute-start | bytes 589832 | tf_op jit(solution)/shard_map/ppermute | solution.py:289
  211.1 16.1 %collective-permute-start.25 = (bf16[96,4096]{1,0:T(8,128)(2,1)S(1)}, bf16[96,4096]{1,0:T(8,128)(2,1)S(1)}, u32[]{:S(2)}, u32[]{:S(2)}) collective-permute-start(bf16[96,4096]{1,0:T(8,128)(2,1)S(1)} %get-tuple-element.105.one_ref), channel_id=1, source_target_pairs={{8,0},{2,10},{12,4},{6,14},{16,8},{10,18},{20,12},{14,22},{24,16},... | collective-permute-start | bytes 2359304 | tf_op jit(solution)/shard_map/ppermute | solution.py:249
  212.5 60.9 %collective-permute-start.16 = (bf16[64,768]{1,0:T(8,128)(2,1)S(1)}, bf16[64,768]{1,0:T(8,128)(2,1)S(1)}, u32[]{:S(2)}, u32[]{:S(2)}) collective-permute-start(bf16[64,768]{1,0:T(8,128)(2,1)S(1)} %pad_maximum_fusion.11), channel_id=1, source_target_pairs={{0,1},{1,0},{2,3},{3,2},{4,5},{5,4},{6,7},{7,6},{8,9},{9,8},{10,11... | collective-permute-start | bytes 294920 | tf_op jit(solution)/shard_map/ppermute | solution.py:263
  217.6 11.3 %collective-permute-start.26 = (bf16[32,4096]{1,0:T(8,128)(2,1)S(1)}, bf16[32,4096]{1,0:T(8,128)(2,1)S(1)}, u32[]{:S(2)}, u32[]{:S(2)}) collective-permute-start(bf16[32,4096]{1,0:T(8,128)(2,1)S(1)} %get-tuple-element.109.two_ref), channel_id=1, source_target_pairs={{0,8},{10,2},{4,12},{14,6},{8,16},{18,10},{12,20},{22,14},{16,24},... | collective-permute-start | bytes 786440 | tf_op jit(solution)/shard_map/ppermute | solution.py:249
  227.6 15.3 %collective-permute-start.29 = (bf16[32,4096]{1,0:T(8,128)(2,1)S(1)}, bf16[32,4096]{1,0:T(8,128)(2,1)S(1)}, u32[]{:S(2)}, u32[]{:S(2)}) collective-permute-start(bf16[32,4096]{1,0:T(8,128)(2,1)S(1)} %get-tuple-element.111.one_ref), channel_id=1, source_target_pairs={{8,0},{2,10},{12,4},{6,14},{16,8},{10,18},{20,12},{14,22},{24,16},... | collective-permute-start | bytes 786440 | tf_op jit(solution)/shard_map/ppermute | solution.py:249
  230.4 14.0 %collective-permute-start.30 = (bf16[32,4096]{1,0:T(8,128)(2,1)S(1)}, bf16[32,4096]{1,0:T(8,128)(2,1)S(1)}, u32[]{:S(2)}, u32[]{:S(2)}) collective-permute-start(bf16[32,4096]{1,0:T(8,128)(2,1)S(1)} %combine.51.two_ref), channel_id=1, source_target_pairs={{0,8},{10,2},{4,12},{14,6},{8,16},{18,10},{12,20},{22,14},{16,24},... | collective-permute-start | bytes 786440 | tf_op jit(solution)/shard_map/ppermute | solution.py:249
  235.1 5.7 %collective-permute-start.27 = (bf16[128,768]{1,0:T(8,128)(2,1)S(1)}, bf16[128,768]{1,0:T(8,128)(2,1)S(1)}, u32[]{:S(2)}, u32[]{:S(2)}) collective-permute-start(bf16[128,768]{1,0:T(8,128)(2,1)S(1)} %pad_maximum_fusion.1), channel_id=1, source_target_pairs={{0,1},{1,0},{2,3},{3,2},{4,5},{5,4},{6,7},{7,6},{8,9},{9,8},{10,11... | collective-permute-start | bytes 589832 | tf_op jit(solution)/shard_map/ppermute | solution.py:263
  240.9 9.7 %collective-permute-start.28 = (bf16[128,768]{1,0:T(8,128)(2,1)S(1)}, bf16[128,768]{1,0:T(8,128)(2,1)S(1)}, u32[]{:S(2)}, u32[]{:S(2)}) collective-permute-start(bf16[128,768]{1,0:T(8,128)(2,1)S(1)} %add_convert_fusion.1), channel_id=1, source_target_pairs={{0,4},{2,6},{4,0},{6,2},{1,5},{3,7},{5,1},{7,3},{8,12},{10,14},{12... | collective-permute-start | bytes 589832 | tf_op jit(solution)/shard_map/ppermute | solution.py:289
  242.9 9.6 %collective-permute-start.31 = (bf16[32,4096]{1,0:T(8,128)(2,1)S(1)}, bf16[32,4096]{1,0:T(8,128)(2,1)S(1)}, u32[]{:S(2)}, u32[]{:S(2)}) collective-permute-start(bf16[32,4096]{1,0:T(8,128)(2,1)S(1)} %combine.52.one_ref), channel_id=1, source_target_pairs={{8,0},{2,10},{12,4},{6,14},{16,8},{10,18},{20,12},{14,22},{24,16},... | collective-permute-start | bytes 786440 | tf_op jit(solution)/shard_map/ppermute | solution.py:249
  245.9 8.4 %collective-permute-start.32 = (bf16[32,4096]{1,0:T(8,128)(2,1)S(1)}, bf16[32,4096]{1,0:T(8,128)(2,1)S(1)}, u32[]{:S(2)}, u32[]{:S(2)}) collective-permute-start(bf16[32,4096]{1,0:T(8,128)(2,1)S(1)} %combine.53.two_ref), channel_id=1, source_target_pairs={{0,8},{10,2},{4,12},{14,6},{8,16},{18,10},{12,20},{22,14},{16,24},... | collective-permute-start | bytes 786440 | tf_op jit(solution)/shard_map/ppermute | solution.py:249
  252.6 8.8 %collective-permute-start.35 = (bf16[32,4096]{1,0:T(8,128)(2,1)S(1)}, bf16[32,4096]{1,0:T(8,128)(2,1)S(1)}, u32[]{:S(2)}, u32[]{:S(2)}) collective-permute-start(bf16[32,4096]{1,0:T(8,128)(2,1)S(1)} %combine.54.one_ref), channel_id=1, source_target_pairs={{8,0},{2,10},{12,4},{6,14},{16,8},{10,18},{20,12},{14,22},{24,16},... | collective-permute-start | bytes 786440 | tf_op jit(solution)/shard_map/ppermute | solution.py:249
  255.9 8.3 %collective-permute-start.36 = (bf16[32,4096]{1,0:T(8,128)(2,1)S(1)}, bf16[32,4096]{1,0:T(8,128)(2,1)S(1)}, u32[]{:S(2)}, u32[]{:S(2)}) collective-permute-start(bf16[32,4096]{1,0:T(8,128)(2,1)S(1)} %combine.55.two_ref), channel_id=1, source_target_pairs={{0,8},{10,2},{4,12},{14,6},{8,16},{18,10},{12,20},{22,14},{16,24},... | collective-permute-start | bytes 786440 | tf_op jit(solution)/shard_map/ppermute | solution.py:249
  260.4 6.4 %collective-permute-start.33 = (bf16[128,768]{1,0:T(8,128)(2,1)S(1)}, bf16[128,768]{1,0:T(8,128)(2,1)S(1)}, u32[]{:S(2)}, u32[]{:S(2)}) collective-permute-start(bf16[128,768]{1,0:T(8,128)(2,1)S(1)} %pad_maximum_fusion.2), channel_id=1, source_target_pairs={{0,1},{1,0},{2,3},{3,2},{4,5},{5,4},{6,7},{7,6},{8,9},{9,8},{10,11... | collective-permute-start | bytes 589832 | tf_op jit(solution)/shard_map/ppermute | solution.py:263
  265.7 4.7 %collective-permute-start.37 = (bf16[64,768]{1,0:T(8,128)(2,1)S(1)}, bf16[64,768]{1,0:T(8,128)(2,1)S(1)}, u32[]{:S(2)}, u32[]{:S(2)}) collective-permute-start(bf16[64,768]{1,0:T(8,128)(2,1)S(1)} %pad_maximum_fusion.15), channel_id=1, source_target_pairs={{0,1},{1,0},{2,3},{3,2},{4,5},{5,4},{6,7},{7,6},{8,9},{9,8},{10,11... | collective-permute-start | bytes 294920 | tf_op jit(solution)/shard_map/ppermute | solution.py:263
  266.8 5.8 %collective-permute-start.34 = (bf16[128,768]{1,0:T(8,128)(2,1)S(1)}, bf16[128,768]{1,0:T(8,128)(2,1)S(1)}, u32[]{:S(2)}, u32[]{:S(2)}) collective-permute-start(bf16[128,768]{1,0:T(8,128)(2,1)S(1)} %add_convert_fusion), channel_id=1, source_target_pairs={{0,6},{2,4},{4,2},{6,0},{1,7},{3,5},{5,3},{7,1},{8,14},{10,12},{12... | collective-permute-start | bytes 589832 | tf_op jit(solution)/shard_map/ppermute | solution.py:289
  270.4 4.6 %copy-start.1 = (bf16[256,768]{1,0:T(8,128)(2,1)S(1)}, bf16[256,768]{1,0:T(8,128)(2,1)}, u32[]{:S(2)}) copy-start(bf16[256,768]{1,0:T(8,128)(2,1)} %param.6) | copy-start | bytes 1179652
  (2 other events, 1.4 us)
where the time goes:
time: 276 us; the launch traced here: 275 us
  starting transfers between devices  91.3 us (33%)
  waiting for transfers between devices  81.7 us (30%)
  Pallas kernels  56.9 us (21%)
  local copies, waits for them, and re-layouts  29.3 us (11%)
  matrix products  5.71 us (2%)
  between operations  5.32 us (2%)
  other arithmetic  4.7 us (2%)
    ppermute x27, starting transfers between devices, local(): got[f] = lax.ppermute(message, ('dp', 'expert'), flows[f])  81 us
    ppermute x27, waiting for transfers between devices, local(): got[f] = lax.ppermute(message, ('dp', 'expert'), flows[f])  62.9 us
    pallas_call x51, Pallas kernels, call(): pl.pallas_call(body, name=name, out_shape=shapes, in_specs=specs, out_spe...  56.9 us
    unnamed x56, local copies, waits for them, and re-layouts  27.7 us
    ppermute x5, waiting for transfers between devices, across(): other = lax.ppermute(part, 'tensor', [(0, 1), (1, 0)])  11.1 us
    ppermute x3, waiting for transfers between devices, rows_for(): lax.ppermute(picked, 'expert', [(a, a ^ j) for a in range(experts)])  6.26 us
    ppermute x5, starting transfers between devices, across(): other = lax.ppermute(part, 'tensor', [(0, 1), (1, 0)])  5.62 us
  transfers between devices with their start and end apart: 38, of which 16 were waited for; matrix products, arithmetic and copies ran while one was open for 2% of the time, Pallas kernels for 20%

commit v1 on v0

v1 whole, which is shorter than its diff:
```python
import jax
import jax.numpy as jnp
from jax import lax
from jax.experimental import pallas as pl
from jax.experimental.pallas import tpu as pltpu
from jax.sharding import PartitionSpec as P

F32, BF16, I32 = jnp.float32, jnp.bfloat16, jnp.int32
CHUNK = 32
WHOLE = pl.BlockSpec(memory_space=pltpu.VMEM)
SCALAR = pl.BlockSpec(memory_space=pltpu.SMEM)
FAR = pl.BlockSpec(memory_space=pltpu.HBM)
LIGHT = pl.CostEstimate(flops=0, bytes_accessed=0, transcendentals=0)


def chunk_order(experts, per):
    head = max(1, per // 2)
    order = [(0, i) for i in range(head)]
    order += [(j, i) for j in range(1, experts) for i in range(per)]
    return order + [(0, i) for i in range(head, per)]


def pick(options, index):
    out = options[-1]
    for k in range(len(options) - 2, -1, -1):
        out = jnp.where(index == k, options[k], out)
    return out


def array(*shape, dtype=BF16):
    return jax.ShapeDtypeStruct(shape, dtype)


def call(body, name, shapes, args, specs=None, scratch=(), grant=16):
    if specs is None:
        specs = [SCALAR if a.dtype == I32 else WHOLE for a in args]
    return pl.pallas_call(
        body,
        name=name,
        out_shape=shapes,
        in_specs=specs,
        out_specs=[WHOLE] * len(shapes),
        scratch_shapes=scratch,
        cost_estimate=LIGHT,
        compiler_params=pltpu.CompilerParams(vmem_limit_bytes=grant * 2**20),
    )(*args)


def tiles_of(columns, wide):
    wide = wide if columns % wide == 0 else columns
    return [pl.ds(at, wide) for at in range(0, columns, wide)]


def one_hot(mask):
    return jnp.where(mask, 1.0, 0.0).astype(BF16)


def begin(m, experts, capacity, e, ids, tokens, wg, wu):
    n, width = tokens.shape
    units = wg.shape[1]
    half = capacity // 2
    cuts = tiles_of(units, 512)
    names = (experts + 15) // 16 * 16

    def body(e_ref, ids_hbm, tok_hbm, wg_hbm, wu_hbm, place_ref, *rest):
        rows = rest[:experts]
        wg_ref, wu_ref, g_ref, u_ref, x_ref, ids_ref, tok_ref, sems, small = rest[experts:]
        ids_copy = pltpu.make_async_copy(ids_hbm, ids_ref, small.at[0])
        tok_copy = pltpu.make_async_copy(tok_hbm, tok_ref, small.at[1])
        ids_copy.start()
        tok_copy.start()
        pairs = ((wg_hbm, wg_ref, g_ref), (wu_hbm, wu_ref, u_ref))

        def load(k, t):
            return pltpu.make_async_copy(
                pairs[k][0].at[:, cuts[t]], pairs[k][1].at[:, cuts[t]], sems.at[k, t]
            )

        for t in range(len(cuts)):
            for k in range(2):
                load(k, t).start()
        ids_copy.wait()
        index = lax.broadcasted_iota(I32, (names, n), 0)
        ids = [ids_ref[k : k + 1, :] for k in range(2)]
        hits = [index == ids[k] for k in range(2)]
        earlier = lax.broadcasted_iota(I32, (n, n), 0) < lax.broadcasted_iota(I32, (n, n), 1)
        before = jnp.dot(one_hot(hits[0] | hits[1]), one_hot(earlier), preferred_element_type=F32)
        places = []
        for k in range(2):
            rank = jnp.sum(jnp.where(hits[k], before, 0.0), axis=0, keepdims=True)
            places.append(rank.astype(I32) * experts + ids[k])
            place_ref[k : k + 1, :] = places[k]
        lines = lax.broadcasted_iota(I32, (capacity, n), 0) * experts
        tok_copy.wait()
        for j in range(experts):
            mine = lines + (e_ref[0] ^ j)
            chosen = one_hot((mine == places[0]) | (mine == places[1]))
            picked = jnp.dot(chosen, tok_ref[...], preferred_element_type=F32).astype(BF16)
            rows[j][...] = picked
            if j == 0:
                x_ref[:m] = picked[:m]
                x_ref[m:] = picked[half : half + m]
        for t in range(len(cuts)):
            for k in range(2):
                load(k, t).wait()
                pairs[k][2][:, cuts[t]] = jnp.dot(
                    x_ref[...], pairs[k][1][:, cuts[t]], preferred_element_type=F32
                ).astype(BF16)

    shapes = [array(2, n, dtype=I32)] + [array(capacity, width)] * experts
    shapes += [array(width, units)] * 2 + [array(2 * m, units)] * 2
    out = call(
        body,
        "begin",
        shapes,
        (e, ids, tokens, wg, wu),
        [SCALAR, FAR, FAR, FAR, FAR],
        [
            pltpu.VMEM((2 * m, width), BF16),
            pltpu.VMEM((2, n), I32),
            pltpu.VMEM((n, width), BF16),
            pltpu.SemaphoreType.DMA((2, len(cuts))),
            pltpu.SemaphoreType.DMA((2,)),
        ],
        grant=36,
    )
    return out[0], out[1 : 1 + experts], out[1 + experts : 3 + experts], out[3 + experts :]


def project(m, spots, rows, sources, weights, tie):
    used = sorted({c[0] for per_flow in sources for c in per_flow if c})
    width, units = weights[0].shape

    def body(spot_ref, *refs):
        groups = dict(zip(used, refs))
        wg_ref, wu_ref = refs[len(used) : len(used) + 2]
        g_ref, u_ref, x_ref = refs[-3:]
        for f in range(2):
            options = [
                jnp.zeros((m, width), BF16) if c is None else groups[c[0]][c[1] : c[1] + m, :]
                for c in sources[f]
            ]
            x_ref[f * m : (f + 1) * m] = pick(options, spot_ref[f])
        for cols in tiles_of(units, 1024):
            for w_ref, out_ref in ((wg_ref, g_ref), (wu_ref, u_ref)):
                out_ref[:, cols] = jnp.dot(
                    x_ref[...], w_ref[:, cols], preferred_element_type=F32
                ).astype(BF16)

    return call(
        body,
        "project",
        [array(2 * m, units)] * 2,
        (spots, *(rows[j] for j in used), *weights, tie),
        scratch=[pltpu.VMEM((2 * m, width), BF16)],
    )


def combine(m, units, f, first, came, partial, act, summing, sending, fresh, spots, ties, relay):
    args, use = [], {}

    def take(key, value):
        if value is not None:
            use[key] = len(args)
            args.append(value)

    take("spots", spots if act is not None and came is not None else None)
    take("came", came)
    if summing:
        take("g", partial[0])
        take("u", partial[1])
    take("act", act)
    take("relay", relay)
    taken = len(args)
    args += ties
    sums = 2 * m if summing and sending else 0
    hidden = act is not None or (came is not None and came.shape[0] % (2 * m) == m)
    rows = sums + (m if hidden else 0)
    shapes = [array(rows, units)] if rows else []
    if fresh:
        shapes.append(array(m, units))
    if relay is not None:
        shapes.append(array(*relay.shape))

    def body(*refs):
        ins, outs = refs[:taken], refs[len(args) :]
        ref = {key: ins[at] for key, at in use.items()}
        if relay is not None:
            outs[-1][...] = ref["relay"][...]

        def step(cols):
            if summing:
                total = []
                for k, key in enumerate(("g", "u")):
                    value = ref[key][f * m : (f + 1) * m, cols].astype(F32)
                    if not first:
                        value = value + ref["came"][k * m : (k + 1) * m, cols].astype(F32)
                    total.append(value)
                    if sending:
                        outs[0][k * m : (k + 1) * m, cols] = value.astype(BF16)
                if fresh:
                    g, u = total
                    outs[1 if rows else 0][:, cols] = (g / (1.0 + jnp.exp(-g)) * u).astype(BF16)
            if hidden:
                if "came" in ref and came.shape[0] % (2 * m) == m:
                    h = ref["came"][came.shape[0] - m :, cols]
                    if "act" in ref:
                        h = jnp.where(ref["spots"][f] == 0, ref["act"][:, cols], h)
                else:
                    h = ref["act"][:, cols]
                outs[0][sums:, cols] = h

        wide = 512 if units % 512 == 0 else units

        def loop(i, carry):
            step(pl.ds(pl.multiple_of(i * wide, wide), wide))
            return carry

        lax.fori_loop(0, units // wide, loop, 0)

    out = list(call(body, "combine", shapes, args))
    relayed = out.pop() if relay is not None else None
    activated = out.pop() if fresh else None
    return (out[0] if rows else None), activated, relayed


def lower(m, one, two, wd, tie):
    columns = wd.shape[1]

    def body(one_ref, two_ref, w_ref, *rest):
        h = jnp.concatenate([r[r.shape[0] - m :, :] for r in (one_ref, two_ref)])
        for cols in tiles_of(columns, 256):
            rest[-1][:, cols] = jnp.dot(h, w_ref[:, cols], preferred_element_type=F32).astype(BF16)

    return call(body, "lower", [array(2 * m, columns)], (one, two, wd, *tie))[0]


def local(tokens, route_ids, gates, w_gate, w_up, w_down):
    experts = lax.axis_size("expert")
    depth = lax.axis_size("dp")
    tensors = lax.axis_size("tensor")
    z = lax.axis_index("dp")
    e = lax.axis_index("expert")
    n, width = tokens.shape
    units = w_gate.shape[2]
    capacity = max(3 * n // 8, 2 * n // experts)
    capacity = (capacity + 15) // 16 * 16
    half = capacity // 2
    m = CHUNK if half % CHUNK == 0 else 16
    per = half // m
    order = chunk_order(experts, per)
    chunks = len(order)
    last = depth - 1

    even = e % 2 == 0
    spot = [jnp.where(even, z, last - z), jnp.where(even, last - z, z)]
    spots = jnp.stack(spot).astype(I32)
    climb = [(a * experts + b, (a + 1) * experts + b) for a in range(last) for b in range(experts)]
    flows = [[(a, c) if a % experts % 2 == f else (c, a) for a, c in climb] for f in range(2)]

    places, picked, weights, partial = begin(
        m, experts, capacity, e.astype(I32).reshape(1), route_ids.T, tokens, w_gate[0], w_up[0]
    )
    rows = [picked[0]] + [None] * (experts - 1)
    due = {max(0, order.index((j, 0)) - 2): j for j in range(1, experts)}

    def sources(s):
        found = [[None] * depth for _ in range(2)]
        for f in range(2):
            for a in range(depth):
                if 0 <= s - a < chunks:
                    j, i = order[s - a]
                    found[f][a] = (j, f * half + i * m)
        return found

    wd = w_down[0]
    sums_end = chunks + last
    got = [None, None]
    act = [None, None]
    held = [{}, {}]
    outs = []
    ties = []
    for s in range(chunks + 2 * last + 1):
        summing = s < sums_end
        following = None
        for f in range(2):
            o = 1 - f
            first = last + 1 if f == 0 else last
            carries = first <= s < first + chunks + last
            if not (summing or carries):
                continue
            message, act[f], relayed = combine(
                m,
                units,
                f,
                s == 0,
                got[f] if s else None,
                partial,
                act[o] if carries else None,
                summing,
                s < sums_end - 1,
                summing and s >= last,
                spots,
                ties,
                picked[due[s]] if f == 1 and s in due else None,
            )
            ties = []
            if s < sums_end - 1 or (carries and s < first + chunks + last - 1):
                got[f] = lax.ppermute(message, ("dp", "expert"), flows[f])
            if relayed is not None:
                j = due[s]
                rows[j] = lax.ppermute(relayed, "expert", [(a, a ^ j) for a in range(experts)])
            if carries:
                held[o][s - first] = message
            if f == 0 and s + 1 < sums_end and all(
                rows[c[0]] is not None for per_flow in sources(s + 1) for c in per_flow if c
            ):
                following = project(m, spots, rows, sources(s + 1), weights, message)
                ties.append(following[0])
            if f == 1 and s + 1 < sums_end and following is None:
                following = project(m, spots, rows, sources(s + 1), weights, message)
                ties.append(following[0])
            if f == 1 and s - last - 1 in held[1]:
                q = s - last - 1
                outs.append(lower(m, held[0][q], held[1][q], wd, (message,)))
                ties.append(outs[-1])
            if f == 0 and carries and s == chunks + 2 * last:
                q = s - last - 1
                outs.append(lower(m, held[0][q], held[1][q], wd, ()))
        partial = following

    def finished(start, stop):
        return [
            jnp.concatenate(
                [
                    pick([outs[c + a][f * m : (f + 1) * m] for a in range(depth)], spot[1 - f])
                    for c in range(start, stop)
                ]
            )
            for f in range(2)
        ]

    yields = [jnp.zeros((n, width), F32), jnp.zeros((n, width), F32)]
    spans = []
    for index, (j, i) in enumerate(order):
        if spans and spans[-1][0] == j:
            spans[-1][2] = index + 1
        else:
            spans.append([j, index, index + 1, i])
    for j, start, stop, i in spans:
        size = (stop - start) * m
        part = jnp.concatenate(finished(start, stop))
        if tensors == 2 and stop >= chunks - 1:
            other = lax.ppermute(part, "tensor", [(0, 1), (1, 0)])
            part = (part.astype(F32) + other.astype(F32)).astype(BF16)
        else:
            part = lax.psum(part, "tensor")
        if j:
            part = lax.ppermute(part, "expert", [(a, a ^ j) for a in range(experts)])
        ranks = jnp.arange(size, dtype=I32) + i * m
        ranks = jnp.concatenate([ranks, ranks + half])
        label = ranks * experts + (e ^ j)
        for k in range(2):
            chosen = (label[:, None] == places[k][None, :]).astype(BF16)
            yields[k] += lax.dot_general(
                chosen, part, (((0,), (0,)), ((), ())), preferred_element_type=F32
            )
    mixed = gates[:, 0:1] * yields[0] + gates[:, 1:2] * yields[1]
    return mixed.astype(BF16)


def solution(mesh):
    return jax.shard_map(
        local,
        mesh=mesh,
        in_specs=(
            P("expert", "dp"),
            P("expert", None),
            P("expert", None),
            P("expert", "dp", "tensor"),
            P("expert", "dp", "tensor"),
            P("expert", "tensor", "dp"),
        ),
        out_specs=P("expert", "dp"),
        check_vma=False,
    )
```

time: 276 us -> 312 us (1.13)
  waiting for transfers between devices: 81.7 us -> 104 us
  between operations: 5.32 us -> 14.5 us
  Pallas kernels: 56.9 us -> 63 us
    psum x0 -> x1, waiting for transfers between devices: none -> 19.5 us  [local(): part = lax.psum(part, 'tensor')]
    pallas_call x51, Pallas kernels: 56.9 us -> 63 us  [call(): pl.pallas_call(body, name=name, out_shape=shapes, in_specs=specs, out_spe...]
    ppermute x3, waiting for transfers between devices: 1.47 us -> 6.4 us  [local(): part = lax.ppermute(part, 'expert', [(a, a ^ j) for a in range(experts)])]
    ppermute x8 -> x5, starting transfers between devices: 8.23 us -> 4.05 us  [the longest x2 2.16 us: local(): other = lax.ppermute(part, 'tensor', [(0, 1), (1, 0)])]
    unnamed x56 -> x48, local copies, waits for them, and re-layouts: 27.7 us -> 31 us
    ppermute x8 -> x5, waiting for transfers between devices: 17.4 us -> 14.2 us  [the longest x3 8.3 us: local(): lax.ppermute(relayed, 'expert', [(a, a ^ j) for a in range(experts)])]
    ppermute x27, starting transfers between devices: 81 us -> 84.1 us  [local(): got[f] = lax.ppermute(message, ('dp', 'expert'), flows[f])]
  transfers between devices with their start and end apart: 38 -> 36, of which waited for: 16 -> 21; matrix products, arithmetic and copies ran while one was open for 2% -> 2% of each run, Pallas kernels for 20% -> 18%
where the time goes in v1:
time: 312 us; the launch traced here: 311 us
  waiting for transfers between devices  104 us (33%)
  starting transfers between devices  89.8 us (29%)
  Pallas kernels  63 us (20%)
  local copies, waits for them, and re-layouts  31.1 us (10%)
  between operations  14.5 us (5%)
  matrix products  6.29 us (2%)
    ppermute x27, starting transfers between devices, local(): got[f] = lax.ppermute(message, ('dp', 'expert'), flows[f])  84.1 us
    ppermute x27, waiting for transfers between devices, local(): got[f] = lax.ppermute(message, ('dp', 'expert'), flows[f])  63.9 us
    pallas_call x51, Pallas kernels, call(): pl.pallas_call(body, name=name, out_shape=shapes, in_specs=specs, out_spe...  63 us
    unnamed x48, local copies, waits for them, and re-layouts  31 us
    psum x1, waiting for transfers between devices, local(): part = lax.psum(part, 'tensor')  19.5 us
    ppermute x3, waiting for transfers between devices, local(): lax.ppermute(relayed, 'expert', [(a, a ^ j) for a in range(experts)])  8.3 us
    ppermute x3, waiting for transfers between devices, local(): part = lax.ppermute(part, 'expert', [(a, a ^ j) for a in range(experts)])  6.4 us
    dot_general x10, matrix products, local(): lax.dot_general(chosen, part, (((0,), (0,)), ((), ())), preferred_element...  6.29 us
  transfers between devices with their start and end apart: 36, of which 21 were waited for; matrix products, arithmetic and copies ran while one was open for 2% of the time, Pallas kernels for 18%

profile of v1, /device:TPU:0, one launch (start us, length us, event | category | flops | bytes accessed | tf_op | source)
XLA Modules:
  0.0 310.7 jit_solution(5201171074476519442)
XLA Ops:
  8.2 5.7 %begin.1 = (s32[2,256]{1,0:T(2,128)S(1)}, bf16[128,768]{1,0:T(8,128)(2,1)S(1)}, bf16[128,768]{1,0:T(8,128)(2,1)S(1)}, bf16[128,768]{1,0:T(8,128)(2,1)S(1)}, bf16...) custom-call(s32[1]{0:T(128)} %bitcast.1.e_ref, ...), custom_call_target="tpu_custom_call" | custom-call | tf_op jit(solution)/shard_map/begin/pallas_call | solution.py:37
  13.9 2.6 copy-done.4
  16.5 2.7 copy-done.8
  19.3 5.0 %collective-permute-start.2 = (bf16[64,4096]{1,0:T(8,128)(2,1)S(1)}, bf16[64,4096]{1,0:T(8,128)(2,1)S(1)}, u32[]{:S(2)}, u32[]{:S(2)}) collective-permute-start(bf16[64,4096]{1,0:T(8,128)(2,1)S(1)} %combine.30), channel_id=1, source_target_pairs={{0,8},{10,2},{4,12},{14,6},{8,16},{18,10},{12,20},{22,14},{16,24},... | collective-permute-start | bytes 1572872 | tf_op jit(solution)/shard_map/ppermute | solution.py:309
  24.3 1.3 collective-permute-start
  27.1 2.8 copy-done.5
  29.9 2.8 copy-done.9
  32.7 2.8 project.10
  35.8 4.5 %collective-permute-start.5 = (bf16[64,4096]{1,0:T(8,128)(2,1)S(1)}, bf16[64,4096]{1,0:T(8,128)(2,1)S(1)}, u32[]{:S(2)}, u32[]{:S(2)}) collective-permute-start(bf16[64,4096]{1,0:T(8,128)(2,1)S(1)} %combine.31.refs_4_), channel_id=1, source_target_pairs={{0,8},{10,2},{4,12},{14,6},{8,16},{18,10},{12,20},{22,14},{16,24},... | collective-permute-start | bytes 1572872 | tf_op jit(solution)/shard_map/ppermute | solution.py:309
  40.3 2.8 project.11
  43.3 1.3 collective-permute-start.3
  44.6 1.6 collective-permute-start.4
  46.2 2.1 collective-permute-done.5.refs_0_
  48.5 4.7 %collective-permute-start.7 = (bf16[64,4096]{1,0:T(8,128)(2,1)S(1)}, bf16[64,4096]{1,0:T(8,128)(2,1)S(1)}, u32[]{:S(2)}, u32[]{:S(2)}) collective-permute-start(bf16[64,4096]{1,0:T(8,128)(2,1)S(1)} %combine.33.refs_5_), channel_id=1, source_target_pairs={{0,8},{10,2},{4,12},{14,6},{8,16},{18,10},{12,20},{22,14},{16,24},... | collective-permute-start | bytes 1572872 | tf_op jit(solution)/shard_map/ppermute | solution.py:309
  53.2 2.8 project.12
  56.8 1.3 collective-permute-start.6
  58.1 4.1 %collective-permute-done.7.refs_0_ = bf16[64,4096]{1,0:T(8,128)(2,1)S(1)} collective-permute-done((bf16[64,4096]{1,0:T(8,128)(2,1)S(1)}, bf16[64,4096]{1,0:T(8,128)(2,1)S(1)}, u32[]{:S(2)}, u32[]{:S(2)}) %collective-permute-start.7) | collective-permute-done | bytes 524320 | tf_op jit(solution)/shard_map/ppermute | solution.py:309
  62.6 2.8 project.13
  65.5 2.5 collective-permute-done.6.refs_1_
  68.8 1.3 collective-permute-start.9
  70.1 4.6 %collective-permute-start.8 = (bf16[64,4096]{1,0:T(8,128)(2,1)S(1)}, bf16[64,4096]{1,0:T(8,128)(2,1)S(1)}, u32[]{:S(2)}, u32[]{:S(2)}) collective-permute-start(bf16[64,4096]{1,0:T(8,128)(2,1)S(1)} %get-tuple-element.91.refs_4_), channel_id=1, source_target_pairs={{0,8},{10,2},{4,12},{14,6},{8,16},{18,10},{12,20},{22,14},{16,24},... | collective-permute-start | bytes 1572872 | tf_op jit(solution)/shard_map/ppermute | solution.py:309
  74.7 10.3 %collective-permute-done.8.refs_1_ = bf16[64,4096]{1,0:T(8,128)(2,1)S(1)} collective-permute-done((bf16[64,4096]{1,0:T(8,128)(2,1)S(1)}, bf16[64,4096]{1,0:T(8,128)(2,1)S(1)}, u32[]{:S(2)}, u32[]{:S(2)}) %collective-permute-start.8) | collective-permute-done | bytes 524320 | tf_op jit(solution)/shard_map/ppermute | solution.py:309
  85.8 4.4 %collective-permute-start.11 = (bf16[96,4096]{1,0:T(8,128)(2,1)S(1)}, bf16[96,4096]{1,0:T(8,128)(2,1)S(1)}, u32[]{:S(2)}, u32[]{:S(2)}) collective-permute-start(bf16[96,4096]{1,0:T(8,128)(2,1)S(1)} %get-tuple-element.96.refs_5_.two_ref), channel_id=1, source_target_pairs={{0,8},{10,2},{4,12},{14,6},{8,16},{18,10},{12,20},{22,14},{16,24},... | collective-permute-start | bytes 2359304 | tf_op jit(solution)/shard_map/ppermute | solution.py:309
  90.4 7.1 %collective-permute-done.10.refs_2_.refs_1_ = bf16[128,768]{1,0:T(8,128)(2,1)S(1)} collective-permute-done((bf16[128,768]{1,0:T(8,128)(2,1)S(1)}, bf16[128,768]{1,0:T(8,128)(2,1)S(1)}, u32[]{:S(2)}, u32[]{:S(2)}) %collective-permute-start.10) | collective-permute-done | bytes 196640 | tf_op jit(solution)/shard_map/ppermute | solution.py:312
  97.5 2.8 project.14
  101.2 1.3 collective-permute-start.12
  104.6 4.8 %collective-permute-start.13 = (bf16[96,4096]{1,0:T(8,128)(2,1)S(1)}, bf16[96,4096]{1,0:T(8,128)(2,1)S(1)}, u32[]{:S(2)}, u32[]{:S(2)}) collective-permute-start(bf16[96,4096]{1,0:T(8,128)(2,1)S(1)} %get-tuple-element.103.refs_4_.two_ref), channel_id=1, source_target_pairs={{0,8},{10,2},{4,12},{14,6},{8,16},{18,10},{12,20},{22,14},{16,24},... | collective-permute-start | bytes 2359304 | tf_op jit(solution)/shard_map/ppermute | solution.py:309
  109.4 2.8 project.15
  112.2 6.9 %collective-permute-done.12.refs_1_ = bf16[96,4096]{1,0:T(8,128)(2,1)S(1)} collective-permute-done((bf16[96,4096]{1,0:T(8,128)(2,1)S(1)}, bf16[96,4096]{1,0:T(8,128)(2,1)S(1)}, u32[]{:S(2)}, u32[]{:S(2)}) %collective-permute-start.12) | collective-permute-done | bytes 786464 | tf_op jit(solution)/shard_map/ppermute | solution.py:309
  120.0 1.3 collective-permute-start.14
  123.3 4.6 %collective-permute-start.15 = (bf16[96,4096]{1,0:T(8,128)(2,1)S(1)}, bf16[96,4096]{1,0:T(8,128)(2,1)S(1)}, u32[]{:S(2)}, u32[]{:S(2)}) collective-permute-start(bf16[96,4096]{1,0:T(8,128)(2,1)S(1)} %get-tuple-element.109.refs_5_.two_ref), channel_id=1, source_target_pairs={{0,8},{10,2},{4,12},{14,6},{8,16},{18,10},{12,20},{22,14},{16,24},... | collective-permute-start | bytes 2359304 | tf_op jit(solution)/shard_map/ppermute | solution.py:309
  127.9 2.8 project.16
  130.8 8.2 %collective-permute-done.14.refs_1_ = bf16[96,4096]{1,0:T(8,128)(2,1)S(1)} collective-permute-done((bf16[96,4096]{1,0:T(8,128)(2,1)S(1)}, bf16[96,4096]{1,0:T(8,128)(2,1)S(1)}, u32[]{:S(2)}, u32[]{:S(2)}) %collective-permute-start.14) | collective-permute-done | bytes 786464 | tf_op jit(solution)/shard_map/ppermute | solution.py:309
  139.8 1.3 collective-permute-start.16
  143.2 4.6 %collective-permute-start.17 = (bf16[96,4096]{1,0:T(8,128)(2,1)S(1)}, bf16[96,4096]{1,0:T(8,128)(2,1)S(1)}, u32[]{:S(2)}, u32[]{:S(2)}) collective-permute-start(bf16[96,4096]{1,0:T(8,128)(2,1)S(1)} %get-tuple-element.115.refs_4_.two_ref), channel_id=1, source_target_pairs={{0,8},{10,2},{4,12},{14,6},{8,16},{18,10},{12,20},{22,14},{16,24},... | collective-permute-start | bytes 2359304 | tf_op jit(solution)/shard_map/ppermute | solution.py:309
  147.8 2.8 project.17
  150.7 9.3 %collective-permute-done.16.refs_1_ = bf16[96,4096]{1,0:T(8,128)(2,1)S(1)} collective-permute-done((bf16[96,4096]{1,0:T(8,128)(2,1)S(1)}, bf16[96,4096]{1,0:T(8,128)(2,1)S(1)}, u32[]{:S(2)}, u32[]{:S(2)}) %collective-permute-start.16) | collective-permute-done | bytes 786464 | tf_op jit(solution)/shard_map/ppermute | solution.py:309
  160.8 1.3 collective-permute-start.18
  164.2 6.9 %collective-permute-start.19 = (bf16[96,4096]{1,0:T(8,128)(2,1)S(1)}, bf16[96,4096]{1,0:T(8,128)(2,1)}, u32[]{:S(2)}, u32[]{:S(2)}) collective-permute-start(bf16[96,4096]{1,0:T(8,128)(2,1)S(1)} %get-tuple-element.121.refs_4_.two_ref), channel_id=1, source_target_pairs={{0,8},{10,2},{4,12},{14,6},{8,16},{18,10},{12,20},{22,14},{16,24},... | collective-permute-start | bytes 2359304 | tf_op jit(solution)/shard_map/ppermute | solution.py:309
  171.1 2.8 project.18
  174.8 9.2 %collective-permute-done.18.refs_1_ = bf16[96,4096]{1,0:T(8,128)(2,1)S(1)} collective-permute-done((bf16[96,4096]{1,0:T(8,128)(2,1)S(1)}, bf16[96,4096]{1,0:T(8,128)(2,1)S(1)}, u32[]{:S(2)}, u32[]{:S(2)}) %collective-permute-start.18) | collective-permute-done | bytes 786464 | tf_op jit(solution)/shard_map/ppermute | solution.py:309
  187.1 2.8 copy-done
  191.1 1.5 combine.47
  192.6 5.0 %collective-permute-start.22 = (bf16[96,4096]{1,0:T(8,128)(2,1)S(1)}, bf16[96,4096]{1,0:T(8,128)(2,1)S(1)}, u32[]{:S(2)}, u32[]{:S(2)}) collective-permute-start(bf16[96,4096]{1,0:T(8,128)(2,1)S(1)} %get-tuple-element.127.refs_3_.two_ref), channel_id=1, source_target_pairs={{0,8},{10,2},{4,12},{14,6},{8,16},{18,10},{12,20},{22,14},{16,24},... | collective-permute-start | bytes 2359304 | tf_op jit(solution)/shard_map/ppermute | solution.py:309
  197.6 2.9 copy-done.7
  200.5 2.9 copy-done.10
  203.4 2.8 project.19
  206.3 2.0 collective-permute-done.20.refs_1_
  208.3 1.4 combine.48
  209.8 1.5 collective-permute-start.23
  214.1 4.6 %collective-permute-start.24 = (bf16[32,4096]{1,0:T(8,128)(2,1)S(1)}, bf16[32,4096]{1,0:T(8,128)(2,1)S(1)}, u32[]{:S(2)}, u32[]{:S(2)}) collective-permute-start(bf16[32,4096]{1,0:T(8,128)(2,1)S(1)} %get-tuple-element.133.two_ref), channel_id=1, source_target_pairs={{0,8},{10,2},{4,12},{14,6},{8,16},{18,10},{12,20},{22,14},{16,24},... | collective-permute-start | bytes 786440 | tf_op jit(solution)/shard_map/ppermute | solution.py:309
  218.7 6.3 %collective-permute-done.23.refs_1_ = bf16[96,4096]{1,0:T(8,128)(2,1)S(1)} collective-permute-done((bf16[96,4096]{1,0:T(8,128)(2,1)S(1)}, bf16[96,4096]{1,0:T(8,128)(2,1)S(1)}, u32[]{:S(2)}, u32[]{:S(2)}) %collective-permute-start.23) | collective-permute-done | bytes 786464 | tf_op jit(solution)/shard_map/ppermute | solution.py:309
  229.1 4.6 %collective-permute-start.27 = (bf16[32,4096]{1,0:T(8,128)(2,1)S(1)}, bf16[32,4096]{1,0:T(8,128)(2,1)S(1)}, u32[]{:S(2)}, u32[]{:S(2)}) collective-permute-start(bf16[32,4096]{1,0:T(8,128)(2,1)S(1)} %combine.51.two_ref), channel_id=1, source_target_pairs={{0,8},{10,2},{4,12},{14,6},{8,16},{18,10},{12,20},{22,14},{16,24},... | collective-permute-start | bytes 786440 | tf_op jit(solution)/shard_map/ppermute | solution.py:309
  237.6 4.4 %collective-permute-start.29 = (bf16[32,4096]{1,0:T(8,128)(2,1)S(1)}, bf16[32,4096]{1,0:T(8,128)(2,1)S(1)}, u32[]{:S(2)}, u32[]{:S(2)}) collective-permute-start(bf16[32,4096]{1,0:T(8,128)(2,1)S(1)} %combine.53.two_ref), channel_id=1, source_target_pairs={{0,8},{10,2},{4,12},{14,6},{8,16},{18,10},{12,20},{22,14},{16,24},... | collective-permute-start | bytes 786440 | tf_op jit(solution)/shard_map/ppermute | solution.py:309
  243.8 2.8 copy-done.1
  249.1 4.6 %collective-permute-start.33 = (bf16[32,4096]{1,0:T(8,128)(2,1)S(1)}, bf16[32,4096]{1,0:T(8,128)(2,1)S(1)}, u32[]{:S(2)}, u32[]{:S(2)}) collective-permute-start(bf16[32,4096]{1,0:T(8,128)(2,1)S(1)} %combine.55.two_ref), channel_id=1, source_target_pairs={{0,8},{10,2},{4,12},{14,6},{8,16},{18,10},{12,20},{22,14},{16,24},... | collective-permute-start | bytes 786440 | tf_op jit(solution)/shard_map/ppermute | solution.py:309
  253.7 19.5 %all-reduce.3.cloned.1.call-done = (bf16[64,768]{1,0:T(8,128)(2,1)}, bf16[128,768]{1,0:T(8,128)(2,1)}, bf16[128,768]{1,0:T(8,128)(2,1)}) async-done(((bf16[64,768]{1,0:T(8,128)(2,1)}, bf16[128,768]{1,0:T(8,128)(2,1)}, bf16[128,768]{1,0:T(8,128)(2,1)}), (bf16[64,768]{1,0:T(8,128)(2,1)}, bf16[128,768]{1,0:T(8,128)(2,1)}, bf16[128,768]{1,0:T(8,128)(2,1)})) %all-reduce.3.cloned.1.call-update) | async-done | bytes 491536 | tf_op jit(solution)/shard_map/psum | solution.py:357
  275.7 1.5 collective-permute-start.26
  277.3 2.8 copy-done.2
  281.4 2.8 copy-done.3
  286.1 1.5 collective-permute-start.31
  287.6 3.5 %collective-permute-done.34 = bf16[64,768]{1,0:T(8,128)(2,1)S(1)} collective-permute-done((bf16[64,768]{1,0:T(8,128)(2,1)S(1)}, bf16[64,768]{1,0:T(8,128)(2,1)S(1)}, u32[]{:S(2)}, u32[]{:S(2)}) %collective-permute-start.34) | collective-permute-done | bytes 98336 | tf_op jit(solution)/shard_map/ppermute | solution.py:354
  292.3 2.4 collective-permute-done.31
  295.2 6.4 %collective-permute-done.32 = bf16[128,768]{1,0:T(8,128)(2,1)S(1)} collective-permute-done((bf16[128,768]{1,0:T(8,128)(2,1)S(1)}, bf16[128,768]{1,0:T(8,128)(2,1)S(1)}, u32[]{:S(2)}, u32[]{:S(2)}) %collective-permute-start.32) | collective-permute-done | bytes 196640 | tf_op jit(solution)/shard_map/ppermute | solution.py:359
  (146 shorter events, 48.1 us)
Async XLA Ops:
  6.5 266.7 %all-reduce.3.cloned.1.call-start = ((), (), s32[]{:S(2)}) async-start(), calls=%async_computation | async-start | bytes 983040 | tf_op jit(solution)/shard_map/psum | solution.py:357
  6.5 1.0 copy-start.13
  7.5 0.7 copy-start.16
  13.9 2.6 copy-start.4
  16.5 2.7 copy-start.8
  19.3 16.4 %collective-permute-start.2 = (bf16[64,4096]{1,0:T(8,128)(2,1)S(1)}, bf16[64,4096]{1,0:T(8,128)(2,1)S(1)}, u32[]{:S(2)}, u32[]{:S(2)}) collective-permute-start(bf16[64,4096]{1,0:T(8,128)(2,1)S(1)} %combine.30), channel_id=1, source_target_pairs={{0,8},{10,2},{4,12},{14,6},{8,16},{18,10},{12,20},{22,14},{16,24},... | collective-permute-start | bytes 1572872 | tf_op jit(solution)/shard_map/ppermute | solution.py:309
  24.3 18.8 %collective-permute-start = (bf16[64,4096]{1,0:T(8,128)(2,1)S(1)}, bf16[64,4096]{1,0:T(8,128)(2,1)S(1)}, u32[]{:S(2)}, u32[]{:S(2)}) collective-permute-start(bf16[64,4096]{1,0:T(8,128)(2,1)S(1)} %get-tuple-element.75.refs_4_), channel_id=1, source_target_pairs={{8,0},{2,10},{12,4},{6,14},{16,8},{10,18},{20,12},{14,22},{24,16},... | collective-permute-start | bytes 1572872 | tf_op jit(solution)/shard_map/ppermute | solution.py:309
  25.6 1.5 collective-permute-start.1
  27.1 2.8 copy-start.5
  29.9 2.8 copy-start.9
  32.7 7.6 %copy-start.6 = (bf16[768,4096]{1,0:T(8,128)(2,1)S(1)}, bf16[768,4096]{1,0:T(8,128)(2,1)}, u32[]{:S(2)}) copy-start(bf16[768,4096]{1,0:T(8,128)(2,1)} %copy-done.4) | copy-start | bytes 18874372
  35.8 12.5 %collective-permute-start.5 = (bf16[64,4096]{1,0:T(8,128)(2,1)S(1)}, bf16[64,4096]{1,0:T(8,128)(2,1)S(1)}, u32[]{:S(2)}, u32[]{:S(2)}) collective-permute-start(bf16[64,4096]{1,0:T(8,128)(2,1)S(1)} %combine.31.refs_4_), channel_id=1, source_target_pairs={{0,8},{10,2},{4,12},{14,6},{8,16},{18,10},{12,20},{22,14},{16,24},... | collective-permute-start | bytes 1572872 | tf_op jit(solution)/shard_map/ppermute | solution.py:309
  43.3 13.4 %collective-permute-start.3 = (bf16[64,4096]{1,0:T(8,128)(2,1)S(1)}, bf16[64,4096]{1,0:T(8,128)(2,1)S(1)}, u32[]{:S(2)}, u32[]{:S(2)}) collective-permute-start(bf16[64,4096]{1,0:T(8,128)(2,1)S(1)} %get-tuple-element.84), channel_id=1, source_target_pairs={{8,0},{2,10},{12,4},{6,14},{16,8},{10,18},{20,12},{14,22},{24,16},... | collective-permute-start | bytes 1572872 | tf_op jit(solution)/shard_map/ppermute | solution.py:309
  44.6 8.6 %collective-permute-start.4 = (bf16[128,768]{1,0:T(8,128)(2,1)S(1)}, bf16[128,768]{1,0:T(8,128)(2,1)S(1)}, u32[]{:S(2)}, u32[]{:S(2)}) collective-permute-start(bf16[128,768]{1,0:T(8,128)(2,1)S(1)} %get-tuple-element.86), channel_id=1, source_target_pairs={{0,4},{2,6},{4,0},{6,2},{1,5},{3,7},{5,1},{7,3},{8,12},{10,14},{12... | collective-permute-start | bytes 589832 | tf_op jit(solution)/shard_map/ppermute | solution.py:312
  48.3 14.3 %slice-start.4 = ((s8[6291456]{0:T(1024)(128)(4,1)}), s8[4194304]{0:T(1024)(128)(4,1)S(1)}, s32[]{:S(2)}) async-start(s8[6291456]{0:T(1024)(128)(4,1)} %bitcast.34), calls=%async_computation.5 | async-start | bytes 8388608
  48.5 14.1 %slice-start.5 = ((s8[6291456]{0:T(1024)(128)(4,1)}), s8[2097152]{0:T(1024)(128)(4,1)S(1)}, s32[]{:S(2)}) async-start(s8[6291456]{0:T(1024)(128)(4,1)} %bitcast.34), calls=%async_computation.6 | async-start | bytes 4194304
  48.5 13.8 %collective-permute-start.7 = (bf16[64,4096]{1,0:T(8,128)(2,1)S(1)}, bf16[64,4096]{1,0:T(8,128)(2,1)S(1)}, u32[]{:S(2)}, u32[]{:S(2)}) collective-permute-start(bf16[64,4096]{1,0:T(8,128)(2,1)S(1)} %combine.33.refs_5_), channel_id=1, source_target_pairs={{0,8},{10,2},{4,12},{14,6},{8,16},{18,10},{12,20},{22,14},{16,24},... | collective-permute-start | bytes 1572872 | tf_op jit(solution)/shard_map/ppermute | solution.py:309
  56.8 11.1 %collective-permute-start.6 = (bf16[64,4096]{1,0:T(8,128)(2,1)S(1)}, bf16[64,4096]{1,0:T(8,128)(2,1)S(1)}, u32[]{:S(2)}, u32[]{:S(2)}) collective-permute-start(bf16[64,4096]{1,0:T(8,128)(2,1)S(1)} %combine.34), channel_id=1, source_target_pairs={{8,0},{2,10},{12,4},{6,14},{16,8},{10,18},{20,12},{14,22},{24,16},... | collective-permute-start | bytes 1572872 | tf_op jit(solution)/shard_map/ppermute | solution.py:309
  68.8 31.5 %collective-permute-start.9 = (bf16[96,4096]{1,0:T(8,128)(2,1)S(1)}, bf16[96,4096]{1,0:T(8,128)(2,1)S(1)}, u32[]{:S(2)}, u32[]{:S(2)}) collective-permute-start(bf16[96,4096]{1,0:T(8,128)(2,1)S(1)} %get-tuple-element.93.one_ref), channel_id=1, source_target_pairs={{8,0},{2,10},{12,4},{6,14},{16,8},{10,18},{20,12},{14,22},{24,16},... | collective-permute-start | bytes 2359304 | tf_op jit(solution)/shard_map/ppermute | solution.py:309
  70.1 14.9 %collective-permute-start.8 = (bf16[64,4096]{1,0:T(8,128)(2,1)S(1)}, bf16[64,4096]{1,0:T(8,128)(2,1)S(1)}, u32[]{:S(2)}, u32[]{:S(2)}) collective-permute-start(bf16[64,4096]{1,0:T(8,128)(2,1)S(1)} %get-tuple-element.91.refs_4_), channel_id=1, source_target_pairs={{0,8},{10,2},{4,12},{14,6},{8,16},{18,10},{12,20},{22,14},{16,24},... | collective-permute-start | bytes 1572872 | tf_op jit(solution)/shard_map/ppermute | solution.py:309
  85.8 17.9 %collective-permute-start.11 = (bf16[96,4096]{1,0:T(8,128)(2,1)S(1)}, bf16[96,4096]{1,0:T(8,128)(2,1)S(1)}, u32[]{:S(2)}, u32[]{:S(2)}) collective-permute-start(bf16[96,4096]{1,0:T(8,128)(2,1)S(1)} %get-tuple-element.96.refs_5_.two_ref), channel_id=1, source_target_pairs={{0,8},{10,2},{4,12},{14,6},{8,16},{18,10},{12,20},{22,14},{16,24},... | collective-permute-start | bytes 2359304 | tf_op jit(solution)/shard_map/ppermute | solution.py:309
  90.3 12.2 %slice-start = ((s8[6291456]{0:T(1024)(128)(4,1)}), s8[4194304]{0:T(1024)(128)(4,1)S(1)}, s32[]{:S(2)}) async-start(s8[6291456]{0:T(1024)(128)(4,1)} %bitcast.19), calls=%async_computation.1 | async-start | bytes 8388608
  90.3 12.2 %slice-start.1 = ((s8[6291456]{0:T(1024)(128)(4,1)}), s8[2097152]{0:T(1024)(128)(4,1)S(1)}, s32[]{:S(2)}) async-start(s8[6291456]{0:T(1024)(128)(4,1)} %bitcast.19), calls=%async_computation.2 | async-start | bytes 4194304
  90.3 7.2 %collective-permute-start.10 = (bf16[128,768]{1,0:T(8,128)(2,1)S(1)}, bf16[128,768]{1,0:T(8,128)(2,1)S(1)}, u32[]{:S(2)}, u32[]{:S(2)}) collective-permute-start(bf16[128,768]{1,0:T(8,128)(2,1)S(1)} %get-tuple-element.98), channel_id=1, source_target_pairs={{0,6},{2,4},{4,2},{6,0},{1,7},{3,5},{5,3},{7,1},{8,14},{10,12},{12... | collective-permute-start | bytes 589832 | tf_op jit(solution)/shard_map/ppermute | solution.py:312
  101.2 17.9 %collective-permute-start.12 = (bf16[96,4096]{1,0:T(8,128)(2,1)S(1)}, bf16[96,4096]{1,0:T(8,128)(2,1)S(1)}, u32[]{:S(2)}, u32[]{:S(2)}) collective-permute-start(bf16[96,4096]{1,0:T(8,128)(2,1)S(1)} %get-tuple-element.100.rest_0_.one_ref), channel_id=1, source_target_pairs={{8,0},{2,10},{12,4},{6,14},{16,8},{10,18},{20,12},{14,22},{24,16},... | collective-permute-start | bytes 2359304 | tf_op jit(solution)/shard_map/ppermute | solution.py:309
  104.6 17.9 %collective-permute-start.13 = (bf16[96,4096]{1,0:T(8,128)(2,1)S(1)}, bf16[96,4096]{1,0:T(8,128)(2,1)S(1)}, u32[]{:S(2)}, u32[]{:S(2)}) collective-permute-start(bf16[96,4096]{1,0:T(8,128)(2,1)S(1)} %get-tuple-element.103.refs_4_.two_ref), channel_id=1, source_target_pairs={{0,8},{10,2},{4,12},{14,6},{8,16},{18,10},{12,20},{22,14},{16,24},... | collective-permute-start | bytes 2359304 | tf_op jit(solution)/shard_map/ppermute | solution.py:309
  120.0 19.0 %collective-permute-start.14 = (bf16[96,4096]{1,0:T(8,128)(2,1)S(1)}, bf16[96,4096]{1,0:T(8,128)(2,1)S(1)}, u32[]{:S(2)}, u32[]{:S(2)}) collective-permute-start(bf16[96,4096]{1,0:T(8,128)(2,1)S(1)} %get-tuple-element.106.rest_0_.one_ref), channel_id=1, source_target_pairs={{8,0},{2,10},{12,4},{6,14},{16,8},{10,18},{20,12},{14,22},{24,16},... | collective-permute-start | bytes 2359304 | tf_op jit(solution)/shard_map/ppermute | solution.py:309
  123.3 19.0 %collective-permute-start.15 = (bf16[96,4096]{1,0:T(8,128)(2,1)S(1)}, bf16[96,4096]{1,0:T(8,128)(2,1)S(1)}, u32[]{:S(2)}, u32[]{:S(2)}) collective-permute-start(bf16[96,4096]{1,0:T(8,128)(2,1)S(1)} %get-tuple-element.109.refs_5_.two_ref), channel_id=1, source_target_pairs={{0,8},{10,2},{4,12},{14,6},{8,16},{18,10},{12,20},{22,14},{16,24},... | collective-permute-start | bytes 2359304 | tf_op jit(solution)/shard_map/ppermute | solution.py:309
  139.8 20.1 %collective-permute-start.16 = (bf16[96,4096]{1,0:T(8,128)(2,1)S(1)}, bf16[96,4096]{1,0:T(8,128)(2,1)S(1)}, u32[]{:S(2)}, u32[]{:S(2)}) collective-permute-start(bf16[96,4096]{1,0:T(8,128)(2,1)S(1)} %get-tuple-element.112.rest_0_.one_ref), channel_id=1, source_target_pairs={{8,0},{2,10},{12,4},{6,14},{16,8},{10,18},{20,12},{14,22},{24,16},... | collective-permute-start | bytes 2359304 | tf_op jit(solution)/shard_map/ppermute | solution.py:309
  143.2 20.1 %collective-permute-start.17 = (bf16[96,4096]{1,0:T(8,128)(2,1)S(1)}, bf16[96,4096]{1,0:T(8,128)(2,1)S(1)}, u32[]{:S(2)}, u32[]{:S(2)}) collective-permute-start(bf16[96,4096]{1,0:T(8,128)(2,1)S(1)} %get-tuple-element.115.refs_4_.two_ref), channel_id=1, source_target_pairs={{0,8},{10,2},{4,12},{14,6},{8,16},{18,10},{12,20},{22,14},{16,24},... | collective-permute-start | bytes 2359304 | tf_op jit(solution)/shard_map/ppermute | solution.py:309
  160.8 23.2 %collective-permute-start.18 = (bf16[96,4096]{1,0:T(8,128)(2,1)S(1)}, bf16[96,4096]{1,0:T(8,128)(2,1)S(1)}, u32[]{:S(2)}, u32[]{:S(2)}) collective-permute-start(bf16[96,4096]{1,0:T(8,128)(2,1)S(1)} %get-tuple-element.118.rest_0_.one_ref), channel_id=1, source_target_pairs={{8,0},{2,10},{12,4},{6,14},{16,8},{10,18},{20,12},{14,22},{24,16},... | collective-permute-start | bytes 2359304 | tf_op jit(solution)/shard_map/ppermute | solution.py:309
  164.2 26.9 %collective-permute-start.19 = (bf16[96,4096]{1,0:T(8,128)(2,1)S(1)}, bf16[96,4096]{1,0:T(8,128)(2,1)}, u32[]{:S(2)}, u32[]{:S(2)}) collective-permute-start(bf16[96,4096]{1,0:T(8,128)(2,1)S(1)} %get-tuple-element.121.refs_4_.two_ref), channel_id=1, source_target_pairs={{0,8},{10,2},{4,12},{14,6},{8,16},{18,10},{12,20},{22,14},{16,24},... | collective-permute-start | bytes 2359304 | tf_op jit(solution)/shard_map/ppermute | solution.py:309
  173.9 0.8 copy-start.11
  184.9 0.7 copy-start.14
  185.6 22.7 %collective-permute-start.20 = (bf16[96,4096]{1,0:T(8,128)(2,1)S(1)}, bf16[96,4096]{1,0:T(8,128)(2,1)}, u32[]{:S(2)}, u32[]{:S(2)}) collective-permute-start(bf16[96,4096]{1,0:T(8,128)(2,1)S(1)} %get-tuple-element.124.rest_0_.one_ref), channel_id=1, source_target_pairs={{8,0},{2,10},{12,4},{6,14},{16,8},{10,18},{20,12},{14,22},{24,16},... | collective-permute-start | bytes 2359304 | tf_op jit(solution)/shard_map/ppermute | solution.py:309
  187.1 2.8 copy-start
  189.9 1.2 copy-start.12
  189.9 1.2 copy-start.15
  192.6 20.7 %collective-permute-start.22 = (bf16[96,4096]{1,0:T(8,128)(2,1)S(1)}, bf16[96,4096]{1,0:T(8,128)(2,1)S(1)}, u32[]{:S(2)}, u32[]{:S(2)}) collective-permute-start(bf16[96,4096]{1,0:T(8,128)(2,1)S(1)} %get-tuple-element.127.refs_3_.two_ref), channel_id=1, source_target_pairs={{0,8},{10,2},{4,12},{14,6},{8,16},{18,10},{12,20},{22,14},{16,24},... | collective-permute-start | bytes 2359304 | tf_op jit(solution)/shard_map/ppermute | solution.py:309
  197.6 14.4 %slice-start.2 = ((s8[6291456]{0:T(1024)(128)(4,1)}), s8[4194304]{0:T(1024)(128)(4,1)S(1)}, s32[]{:S(2)}) async-start(s8[6291456]{0:T(1024)(128)(4,1)} %bitcast.26), calls=%async_computation.3 | async-start | bytes 8388608
  197.6 2.9 copy-start.7
  200.5 2.9 copy-start.10
  203.4 8.6 %slice-start.3 = ((s8[6291456]{0:T(1024)(128)(4,1)}), s8[2097152]{0:T(1024)(128)(4,1)S(1)}, s32[]{:S(2)}) async-start(s8[6291456]{0:T(1024)(128)(4,1)} %bitcast.26), calls=%async_computation.4 | async-start | bytes 4194304
  209.8 15.3 %collective-permute-start.23 = (bf16[96,4096]{1,0:T(8,128)(2,1)S(1)}, bf16[96,4096]{1,0:T(8,128)(2,1)S(1)}, u32[]{:S(2)}, u32[]{:S(2)}) collective-permute-start(bf16[96,4096]{1,0:T(8,128)(2,1)S(1)} %get-tuple-element.130.rest_0_.one_ref), channel_id=1, source_target_pairs={{8,0},{2,10},{12,4},{6,14},{16,8},{10,18},{20,12},{14,22},{24,16},... | collective-permute-start | bytes 2359304 | tf_op jit(solution)/shard_map/ppermute | solution.py:309
  214.1 14.4 %collective-permute-start.24 = (bf16[32,4096]{1,0:T(8,128)(2,1)S(1)}, bf16[32,4096]{1,0:T(8,128)(2,1)S(1)}, u32[]{:S(2)}, u32[]{:S(2)}) collective-permute-start(bf16[32,4096]{1,0:T(8,128)(2,1)S(1)} %get-tuple-element.133.two_ref), channel_id=1, source_target_pairs={{0,8},{10,2},{4,12},{14,6},{8,16},{18,10},{12,20},{22,14},{16,24},... | collective-permute-start | bytes 786440 | tf_op jit(solution)/shard_map/ppermute | solution.py:309
  225.9 8.3 %collective-permute-start.25 = (bf16[32,4096]{1,0:T(8,128)(2,1)S(1)}, bf16[32,4096]{1,0:T(8,128)(2,1)S(1)}, u32[]{:S(2)}, u32[]{:S(2)}) collective-permute-start(bf16[32,4096]{1,0:T(8,128)(2,1)S(1)} %get-tuple-element.135.rest_0_.one_ref), channel_id=1, source_target_pairs={{8,0},{2,10},{12,4},{6,14},{16,8},{10,18},{20,12},{14,22},{24,16},... | collective-permute-start | bytes 786440 | tf_op jit(solution)/shard_map/ppermute | solution.py:309
  228.5 14.4 %copy-start.17 = (f32[256,2]{0,1:T(2,128)S(1)}, f32[256,2]{0,1:T(2,128)}, u32[]{:S(2)}) copy-start(f32[256,2]{0,1:T(2,128)} %param.8) | copy-start | bytes 6148
  229.1 8.4 %collective-permute-start.27 = (bf16[32,4096]{1,0:T(8,128)(2,1)S(1)}, bf16[32,4096]{1,0:T(8,128)(2,1)S(1)}, u32[]{:S(2)}, u32[]{:S(2)}) collective-permute-start(bf16[32,4096]{1,0:T(8,128)(2,1)S(1)} %combine.51.two_ref), channel_id=1, source_target_pairs={{0,8},{10,2},{4,12},{14,6},{8,16},{18,10},{12,20},{22,14},{16,24},... | collective-permute-start | bytes 786440 | tf_op jit(solution)/shard_map/ppermute | solution.py:309
  235.4 8.3 %collective-permute-start.28 = (bf16[32,4096]{1,0:T(8,128)(2,1)S(1)}, bf16[32,4096]{1,0:T(8,128)(2,1)S(1)}, u32[]{:S(2)}, u32[]{:S(2)}) collective-permute-start(bf16[32,4096]{1,0:T(8,128)(2,1)S(1)} %combine.52.rest_0_.one_ref), channel_id=1, source_target_pairs={{8,0},{2,10},{12,4},{6,14},{16,8},{10,18},{20,12},{14,22},{24,16},... | collective-permute-start | bytes 786440 | tf_op jit(solution)/shard_map/ppermute | solution.py:309
  237.6 11.5 %collective-permute-start.29 = (bf16[32,4096]{1,0:T(8,128)(2,1)S(1)}, bf16[32,4096]{1,0:T(8,128)(2,1)S(1)}, u32[]{:S(2)}, u32[]{:S(2)}) collective-permute-start(bf16[32,4096]{1,0:T(8,128)(2,1)S(1)} %combine.53.two_ref), channel_id=1, source_target_pairs={{0,8},{10,2},{4,12},{14,6},{8,16},{18,10},{12,20},{22,14},{16,24},... | collective-permute-start | bytes 786440 | tf_op jit(solution)/shard_map/ppermute | solution.py:309
  243.8 2.8 copy-start.1
  247.7 29.5 %collective-permute-start.30 = (bf16[32,4096]{1,0:T(8,128)(2,1)S(1)}, bf16[32,4096]{1,0:T(8,128)(2,1)S(1)}, u32[]{:S(2)}, u32[]{:S(2)}) collective-permute-start(bf16[32,4096]{1,0:T(8,128)(2,1)S(1)} %combine.54.rest_0_.one_ref), channel_id=1, source_target_pairs={{8,0},{2,10},{12,4},{6,14},{16,8},{10,18},{20,12},{14,22},{24,16},... | collective-permute-start | bytes 786440 | tf_op jit(solution)/shard_map/ppermute | solution.py:309
  249.1 32.2 %collective-permute-start.33 = (bf16[32,4096]{1,0:T(8,128)(2,1)S(1)}, bf16[32,4096]{1,0:T(8,128)(2,1)S(1)}, u32[]{:S(2)}, u32[]{:S(2)}) collective-permute-start(bf16[32,4096]{1,0:T(8,128)(2,1)S(1)} %combine.55.two_ref), channel_id=1, source_target_pairs={{0,8},{10,2},{4,12},{14,6},{8,16},{18,10},{12,20},{22,14},{16,24},... | collective-permute-start | bytes 786440 | tf_op jit(solution)/shard_map/ppermute | solution.py:309
  273.2 18.7 %collective-permute-start.21 = (bf16[128,768]{1,0:T(8,128)(2,1)}, bf16[128,768]{1,0:T(8,128)(2,1)S(1)}, u32[]{:S(2)}, u32[]{:S(2)}) collective-permute-start(bf16[128,768]{1,0:T(8,128)(2,1)} %get-tuple-element.138), channel_id=1, source_target_pairs={{0,2},{2,0},{4,6},{6,4},{1,3},{3,1},{5,7},{7,5},{8,10},{10,8},{12,... | collective-permute-start | bytes 589832 | tf_op jit(solution)/shard_map/ppermute | solution.py:359
  275.7 26.6 %collective-permute-start.26 = (bf16[128,768]{1,0:T(8,128)(2,1)}, bf16[128,768]{1,0:T(8,128)(2,1)S(1)}, u32[]{:S(2)}, u32[]{:S(2)}) collective-permute-start(bf16[128,768]{1,0:T(8,128)(2,1)} %get-tuple-element.139), channel_id=1, source_target_pairs={{0,4},{2,6},{4,0},{6,2},{1,5},{3,7},{5,1},{7,3},{8,12},{10,14},{12... | collective-permute-start | bytes 589832 | tf_op jit(solution)/shard_map/ppermute | solution.py:359
  277.3 2.8 copy-start.2
  281.4 2.8 copy-start.3
  285.4 5.7 %collective-permute-start.34 = (bf16[64,768]{1,0:T(8,128)(2,1)S(1)}, bf16[64,768]{1,0:T(8,128)(2,1)S(1)}, u32[]{:S(2)}, u32[]{:S(2)}) collective-permute-start(bf16[64,768]{1,0:T(8,128)(2,1)S(1)} %pad_maximum_fusion.4), channel_id=1, source_target_pairs={{0,1},{1,0},{2,3},{3,2},{4,5},{5,4},{6,7},{7,6},{8,9},{9,8},{10,11... | collective-permute-start | bytes 294920 | tf_op jit(solution)/shard_map/ppermute | solution.py:354
  286.1 8.6 %collective-permute-start.31 = (bf16[128,768]{1,0:T(8,128)(2,1)S(1)}, bf16[128,768]{1,0:T(8,128)(2,1)S(1)}, u32[]{:S(2)}, u32[]{:S(2)}) collective-permute-start(bf16[128,768]{1,0:T(8,128)(2,1)S(1)} %pad_maximum_fusion.2), channel_id=1, source_target_pairs={{0,1},{1,0},{2,3},{3,2},{4,5},{5,4},{6,7},{7,6},{8,9},{9,8},{10,11... | collective-permute-start | bytes 589832 | tf_op jit(solution)/shard_map/ppermute | solution.py:354
  294.7 6.8 %collective-permute-start.32 = (bf16[128,768]{1,0:T(8,128)(2,1)S(1)}, bf16[128,768]{1,0:T(8,128)(2,1)S(1)}, u32[]{:S(2)}, u32[]{:S(2)}) collective-permute-start(bf16[128,768]{1,0:T(8,128)(2,1)S(1)} %add_convert_fusion), channel_id=1, source_target_pairs={{0,6},{2,4},{4,2},{6,0},{1,7},{3,5},{5,3},{7,1},{8,14},{10,12},{12... | collective-permute-start | bytes 589832 | tf_op jit(solution)/shard_map/ppermute | solution.py:359
Sparse Core Ops, SparseCore 0:
  242.9 30.2 all-reduce.2

commit v2 on v1

--- a/solution.py
+++ b/solution.py
@@ -55,6 +55,24 @@
     return jnp.where(mask, 1.0, 0.0).astype(BF16)
 
 
+def streamed(pieces, buffers, sems, use):
+    slots = buffers.shape[0]
+
+    def load(i):
+        return pltpu.make_async_copy(pieces[i], buffers.at[i % slots], sems.at[i % slots])
+
+    for i in range(min(slots, len(pieces))):
+        load(i).start()
+
+    def run(i):
+        load(i).wait()
+        use(i, buffers.at[i % slots])
+        if i + slots < len(pieces):
+            load(i + slots).start()
+
+    return run
+
+
 def begin(m, experts, capacity, e, ids, tokens, wg, wu):
     n, width = tokens.shape
     units = wg.shape[1]
@@ -64,21 +82,19 @@
 
     def body(e_ref, ids_hbm, tok_hbm, wg_hbm, wu_hbm, place_ref, *rest):
         rows = rest[:experts]
-        wg_ref, wu_ref, g_ref, u_ref, x_ref, ids_ref, tok_ref, sems, small = rest[experts:]
+        g_ref, u_ref, x_ref, ids_ref, tok_ref, buffers, sems, small = rest[experts:]
         ids_copy = pltpu.make_async_copy(ids_hbm, ids_ref, small.at[0])
         tok_copy = pltpu.make_async_copy(tok_hbm, tok_ref, small.at[1])
         ids_copy.start()
         tok_copy.start()
-        pairs = ((wg_hbm, wg_ref, g_ref), (wu_hbm, wu_ref, u_ref))
-
-        def load(k, t):
-            return pltpu.make_async_copy(
-                pairs[k][0].at[:, cuts[t]], pairs[k][1].at[:, cuts[t]], sems.at[k, t]
-            )
-
-        for t in range(len(cuts)):
-            for k in range(2):
-                load(k, t).start()
+
+        def use(i, w_ref):
+            (g_ref, u_ref)[i % 2][:, cuts[i // 2]] = jnp.dot(
+                x_ref[...], w_ref[...], preferred_element_type=F32
+            ).astype(BF16)
+
+        pieces = [w.at[:, c] for c in cuts for w in (wg_hbm, wu_hbm)]
+        run = streamed(pieces, buffers, sems, use)
         ids_copy.wait()
         index = lax.broadcasted_iota(I32, (names, n), 0)
         ids = [ids_ref[k : k + 1, :] for k in range(2)]
@@ -100,15 +116,12 @@
             if j == 0:
                 x_ref[:m] = picked[:m]
                 x_ref[m:] = picked[half : half + m]
-        for t in range(len(cuts)):
-            for k in range(2):
-                load(k, t).wait()
-                pairs[k][2][:, cuts[t]] = jnp.dot(
-                    x_ref[...], pairs[k][1][:, cuts[t]], preferred_element_type=F32
-                ).astype(BF16)
+        for i in range(len(pieces)):
+            run(i)
 
     shapes = [array(2, n, dtype=I32)] + [array(capacity, width)] * experts
-    shapes += [array(width, units)] * 2 + [array(2 * m, units)] * 2
+    shapes += [array(2 * m, units)] * 2
+    slots = 2 * len(cuts)
     out = call(
         body,
         "begin",
@@ -119,44 +132,62 @@
             pltpu.VMEM((2 * m, width), BF16),
             pltpu.VMEM((2, n), I32),
             pltpu.VMEM((n, width), BF16),
-            pltpu.SemaphoreType.DMA((2, len(cuts))),
+            pltpu.VMEM((slots, width, units // len(cuts)), BF16),
+            pltpu.SemaphoreType.DMA((slots,)),
             pltpu.SemaphoreType.DMA((2,)),
         ],
-        grant=36,
+        grant=48,
     )
-    return out[0], out[1 : 1 + experts], out[1 + experts : 3 + experts], out[3 + experts :]
-
-
-def project(m, spots, rows, sources, weights, tie):
-    used = sorted({c[0] for per_flow in sources for c in per_flow if c})
+    return out[0], out[1 : 1 + experts], out[1 + experts :]
+
+
+def project(m, spot, rows, plans, weights, tie):
+    used = sorted({c[0] for plan in plans for per_flow in plan for c in per_flow if c})
     width, units = weights[0].shape
-
-    def body(spot_ref, *refs):
+    total = 2 * m * len(plans)
+    cuts = tiles_of(units, 512)
+
+    def body(spot0_ref, spot1_ref, *refs):
         groups = dict(zip(used, refs))
-        wg_ref, wu_ref = refs[len(used) : len(used) + 2]
-        g_ref, u_ref, x_ref = refs[-3:]
-        for f in range(2):
-            options = [
-                jnp.zeros((m, width), BF16) if c is None else groups[c[0]][c[1] : c[1] + m, :]
-                for c in sources[f]
-            ]
-            x_ref[f * m : (f + 1) * m] = pick(options, spot_ref[f])
-        for cols in tiles_of(units, 1024):
-            for w_ref, out_ref in ((wg_ref, g_ref), (wu_ref, u_ref)):
-                out_ref[:, cols] = jnp.dot(
-                    x_ref[...], w_ref[:, cols], preferred_element_type=F32
-                ).astype(BF16)
-
+        w_hbm = refs[len(used) : len(used) + 2]
+        g_ref, u_ref, x_ref, buffers, sems = refs[-5:]
+
+        def use(i, w_ref):
+            (g_ref, u_ref)[i % 2][:, cuts[i // 2]] = jnp.dot(
+                x_ref[...], w_ref[...], preferred_element_type=F32
+            ).astype(BF16)
+
+        pieces = [w.at[:, c] for c in cuts for w in w_hbm]
+        run = streamed(pieces, buffers, sems, use)
+        for r, plan in enumerate(plans):
+            for f in range(2):
+                options = [
+                    jnp.zeros((m, width), BF16) if c is None else groups[c[0]][c[1] : c[1] + m, :]
+                    for c in plan[f]
+                ]
+                at = (2 * r + f) * m
+                x_ref[at : at + m] = pick(options, (spot0_ref, spot1_ref)[f][0])
+        for i in range(len(pieces)):
+            run(i)
+
+    args = (*spot, *(rows[j] for j in used), *weights, tie)
+    slots = min(8, 2 * len(cuts))
     return call(
         body,
         "project",
-        [array(2 * m, units)] * 2,
-        (spots, *(rows[j] for j in used), *weights, tie),
-        scratch=[pltpu.VMEM((2 * m, width), BF16)],
+        [array(total, units)] * 2,
+        args,
+        [SCALAR] * 2 + [WHOLE] * len(used) + [FAR] * 2 + [WHOLE],
+        [
+            pltpu.VMEM((total, width), BF16),
+            pltpu.VMEM((slots, width, units // len(cuts)), BF16),
+            pltpu.SemaphoreType.DMA((slots,)),
+        ],
+        grant=48,
     )
 
 
-def combine(m, units, f, first, came, partial, act, summing, sending, fresh, spots, ties, relay):
+def combine(m, units, f, first, came, partial, act, summing, sending, fresh, spot, ties, relay):
     args, use = [], {}
 
     def take(key, value):
@@ -164,11 +195,12 @@
             use[key] = len(args)
             args.append(value)
 
-    take("spots", spots if act is not None and came is not None else None)
+    take("spot", spot if act is not None and came is not None else None)
     take("came", came)
     if summing:
         take("g", partial[0])
         take("u", partial[1])
+        base = partial[2] + f * m
     take("act", act)
     take("relay", relay)
     taken = len(args)
@@ -192,7 +224,7 @@
             if summing:
                 total = []
                 for k, key in enumerate(("g", "u")):
-                    value = ref[key][f * m : (f + 1) * m, cols].astype(F32)
+                    value = ref[key][base : base + m, cols].astype(F32)
                     if not first:
                         value = value + ref["came"][k * m : (k + 1) * m, cols].astype(F32)
                     total.append(value)
@@ -205,7 +237,7 @@
                 if "came" in ref and came.shape[0] % (2 * m) == m:
                     h = ref["came"][came.shape[0] - m :, cols]
                     if "act" in ref:
-                        h = jnp.where(ref["spots"][f] == 0, ref["act"][:, cols], h)
+                        h = jnp.where(ref["spot"][0] == 0, ref["act"][:, cols], h)
                 else:
                     h = ref["act"][:, cols]
                 outs[0][sums:, cols] = h
@@ -224,15 +256,44 @@
     return (out[0] if rows else None), activated, relayed
 
 
-def lower(m, one, two, wd, tie):
-    columns = wd.shape[1]
-
-    def body(one_ref, two_ref, w_ref, *rest):
-        h = jnp.concatenate([r[r.shape[0] - m :, :] for r in (one_ref, two_ref)])
-        for cols in tiles_of(columns, 256):
-            rest[-1][:, cols] = jnp.dot(h, w_ref[:, cols], preferred_element_type=F32).astype(BF16)
-
-    return call(body, "lower", [array(2 * m, columns)], (one, two, wd, *tie))[0]
+def lower(m, pairs, wd, tie):
+    units, columns = wd.shape
+    total = 2 * m * len(pairs)
+    cuts = tiles_of(units, 512)
+    flat = [message for pair in pairs for message in pair]
+
+    def body(*refs):
+        messages, w_hbm = refs[: len(flat)], refs[len(flat)]
+        out_ref, sum_ref, buffers, sems = refs[-4:]
+
+        def use(i, w_ref):
+            h = jnp.concatenate([r[r.shape[0] - m :, cuts[i]] for r in messages])
+            part = jnp.dot(h, w_ref[...], preferred_element_type=F32)
+            if i:
+                part = part + sum_ref[...]
+            if i == len(cuts) - 1:
+                out_ref[...] = part.astype(BF16)
+            else:
+                sum_ref[...] = part
+
+        run = streamed([w_hbm.at[c, :] for c in cuts], buffers, sems, use)
+        for i in range(len(cuts)):
+            run(i)
+
+    slots = min(6, len(cuts))
+    return call(
+        body,
+        "lower",
+        [array(total, columns)],
+        (*flat, wd, *tie),
+        [WHOLE] * len(flat) + [FAR] + [WHOLE] * len(tie),
+        [
+            pltpu.VMEM((total, columns), F32),
+            pltpu.VMEM((slots, units // len(cuts), columns), BF16),
+            pltpu.SemaphoreType.DMA((slots,)),
+        ],
+        grant=48,
+    )[0]
 
 
 def local(tokens, route_ids, gates, w_gate, w_up, w_down):
@@ -254,12 +315,13 @@
 
     even = e % 2 == 0
     spot = [jnp.where(even, z, last - z), jnp.where(even, last - z, z)]
-    spots = jnp.stack(spot).astype(I32)
+    spot = [a.astype(I32).reshape(1) for a in spot]
     climb = [(a * experts + b, (a + 1) * experts + b) for a in range(last) for b in range(experts)]
     flows = [[(a, c) if a % experts % 2 == f else (c, a) for a, c in climb] for f in range(2)]
 
-    places, picked, weights, partial = begin(
-        m, experts, capacity, e.astype(I32).reshape(1), route_ids.T, tokens, w_gate[0], w_up[0]
+    weights = (w_gate[0], w_up[0])
+    places, picked, opening = begin(
+        m, experts, capacity, e.astype(I32).reshape(1), route_ids.T, tokens, *weights
     )
     rows = [picked[0]] + [None] * (experts - 1)
     due = {max(0, order.index((j, 0)) - 2): j for j in range(1, experts)}
@@ -275,15 +337,16 @@
 
     wd = w_down[0]
     sums_end = chunks + last
+    ticks = chunks + 2 * last + 1
+    partial = {0: (*opening, 0)}
     got = [None, None]
     act = [None, None]
     held = [{}, {}]
-    outs = []
+    outs = {}
     ties = []
-    for s in range(chunks + 2 * last + 1):
+    for s in range(ticks):
         summing = s < sums_end
-        following = None
-        for f in range(2):
+        for f in (0, 1):
             o = 1 - f
             first = last + 1 if f == 0 else last
             carries = first <= s < first + chunks + last
@@ -295,12 +358,12 @@
                 f,
                 s == 0,
                 got[f] if s else None,
-                partial,
+                partial.get(s),
                 act[o] if carries else None,
                 summing,
                 s < sums_end - 1,
                 summing and s >= last,
-                spots,
+                spot[f],
                 ties,
                 picked[due[s]] if f == 1 and s in due else None,
             )
@@ -312,28 +375,28 @@
                 rows[j] = lax.ppermute(relayed, "expert", [(a, a ^ j) for a in range(experts)])
             if carries:
                 held[o][s - first] = message
-            if f == 0 and s + 1 < sums_end and all(
-                rows[c[0]] is not None for per_flow in sources(s + 1) for c in per_flow if c
-            ):
-                following = project(m, spots, rows, sources(s + 1), weights, message)
-                ties.append(following[0])
-            if f == 1 and s + 1 < sums_end and following is None:
-                following = project(m, spots, rows, sources(s + 1), weights, message)
-                ties.append(following[0])
-            if f == 1 and s - last - 1 in held[1]:
-                q = s - last - 1
-                outs.append(lower(m, held[0][q], held[1][q], wd, (message,)))
-                ties.append(outs[-1])
-            if f == 0 and carries and s == chunks + 2 * last:
-                q = s - last - 1
-                outs.append(lower(m, held[0][q], held[1][q], wd, ()))
-        partial = following
+            if f == 1 and s + 1 < sums_end and s + 1 not in partial:
+                rounds = [r for r in (s + 1, s + 2) if r < sums_end]
+                g, u = project(m, spot, rows, [sources(r) for r in rounds], weights, message)
+                for k, r in enumerate(rounds):
+                    partial[r] = (g, u, 2 * m * k)
+                ties = [g]
+            if f == 1 or s == ticks - 1:
+                ready = [q for q in range(chunks + last) if q in held[0] and q in held[1]]
+                ready = [q for q in ready if q not in outs]
+                if len(ready) == 2 or (ready and ready[0] >= chunks):
+                    tie = () if s == ticks - 1 else (message,)
+                    pairs = [(held[0][q], held[1][q]) for q in ready]
+                    result = lower(m, pairs, wd, tie)
+                    for k, q in enumerate(ready):
+                        outs[q] = result[2 * m * k : 2 * m * (k + 1)]
+                    ties = ties + [result]
 
     def finished(start, stop):
         return [
             jnp.concatenate(
                 [
-                    pick([outs[c + a][f * m : (f + 1) * m] for a in range(depth)], spot[1 - f])
+                    pick([outs[c + a][f * m : (f + 1) * m] for a in range(depth)], spot[1 - f][0])
                     for c in range(start, stop)
                 ]
             )
@@ -350,7 +413,7 @@
     for j, start, stop, i in spans:
         size = (stop - start) * m
         part = jnp.concatenate(finished(start, stop))
-        if tensors == 2 and stop >= chunks - 1:
+        if tensors == 2:
             other = lax.ppermute(part, "tensor", [(0, 1), (1, 0)])
             part = (part.astype(F32) + other.astype(F32)).astype(BF16)
         else:

time: 312 us -> 270 us (0.87)
  local copies, waits for them, and re-layouts: 31.1 us -> 1.7 us
  between operations: 14.5 us -> 0.92 us
  starting transfers between devices: 89.8 us -> 94.7 us
    unnamed x48 -> x6, local copies, waits for them, and re-layouts: 31 us -> 1.68 us
    psum x1 -> x0, waiting for transfers between devices: 19.5 us -> none  [local(): part = lax.psum(part, 'tensor')]
    ppermute x27, waiting for transfers between devices: 63.9 us -> 74.3 us  [local(): got[f] = lax.ppermute(message, ('dp', 'expert'), flows[f])]
    ppermute x2 -> x5, starting transfers between devices: 2.16 us -> 6.46 us  [local(): other = lax.ppermute(part, 'tensor', [(0, 1), (1, 0)])]
    ppermute x2 -> x5, waiting for transfers between devices: 5.89 us -> 10.1 us  [local(): other = lax.ppermute(part, 'tensor', [(0, 1), (1, 0)])]
    pallas_call x51 -> x42, Pallas kernels: 63 us -> 65.4 us  [call(): pl.pallas_call(body, name=name, out_shape=shapes, in_specs=specs, out_spe...]
  transfers between devices with their start and end apart: 36 -> 38, of which waited for: 21 -> 18; matrix products, arithmetic and copies ran while one was open for 2% -> 1% of each run, Pallas kernels for 18% -> 22%
where the time goes in v2:
time: 270 us; the launch traced here: 269 us
  waiting for transfers between devices  101 us (37%)
  starting transfers between devices  94.7 us (35%)
  Pallas kernels  65.4 us (24%)
  matrix products  4.57 us (2%)
    ppermute x27, starting transfers between devices, local(): got[f] = lax.ppermute(message, ('dp', 'expert'), flows[f])  82.1 us
    ppermute x27, waiting for transfers between devices, local(): got[f] = lax.ppermute(message, ('dp', 'expert'), flows[f])  74.3 us
    pallas_call x42, Pallas kernels, call(): pl.pallas_call(body, name=name, out_shape=shapes, in_specs=specs, out_spe...  65.4 us
    ppermute x3, waiting for transfers between devices, local(): lax.ppermute(relayed, 'expert', [(a, a ^ j) for a in range(experts)])  10.6 us
    ppermute x5, waiting for transfers between devices, local(): other = lax.ppermute(part, 'tensor', [(0, 1), (1, 0)])  10.1 us
    ppermute x5, starting transfers between devices, local(): other = lax.ppermute(part, 'tensor', [(0, 1), (1, 0)])  6.46 us
    ppermute x3, waiting for transfers between devices, local(): part = lax.ppermute(part, 'expert', [(a, a ^ j) for a in range(experts)])  5.88 us
  transfers between devices with their start and end apart: 38, of which 18 were waited for; matrix products, arithmetic and copies ran while one was open for 1% of the time, Pallas kernels for 22%

profile of v2, /device:TPU:0, one launch (start us, length us, event | category | flops | bytes accessed | tf_op | source)
XLA Modules:
  0.0 268.6 jit_solution(13278000423589532346)
XLA Ops:
  1.7 5.7 %begin.1 = (s32[2,256]{1,0:T(2,128)S(1)}, bf16[128,768]{1,0:T(8,128)(2,1)S(1)}, bf16[128,768]{1,0:T(8,128)(2,1)S(1)}, bf16[128,768]{1,0:T(8,128)(2,1)S(1)}, bf16...) custom-call(s32[1]{0:T(128)} %bitcast.1.e_ref, s32[2,256]{1,0:T(2,128)S(1)} %bitcast.17, ...), custom_call_target="tpu_custom_call" | custom-call | tf_op jit(solution)/shard_map/begin/pallas_call | solution.py:37
  7.4 5.0 %collective-permute-start.5 = (bf16[64,4096]{1,0:T(8,128)(2,1)S(1)}, bf16[64,4096]{1,0:T(8,128)(2,1)S(1)}, u32[]{:S(2)}, u32[]{:S(2)}) collective-permute-start(bf16[64,4096]{1,0:T(8,128)(2,1)S(1)} %combine.32), channel_id=1, source_target_pairs={{0,8},{10,2},{4,12},{14,6},{8,16},{18,10},{12,20},{22,14},{16,24},... | collective-permute-start | bytes 1572872 | tf_op jit(solution)/shard_map/ppermute | solution.py:372
  12.5 1.3 collective-permute-start
  14.0 1.3 collective-permute-done.1.refs_1_.refs_0_
  15.3 5.6 %project.5 = (bf16[128,4096]{1,0:T(8,128)(2,1)S(1)}, bf16[128,4096]{1,0:T(8,128)(2,1)S(1)}) custom-call(s32[1]{0:T(128)} %bitcast.7.spot0_ref.refs_0_, s32[1]{0:T(128)} %bitcast.6.spot1_ref.refs_0_, bf16[128,768]{1,0:T(8,128)(2,1)S(1)} %get-tuple-element.64.refs_0_, bf16[128,768]{1,0:T(8,128)(2,1)S(1)} %collective-permute-done.1.refs_1_.refs_0_, ...), custom_call_target="tpu_custom_call" | custom-call | tf_op jit(solution)/shard_map/project/pallas_call | solution.py:37
  20.9 2.9 %collective-permute-done.5.refs_0_ = bf16[64,4096]{1,0:T(8,128)(2,1)S(1)} collective-permute-done((bf16[64,4096]{1,0:T(8,128)(2,1)S(1)}, bf16[64,4096]{1,0:T(8,128)(2,1)S(1)}, u32[]{:S(2)}, u32[]{:S(2)}) %collective-permute-start.5) | collective-permute-done | bytes 524320 | tf_op jit(solution)/shard_map/ppermute | solution.py:372
  24.0 4.4 %collective-permute-start.6 = (bf16[64,4096]{1,0:T(8,128)(2,1)S(1)}, bf16[64,4096]{1,0:T(8,128)(2,1)S(1)}, u32[]{:S(2)}, u32[]{:S(2)}) collective-permute-start(bf16[64,4096]{1,0:T(8,128)(2,1)S(1)} %combine.33), channel_id=1, source_target_pairs={{0,8},{10,2},{4,12},{14,6},{8,16},{18,10},{12,20},{22,14},{16,24},... | collective-permute-start | bytes 1572872 | tf_op jit(solution)/shard_map/ppermute | solution.py:372
  28.6 1.3 collective-permute-start.2
  29.9 10.5 %collective-permute-done.6.refs_0_ = bf16[64,4096]{1,0:T(8,128)(2,1)S(1)} collective-permute-done((bf16[64,4096]{1,0:T(8,128)(2,1)S(1)}, bf16[64,4096]{1,0:T(8,128)(2,1)S(1)}, u32[]{:S(2)}, u32[]{:S(2)}) %collective-permute-start.6) | collective-permute-done | bytes 524320 | tf_op jit(solution)/shard_map/ppermute | solution.py:372
  40.6 4.4 %collective-permute-start.7 = (bf16[64,4096]{1,0:T(8,128)(2,1)S(1)}, bf16[64,4096]{1,0:T(8,128)(2,1)S(1)}, u32[]{:S(2)}, u32[]{:S(2)}) collective-permute-start(bf16[64,4096]{1,0:T(8,128)(2,1)S(1)} %combine.34), channel_id=1, source_target_pairs={{0,8},{10,2},{4,12},{14,6},{8,16},{18,10},{12,20},{22,14},{16,24},... | collective-permute-start | bytes 1572872 | tf_op jit(solution)/shard_map/ppermute | solution.py:372
  45.2 1.3 collective-permute-start.3
  46.5 1.6 collective-permute-start.4
  48.1 4.2 %collective-permute-done.4.refs_2_.refs_1_ = bf16[128,768]{1,0:T(8,128)(2,1)S(1)} collective-permute-done((bf16[128,768]{1,0:T(8,128)(2,1)S(1)}, bf16[128,768]{1,0:T(8,128)(2,1)S(1)}, u32[]{:S(2)}, u32[]{:S(2)}) %collective-permute-start.4) | collective-permute-done | bytes 196640 | tf_op jit(solution)/shard_map/ppermute | solution.py:375
  52.2 5.6 %project.6 = (bf16[128,4096]{1,0:T(8,128)(2,1)S(1)}, bf16[128,4096]{1,0:T(8,128)(2,1)S(1)}) custom-call(s32[1]{0:T(128)} %bitcast.7.spot0_ref.refs_0_, s32[1]{0:T(128)} %bitcast.6.spot1_ref.refs_0_, bf16[128,768]{1,0:T(8,128)(2,1)S(1)} %get-tuple-element.64.refs_0_, bf16[128,768]{1,0:T(8,128)(2,1)S(1)} %collective-permute-done.1.refs_1_.refs_0_, ...), custom_call_target="tpu_custom_call" | custom-call | tf_op jit(solution)/shard_map/project/pallas_call | solution.py:37
  58.5 1.3 collective-permute-start.9
  59.8 5.2 %collective-permute-start.8 = (bf16[64,4096]{1,0:T(8,128)(2,1)S(1)}, bf16[64,4096]{1,0:T(8,128)(2,1)S(1)}, u32[]{:S(2)}, u32[]{:S(2)}) collective-permute-start(bf16[64,4096]{1,0:T(8,128)(2,1)S(1)} %get-tuple-element.76), channel_id=1, source_target_pairs={{0,8},{10,2},{4,12},{14,6},{8,16},{18,10},{12,20},{22,14},{16,24},... | collective-permute-start | bytes 1572872 | tf_op jit(solution)/shard_map/ppermute | solution.py:372
  65.0 8.9 %collective-permute-done.8.refs_1_ = bf16[64,4096]{1,0:T(8,128)(2,1)S(1)} collective-permute-done((bf16[64,4096]{1,0:T(8,128)(2,1)S(1)}, bf16[64,4096]{1,0:T(8,128)(2,1)S(1)}, u32[]{:S(2)}, u32[]{:S(2)}) %collective-permute-start.8) | collective-permute-done | bytes 524320 | tf_op jit(solution)/shard_map/ppermute | solution.py:372
  74.2 4.4 %collective-permute-start.10 = (bf16[96,4096]{1,0:T(8,128)(2,1)S(1)}, bf16[96,4096]{1,0:T(8,128)(2,1)S(1)}, u32[]{:S(2)}, u32[]{:S(2)}) collective-permute-start(bf16[96,4096]{1,0:T(8,128)(2,1)S(1)} %get-tuple-element.78.refs_1_), channel_id=1, source_target_pairs={{0,8},{10,2},{4,12},{14,6},{8,16},{18,10},{12,20},{22,14},{16,24},... | collective-permute-start | bytes 2359304 | tf_op jit(solution)/shard_map/ppermute | solution.py:372
  79.0 1.3 collective-permute-start.12
  80.3 2.5 collective-permute-start.11
  82.8 5.2 %collective-permute-done.11.refs_2_.refs_1_ = bf16[128,768]{1,0:T(8,128)(2,1)S(1)} collective-permute-done((bf16[128,768]{1,0:T(8,128)(2,1)S(1)}, bf16[128,768]{1,0:T(8,128)(2,1)S(1)}, u32[]{:S(2)}, u32[]{:S(2)}) %collective-permute-start.11) | collective-permute-done | bytes 196640 | tf_op jit(solution)/shard_map/ppermute | solution.py:375
  88.0 5.6 %project.7 = (bf16[128,4096]{1,0:T(8,128)(2,1)S(1)}, bf16[128,4096]{1,0:T(8,128)(2,1)S(1)}) custom-call(s32[1]{0:T(128)} %bitcast.7.spot0_ref.refs_0_, s32[1]{0:T(128)} %bitcast.6.spot1_ref.refs_0_, bf16[128,768]{1,0:T(8,128)(2,1)S(1)} %collective-permute-done.1.refs_1_.refs_0_, bf16[128,768]{1,0:T(8,128)(2,1)S(1)} %collective-permute-done.4.refs_2_.refs_1_, ...), custom_call_target="tpu_custom_call" | custom-call | tf_op jit(solution)/shard_map/project/pallas_call | solution.py:37
  95.0 4.4 %collective-permute-start.13 = (bf16[96,4096]{1,0:T(8,128)(2,1)S(1)}, bf16[96,4096]{1,0:T(8,128)(2,1)S(1)}, u32[]{:S(2)}, u32[]{:S(2)}) collective-permute-start(bf16[96,4096]{1,0:T(8,128)(2,1)S(1)} %get-tuple-element.85.refs_3_), channel_id=1, source_target_pairs={{0,8},{10,2},{4,12},{14,6},{8,16},{18,10},{12,20},{22,14},{16,24},... | collective-permute-start | bytes 2359304 | tf_op jit(solution)/shard_map/ppermute | solution.py:372
  99.7 1.3 collective-permute-start.14
  101.0 3.3 %lower.7.refs_5_ = bf16[128,768]{1,0:T(8,128)(2,1)S(1)} custom-call(bf16[96,4096]{1,0:T(8,128)(2,1)S(1)} %get-tuple-element.75.refs_0_, bf16[96,4096]{1,0:T(8,128)(2,1)S(1)} %get-tuple-element.78.refs_1_, bf16[96,4096]{1,0:T(8,128)(2,1)S(1)} %get-tuple-element.80.refs_5_.refs_2_, bf16[96,4096]{1,0:T(8,128)(2,1)S(1)} %get-tuple-element.85.refs_3_, ...), custom_call_target="tpu_custom_call" | custom-call | tf_op jit(solution)/shard_map/lower/pallas_call | solution.py:37
  104.4 12.2 %collective-permute-done.13.refs_1_ = bf16[96,4096]{1,0:T(8,128)(2,1)S(1)} collective-permute-done((bf16[96,4096]{1,0:T(8,128)(2,1)S(1)}, bf16[96,4096]{1,0:T(8,128)(2,1)S(1)}, u32[]{:S(2)}, u32[]{:S(2)}) %collective-permute-start.13) | collective-permute-done | bytes 786464 | tf_op jit(solution)/shard_map/ppermute | solution.py:372
  116.9 4.7 %collective-permute-start.15 = (bf16[96,4096]{1,0:T(8,128)(2,1)S(1)}, bf16[96,4096]{1,0:T(8,128)(2,1)S(1)}, u32[]{:S(2)}, u32[]{:S(2)}) collective-permute-start(bf16[96,4096]{1,0:T(8,128)(2,1)S(1)} %get-tuple-element.89.refs_1_), channel_id=1, source_target_pairs={{0,8},{10,2},{4,12},{14,6},{8,16},{18,10},{12,20},{22,14},{16,24},... | collective-permute-start | bytes 2359304 | tf_op jit(solution)/shard_map/ppermute | solution.py:372
  121.9 1.5 collective-permute-start.16
  123.4 5.6 %project.8 = (bf16[128,4096]{1,0:T(8,128)(2,1)S(1)}, bf16[128,4096]{1,0:T(8,128)(2,1)S(1)}) custom-call(s32[1]{0:T(128)} %bitcast.7.spot0_ref.refs_0_, s32[1]{0:T(128)} %bitcast.6.spot1_ref.refs_0_, bf16[128,768]{1,0:T(8,128)(2,1)S(1)} %get-tuple-element.64.refs_0_, bf16[128,768]{1,0:T(8,128)(2,1)S(1)} %collective-permute-done.4.refs_2_.refs_1_, ...), custom_call_target="tpu_custom_call" | custom-call | tf_op jit(solution)/shard_map/project/pallas_call | solution.py:37
  129.0 9.9 %collective-permute-done.15.refs_1_ = bf16[96,4096]{1,0:T(8,128)(2,1)S(1)} collective-permute-done((bf16[96,4096]{1,0:T(8,128)(2,1)S(1)}, bf16[96,4096]{1,0:T(8,128)(2,1)S(1)}, u32[]{:S(2)}, u32[]{:S(2)}) %collective-permute-start.15) | collective-permute-done | bytes 786464 | tf_op jit(solution)/shard_map/ppermute | solution.py:372
  139.2 4.4 %collective-permute-start.18 = (bf16[96,4096]{1,0:T(8,128)(2,1)S(1)}, bf16[96,4096]{1,0:T(8,128)(2,1)S(1)}, u32[]{:S(2)}, u32[]{:S(2)}) collective-permute-start(bf16[96,4096]{1,0:T(8,128)(2,1)S(1)} %get-tuple-element.95.refs_3_), channel_id=1, source_target_pairs={{0,8},{10,2},{4,12},{14,6},{8,16},{18,10},{12,20},{22,14},{16,24},... | collective-permute-start | bytes 2359304 | tf_op jit(solution)/shard_map/ppermute | solution.py:372
  144.0 1.3 collective-permute-start.19
  145.3 3.3 %lower.8.refs_5_ = bf16[128,768]{1,0:T(8,128)(2,1)S(1)} custom-call(bf16[96,4096]{1,0:T(8,128)(2,1)S(1)} %get-tuple-element.87.refs_5_.refs_0_, bf16[96,4096]{1,0:T(8,128)(2,1)S(1)} %get-tuple-element.89.refs_1_, bf16[96,4096]{1,0:T(8,128)(2,1)S(1)} %get-tuple-element.91.refs_5_.refs_2_, bf16[96,4096]{1,0:T(8,128)(2,1)S(1)} %get-tuple-element.95.refs_3_, ...), custom_call_target="tpu_custom_call" | custom-call | tf_op jit(solution)/shard_map/lower/pallas_call | solution.py:37
  148.7 11.6 %collective-permute-done.18.refs_1_ = bf16[96,4096]{1,0:T(8,128)(2,1)S(1)} collective-permute-done((bf16[96,4096]{1,0:T(8,128)(2,1)S(1)}, bf16[96,4096]{1,0:T(8,128)(2,1)S(1)}, u32[]{:S(2)}, u32[]{:S(2)}) %collective-permute-start.18) | collective-permute-done | bytes 786464 | tf_op jit(solution)/shard_map/ppermute | solution.py:372
  160.6 5.3 %collective-permute-start.20 = (bf16[96,4096]{1,0:T(8,128)(2,1)S(1)}, bf16[96,4096]{1,0:T(8,128)(2,1)}, u32[]{:S(2)}, u32[]{:S(2)}) collective-permute-start(bf16[96,4096]{1,0:T(8,128)(2,1)S(1)} %get-tuple-element.99.refs_1_), channel_id=1, source_target_pairs={{0,8},{10,2},{4,12},{14,6},{8,16},{18,10},{12,20},{22,14},{16,24},... | collective-permute-start | bytes 2359304 | tf_op jit(solution)/shard_map/ppermute | solution.py:372
  166.2 1.3 collective-permute-start.21
  167.6 5.6 %project.9 = (bf16[128,4096]{1,0:T(8,128)(2,1)S(1)}, bf16[128,4096]{1,0:T(8,128)(2,1)S(1)}) custom-call(s32[1]{0:T(128)} %bitcast.7.spot0_ref.refs_0_, s32[1]{0:T(128)} %bitcast.6.spot1_ref.refs_0_, bf16[128,768]{1,0:T(8,128)(2,1)S(1)} %get-tuple-element.64.refs_0_, bf16[128,768]{1,0:T(8,128)(2,1)S(1)} %collective-permute-done.11.refs_2_.refs_1_, ...), custom_call_target="tpu_custom_call" | custom-call | tf_op jit(solution)/shard_map/project/pallas_call | solution.py:37
  173.3 7.4 %collective-permute-done.20.refs_1_ = bf16[96,4096]{1,0:T(8,128)(2,1)} collective-permute-done((bf16[96,4096]{1,0:T(8,128)(2,1)S(1)}, bf16[96,4096]{1,0:T(8,128)(2,1)}, u32[]{:S(2)}, u32[]{:S(2)}) %collective-permute-start.20) | collective-permute-done | bytes 786464 | tf_op jit(solution)/shard_map/ppermute | solution.py:372
  180.7 1.4 combine.47
  182.1 4.5 %collective-permute-start.24 = (bf16[96,4096]{1,0:T(8,128)(2,1)S(1)}, bf16[96,4096]{1,0:T(8,128)(2,1)S(1)}, u32[]{:S(2)}, u32[]{:S(2)}) collective-permute-start(bf16[96,4096]{1,0:T(8,128)(2,1)S(1)} %get-tuple-element.105.refs_3_), channel_id=1, source_target_pairs={{0,8},{10,2},{4,12},{14,6},{8,16},{18,10},{12,20},{22,14},{16,24},... | collective-permute-start | bytes 2359304 | tf_op jit(solution)/shard_map/ppermute | solution.py:372
  186.7 1.4 combine.48
  188.1 1.3 collective-permute-start.25
  189.6 3.3 %lower.9.refs_5_ = bf16[128,768]{1,0:T(8,128)(2,1)S(1)} custom-call(bf16[96,4096]{1,0:T(8,128)(2,1)S(1)} %get-tuple-element.97.refs_5_.refs_0_, bf16[96,4096]{1,0:T(8,128)(2,1)S(1)} %get-tuple-element.99.refs_1_, bf16[96,4096]{1,0:T(8,128)(2,1)S(1)} %get-tuple-element.101.refs_4_.refs_2_, bf16[96,4096]{1,0:T(8,128)(2,1)S(1)} %get-tuple-element.105.refs_3_, ...), custom_call_target="tpu_custom_call" | custom-call | tf_op jit(solution)/shard_map/lower/pallas_call | solution.py:37
  192.9 8.5 %collective-permute-done.24.refs_1_ = bf16[96,4096]{1,0:T(8,128)(2,1)S(1)} collective-permute-done((bf16[96,4096]{1,0:T(8,128)(2,1)S(1)}, bf16[96,4096]{1,0:T(8,128)(2,1)S(1)}, u32[]{:S(2)}, u32[]{:S(2)}) %collective-permute-start.24) | collective-permute-done | bytes 786464 | tf_op jit(solution)/shard_map/ppermute | solution.py:372
  201.8 4.4 %collective-permute-start.26 = (bf16[32,4096]{1,0:T(8,128)(2,1)S(1)}, bf16[32,4096]{1,0:T(8,128)(2,1)S(1)}, u32[]{:S(2)}, u32[]{:S(2)}) collective-permute-start(bf16[32,4096]{1,0:T(8,128)(2,1)S(1)} %get-tuple-element.109.refs_1_), channel_id=1, source_target_pairs={{0,8},{10,2},{4,12},{14,6},{8,16},{18,10},{12,20},{22,14},{16,24},... | collective-permute-start | bytes 786440 | tf_op jit(solution)/shard_map/ppermute | solution.py:372
  206.6 1.3 collective-permute-start.27
  207.9 2.1 collective-permute-start.17
  210.1 4.6 %collective-permute-start.30 = (bf16[32,4096]{1,0:T(8,128)(2,1)S(1)}, bf16[32,4096]{1,0:T(8,128)(2,1)S(1)}, u32[]{:S(2)}, u32[]{:S(2)}) collective-permute-start(bf16[32,4096]{1,0:T(8,128)(2,1)S(1)} %combine.51.refs_3_), channel_id=1, source_target_pairs={{0,8},{10,2},{4,12},{14,6},{8,16},{18,10},{12,20},{22,14},{16,24},... | collective-permute-start | bytes 786440 | tf_op jit(solution)/shard_map/ppermute | solution.py:372
  215.2 3.3 %lower.10.refs_1_ = bf16[128,768]{1,0:T(8,128)(2,1)S(1)} custom-call(bf16[96,4096]{1,0:T(8,128)(2,1)S(1)} %get-tuple-element.107.refs_5_.refs_0_, bf16[32,4096]{1,0:T(8,128)(2,1)S(1)} %get-tuple-element.109.refs_1_, bf16[32,4096]{1,0:T(8,128)(2,1)S(1)} %get-tuple-element.111.refs_2_, bf16[32,4096]{1,0:T(8,128)(2,1)S(1)} %combine.51.refs_3_, ...), custom_call_target="tpu_custom_call" | custom-call | tf_op jit(solution)/shard_map/lower/pallas_call | solution.py:37
  218.5 1.3 collective-permute-start.31
  219.9 1.9 collective-permute-start.22
  221.8 4.6 %collective-permute-start.32 = (bf16[32,4096]{1,0:T(8,128)(2,1)S(1)}, bf16[32,4096]{1,0:T(8,128)(2,1)S(1)}, u32[]{:S(2)}, u32[]{:S(2)}) collective-permute-start(bf16[32,4096]{1,0:T(8,128)(2,1)S(1)} %combine.53.refs_1_), channel_id=1, source_target_pairs={{0,8},{10,2},{4,12},{14,6},{8,16},{18,10},{12,20},{22,14},{16,24},... | collective-permute-start | bytes 786440 | tf_op jit(solution)/shard_map/ppermute | solution.py:372
  226.8 5.3 %collective-permute-done.28 = bf16[128,768]{1,0:T(8,128)(2,1)S(1)} collective-permute-done((bf16[128,768]{1,0:T(8,128)(2,1)S(1)}, bf16[128,768]{1,0:T(8,128)(2,1)S(1)}, u32[]{:S(2)}, u32[]{:S(2)}) %collective-permute-start.28) | collective-permute-done | bytes 196640 | tf_op jit(solution)/shard_map/ppermute | solution.py:417
  232.2 1.6 collective-permute-start.29
  233.8 3.3 %lower.11.refs_1_ = bf16[64,768]{1,0:T(8,128)(2,1)S(1)} custom-call(bf16[32,4096]{1,0:T(8,128)(2,1)S(1)} %combine.52.refs_5_.refs_0_, bf16[32,4096]{1,0:T(8,128)(2,1)S(1)} %combine.53.refs_1_, bf16[4096,768]{1,0:T(8,128)(2,1)} %bitcast.22, bf16[32,4096]{1,0:T(8,128)(2,1)S(1)} %combine.54.refs_3_.refs_0_), custom_call_target="tpu_custom_call" | custom-call | tf_op jit(solution)/shard_map/lower/pallas_call | solution.py:37
  237.2 1.3 collective-permute-start.33
  238.5 4.8 %collective-permute-start.36 = (bf16[32,4096]{1,0:T(8,128)(2,1)S(1)}, bf16[32,4096]{1,0:T(8,128)(2,1)S(1)}, u32[]{:S(2)}, u32[]{:S(2)}) collective-permute-start(bf16[32,4096]{1,0:T(8,128)(2,1)S(1)} %combine.55.refs_1_), channel_id=1, source_target_pairs={{0,8},{10,2},{4,12},{14,6},{8,16},{18,10},{12,20},{22,14},{16,24},... | collective-permute-start | bytes 786440 | tf_op jit(solution)/shard_map/ppermute | solution.py:372
  245.8 3.3 %lower.12.refs_1_ = bf16[64,768]{1,0:T(8,128)(2,1)S(1)} custom-call(bf16[32,4096]{1,0:T(8,128)(2,1)S(1)} %combine.54.refs_3_.refs_0_, bf16[32,4096]{1,0:T(8,128)(2,1)S(1)} %combine.55.refs_1_, bf16[4096,768]{1,0:T(8,128)(2,1)} %bitcast.23, bf16[32,4096]{1,0:T(8,128)(2,1)S(1)} %combine.56.refs_3_.refs_0_), custom_call_target="tpu_custom_call" | custom-call | tf_op jit(solution)/shard_map/lower/pallas_call | solution.py:37
  249.2 3.3 %lower.13 = bf16[64,768]{1,0:T(8,128)(2,1)S(1)} custom-call(bf16[32,4096]{1,0:T(8,128)(2,1)S(1)} %combine.56.refs_3_.refs_0_, bf16[32,4096]{1,0:T(8,128)(2,1)S(1)} %combine.57.refs_1_, bf16[4096,768]{1,0:T(8,128)(2,1)} %bitcast.24), custom_call_target="tpu_custom_call" | custom-call | tf_op jit(solution)/shard_map/lower/pallas_call | solution.py:37
  252.6 1.6 collective-permute-start.37
  254.7 2.5 collective-permute-done.37
  257.6 2.3 collective-permute-done.34
  260.4 5.9 %collective-permute-done.35 = bf16[128,768]{1,0:T(8,128)(2,1)S(1)} collective-permute-done((bf16[128,768]{1,0:T(8,128)(2,1)S(1)}, bf16[128,768]{1,0:T(8,128)(2,1)S(1)}, u32[]{:S(2)}, u32[]{:S(2)}) %collective-permute-start.35) | collective-permute-done | bytes 196640 | tf_op jit(solution)/shard_map/ppermute | solution.py:422
  267.4 1.2 fusion.9
  (96 shorter events, 14.8 us)
Async XLA Ops:
  0.0 1.0 copy-start
  1.0 0.7 copy-start.1
  7.4 16.4 %collective-permute-start.5 = (bf16[64,4096]{1,0:T(8,128)(2,1)S(1)}, bf16[64,4096]{1,0:T(8,128)(2,1)S(1)}, u32[]{:S(2)}, u32[]{:S(2)}) collective-permute-start(bf16[64,4096]{1,0:T(8,128)(2,1)S(1)} %combine.32), channel_id=1, source_target_pairs={{0,8},{10,2},{4,12},{14,6},{8,16},{18,10},{12,20},{22,14},{16,24},... | collective-permute-start | bytes 1572872 | tf_op jit(solution)/shard_map/ppermute | solution.py:372
  12.5 15.9 %collective-permute-start = (bf16[64,4096]{1,0:T(8,128)(2,1)S(1)}, bf16[64,4096]{1,0:T(8,128)(2,1)S(1)}, u32[]{:S(2)}, u32[]{:S(2)}) collective-permute-start(bf16[64,4096]{1,0:T(8,128)(2,1)S(1)} %get-tuple-element.63.refs_4_), channel_id=1, source_target_pairs={{8,0},{2,10},{12,4},{6,14},{16,8},{10,18},{20,12},{14,22},{24,16},... | collective-permute-start | bytes 1572872 | tf_op jit(solution)/shard_map/ppermute | solution.py:372
  13.8 1.5 collective-permute-start.1
  24.0 16.4 %collective-permute-start.6 = (bf16[64,4096]{1,0:T(8,128)(2,1)S(1)}, bf16[64,4096]{1,0:T(8,128)(2,1)S(1)}, u32[]{:S(2)}, u32[]{:S(2)}) collective-permute-start(bf16[64,4096]{1,0:T(8,128)(2,1)S(1)} %combine.33), channel_id=1, source_target_pairs={{0,8},{10,2},{4,12},{14,6},{8,16},{18,10},{12,20},{22,14},{16,24},... | collective-permute-start | bytes 1572872 | tf_op jit(solution)/shard_map/ppermute | solution.py:372
  28.6 16.4 %collective-permute-start.2 = (bf16[64,4096]{1,0:T(8,128)(2,1)S(1)}, bf16[64,4096]{1,0:T(8,128)(2,1)S(1)}, u32[]{:S(2)}, u32[]{:S(2)}) collective-permute-start(bf16[64,4096]{1,0:T(8,128)(2,1)S(1)} %get-tuple-element.69), channel_id=1, source_target_pairs={{8,0},{2,10},{12,4},{6,14},{16,8},{10,18},{20,12},{14,22},{24,16},... | collective-permute-start | bytes 1572872 | tf_op jit(solution)/shard_map/ppermute | solution.py:372
  40.6 17.3 %collective-permute-start.7 = (bf16[64,4096]{1,0:T(8,128)(2,1)S(1)}, bf16[64,4096]{1,0:T(8,128)(2,1)S(1)}, u32[]{:S(2)}, u32[]{:S(2)}) collective-permute-start(bf16[64,4096]{1,0:T(8,128)(2,1)S(1)} %combine.34), channel_id=1, source_target_pairs={{0,8},{10,2},{4,12},{14,6},{8,16},{18,10},{12,20},{22,14},{16,24},... | collective-permute-start | bytes 1572872 | tf_op jit(solution)/shard_map/ppermute | solution.py:372
  45.2 13.0 %collective-permute-start.3 = (bf16[64,4096]{1,0:T(8,128)(2,1)S(1)}, bf16[64,4096]{1,0:T(8,128)(2,1)S(1)}, u32[]{:S(2)}, u32[]{:S(2)}) collective-permute-start(bf16[64,4096]{1,0:T(8,128)(2,1)S(1)} %combine.31.refs_5_), channel_id=1, source_target_pairs={{8,0},{2,10},{12,4},{6,14},{16,8},{10,18},{20,12},{14,22},{24,16},... | collective-permute-start | bytes 1572872 | tf_op jit(solution)/shard_map/ppermute | solution.py:372
  46.5 5.7 %collective-permute-start.4 = (bf16[128,768]{1,0:T(8,128)(2,1)S(1)}, bf16[128,768]{1,0:T(8,128)(2,1)S(1)}, u32[]{:S(2)}, u32[]{:S(2)}) collective-permute-start(bf16[128,768]{1,0:T(8,128)(2,1)S(1)} %get-tuple-element.70), channel_id=1, source_target_pairs={{0,4},{2,6},{4,0},{6,2},{1,5},{3,7},{5,1},{7,3},{8,12},{10,14},{12... | collective-permute-start | bytes 589832 | tf_op jit(solution)/shard_map/ppermute | solution.py:375
  58.5 20.2 %collective-permute-start.9 = (bf16[96,4096]{1,0:T(8,128)(2,1)S(1)}, bf16[96,4096]{1,0:T(8,128)(2,1)S(1)}, u32[]{:S(2)}, u32[]{:S(2)}) collective-permute-start(bf16[96,4096]{1,0:T(8,128)(2,1)S(1)} %get-tuple-element.75.refs_0_), channel_id=1, source_target_pairs={{8,0},{2,10},{12,4},{6,14},{16,8},{10,18},{20,12},{14,22},{24,16},... | collective-permute-start | bytes 2359304 | tf_op jit(solution)/shard_map/ppermute | solution.py:372
  59.8 14.2 %collective-permute-start.8 = (bf16[64,4096]{1,0:T(8,128)(2,1)S(1)}, bf16[64,4096]{1,0:T(8,128)(2,1)S(1)}, u32[]{:S(2)}, u32[]{:S(2)}) collective-permute-start(bf16[64,4096]{1,0:T(8,128)(2,1)S(1)} %get-tuple-element.76), channel_id=1, source_target_pairs={{0,8},{10,2},{4,12},{14,6},{8,16},{18,10},{12,20},{22,14},{16,24},... | collective-permute-start | bytes 1572872 | tf_op jit(solution)/shard_map/ppermute | solution.py:372
  74.2 20.4 %collective-permute-start.10 = (bf16[96,4096]{1,0:T(8,128)(2,1)S(1)}, bf16[96,4096]{1,0:T(8,128)(2,1)S(1)}, u32[]{:S(2)}, u32[]{:S(2)}) collective-permute-start(bf16[96,4096]{1,0:T(8,128)(2,1)S(1)} %get-tuple-element.78.refs_1_), channel_id=1, source_target_pairs={{0,8},{10,2},{4,12},{14,6},{8,16},{18,10},{12,20},{22,14},{16,24},... | collective-permute-start | bytes 2359304 | tf_op jit(solution)/shard_map/ppermute | solution.py:372
  79.0 20.4 %collective-permute-start.12 = (bf16[96,4096]{1,0:T(8,128)(2,1)S(1)}, bf16[96,4096]{1,0:T(8,128)(2,1)S(1)}, u32[]{:S(2)}, u32[]{:S(2)}) collective-permute-start(bf16[96,4096]{1,0:T(8,128)(2,1)S(1)} %get-tuple-element.80.refs_5_.refs_2_), channel_id=1, source_target_pairs={{8,0},{2,10},{12,4},{6,14},{16,8},{10,18},{20,12},{14,22},{24,16},... | collective-permute-start | bytes 2359304 | tf_op jit(solution)/shard_map/ppermute | solution.py:372
  80.3 7.6 %collective-permute-start.11 = (bf16[128,768]{1,0:T(8,128)(2,1)S(1)}, bf16[128,768]{1,0:T(8,128)(2,1)S(1)}, u32[]{:S(2)}, u32[]{:S(2)}) collective-permute-start(bf16[128,768]{1,0:T(8,128)(2,1)S(1)} %get-tuple-element.81), channel_id=1, source_target_pairs={{0,6},{2,4},{4,2},{6,0},{1,7},{3,5},{5,3},{7,1},{8,14},{10,12},{12... | collective-permute-start | bytes 589832 | tf_op jit(solution)/shard_map/ppermute | solution.py:375
  95.0 21.6 %collective-permute-start.13 = (bf16[96,4096]{1,0:T(8,128)(2,1)S(1)}, bf16[96,4096]{1,0:T(8,128)(2,1)S(1)}, u32[]{:S(2)}, u32[]{:S(2)}) collective-permute-start(bf16[96,4096]{1,0:T(8,128)(2,1)S(1)} %get-tuple-element.85.refs_3_), channel_id=1, source_target_pairs={{0,8},{10,2},{4,12},{14,6},{8,16},{18,10},{12,20},{22,14},{16,24},... | collective-permute-start | bytes 2359304 | tf_op jit(solution)/shard_map/ppermute | solution.py:372
  99.7 21.8 %collective-permute-start.14 = (bf16[96,4096]{1,0:T(8,128)(2,1)S(1)}, bf16[96,4096]{1,0:T(8,128)(2,1)S(1)}, u32[]{:S(2)}, u32[]{:S(2)}) collective-permute-start(bf16[96,4096]{1,0:T(8,128)(2,1)S(1)} %get-tuple-element.87.refs_5_.refs_0_), channel_id=1, source_target_pairs={{8,0},{2,10},{12,4},{6,14},{16,8},{10,18},{20,12},{14,22},{24,16},... | collective-permute-start | bytes 2359304 | tf_op jit(solution)/shard_map/ppermute | solution.py:372
  116.9 22.1 %collective-permute-start.15 = (bf16[96,4096]{1,0:T(8,128)(2,1)S(1)}, bf16[96,4096]{1,0:T(8,128)(2,1)S(1)}, u32[]{:S(2)}, u32[]{:S(2)}) collective-permute-start(bf16[96,4096]{1,0:T(8,128)(2,1)S(1)} %get-tuple-element.89.refs_1_), channel_id=1, source_target_pairs={{0,8},{10,2},{4,12},{14,6},{8,16},{18,10},{12,20},{22,14},{16,24},... | collective-permute-start | bytes 2359304 | tf_op jit(solution)/shard_map/ppermute | solution.py:372
  121.9 21.8 %collective-permute-start.16 = (bf16[96,4096]{1,0:T(8,128)(2,1)S(1)}, bf16[96,4096]{1,0:T(8,128)(2,1)S(1)}, u32[]{:S(2)}, u32[]{:S(2)}) collective-permute-start(bf16[96,4096]{1,0:T(8,128)(2,1)S(1)} %get-tuple-element.91.refs_5_.refs_2_), channel_id=1, source_target_pairs={{8,0},{2,10},{12,4},{6,14},{16,8},{10,18},{20,12},{14,22},{24,16},... | collective-permute-start | bytes 2359304 | tf_op jit(solution)/shard_map/ppermute | solution.py:372
  139.2 21.0 %collective-permute-start.18 = (bf16[96,4096]{1,0:T(8,128)(2,1)S(1)}, bf16[96,4096]{1,0:T(8,128)(2,1)S(1)}, u32[]{:S(2)}, u32[]{:S(2)}) collective-permute-start(bf16[96,4096]{1,0:T(8,128)(2,1)S(1)} %get-tuple-element.95.refs_3_), channel_id=1, source_target_pairs={{0,8},{10,2},{4,12},{14,6},{8,16},{18,10},{12,20},{22,14},{16,24},... | collective-permute-start | bytes 2359304 | tf_op jit(solution)/shard_map/ppermute | solution.py:372
  144.0 21.9 %collective-permute-start.19 = (bf16[96,4096]{1,0:T(8,128)(2,1)S(1)}, bf16[96,4096]{1,0:T(8,128)(2,1)S(1)}, u32[]{:S(2)}, u32[]{:S(2)}) collective-permute-start(bf16[96,4096]{1,0:T(8,128)(2,1)S(1)} %get-tuple-element.97.refs_5_.refs_0_), channel_id=1, source_target_pairs={{8,0},{2,10},{12,4},{6,14},{16,8},{10,18},{20,12},{14,22},{24,16},... | collective-permute-start | bytes 2359304 | tf_op jit(solution)/shard_map/ppermute | solution.py:372
  160.6 20.1 %collective-permute-start.20 = (bf16[96,4096]{1,0:T(8,128)(2,1)S(1)}, bf16[96,4096]{1,0:T(8,128)(2,1)}, u32[]{:S(2)}, u32[]{:S(2)}) collective-permute-start(bf16[96,4096]{1,0:T(8,128)(2,1)S(1)} %get-tuple-element.99.refs_1_), channel_id=1, source_target_pairs={{0,8},{10,2},{4,12},{14,6},{8,16},{18,10},{12,20},{22,14},{16,24},... | collective-permute-start | bytes 2359304 | tf_op jit(solution)/shard_map/ppermute | solution.py:372
  166.2 20.5 %collective-permute-start.21 = (bf16[96,4096]{1,0:T(8,128)(2,1)S(1)}, bf16[96,4096]{1,0:T(8,128)(2,1)}, u32[]{:S(2)}, u32[]{:S(2)}) collective-permute-start(bf16[96,4096]{1,0:T(8,128)(2,1)S(1)} %get-tuple-element.101.refs_4_.refs_2_), channel_id=1, source_target_pairs={{8,0},{2,10},{12,4},{6,14},{16,8},{10,18},{20,12},{14,22},{24,16},... | collective-permute-start | bytes 2359304 | tf_op jit(solution)/shard_map/ppermute | solution.py:372
  173.2 16.3 %copy-start.2 = (f32[256,2]{0,1:T(2,128)S(1)}, f32[256,2]{0,1:T(2,128)}, u32[]{:S(2)}) copy-start(f32[256,2]{0,1:T(2,128)} %param.8) | copy-start | bytes 6148
  182.1 19.3 %collective-permute-start.24 = (bf16[96,4096]{1,0:T(8,128)(2,1)S(1)}, bf16[96,4096]{1,0:T(8,128)(2,1)S(1)}, u32[]{:S(2)}, u32[]{:S(2)}) collective-permute-start(bf16[96,4096]{1,0:T(8,128)(2,1)S(1)} %get-tuple-element.105.refs_3_), channel_id=1, source_target_pairs={{0,8},{10,2},{4,12},{14,6},{8,16},{18,10},{12,20},{22,14},{16,24},... | collective-permute-start | bytes 2359304 | tf_op jit(solution)/shard_map/ppermute | solution.py:372
  188.1 18.1 %collective-permute-start.25 = (bf16[96,4096]{1,0:T(8,128)(2,1)S(1)}, bf16[96,4096]{1,0:T(8,128)(2,1)S(1)}, u32[]{:S(2)}, u32[]{:S(2)}) collective-permute-start(bf16[96,4096]{1,0:T(8,128)(2,1)S(1)} %get-tuple-element.107.refs_5_.refs_0_), channel_id=1, source_target_pairs={{8,0},{2,10},{12,4},{6,14},{16,8},{10,18},{20,12},{14,22},{24,16},... | collective-permute-start | bytes 2359304 | tf_op jit(solution)/shard_map/ppermute | solution.py:372
  201.8 8.3 %collective-permute-start.26 = (bf16[32,4096]{1,0:T(8,128)(2,1)S(1)}, bf16[32,4096]{1,0:T(8,128)(2,1)S(1)}, u32[]{:S(2)}, u32[]{:S(2)}) collective-permute-start(bf16[32,4096]{1,0:T(8,128)(2,1)S(1)} %get-tuple-element.109.refs_1_), channel_id=1, source_target_pairs={{0,8},{10,2},{4,12},{14,6},{8,16},{18,10},{12,20},{22,14},{16,24},... | collective-permute-start | bytes 786440 | tf_op jit(solution)/shard_map/ppermute | solution.py:372
  206.6 8.6 %collective-permute-start.27 = (bf16[32,4096]{1,0:T(8,128)(2,1)S(1)}, bf16[32,4096]{1,0:T(8,128)(2,1)S(1)}, u32[]{:S(2)}, u32[]{:S(2)}) collective-permute-start(bf16[32,4096]{1,0:T(8,128)(2,1)S(1)} %get-tuple-element.111.refs_2_), channel_id=1, source_target_pairs={{8,0},{2,10},{12,4},{6,14},{16,8},{10,18},{20,12},{14,22},{24,16},... | collective-permute-start | bytes 786440 | tf_op jit(solution)/shard_map/ppermute | solution.py:372
  207.9 59.1 %collective-permute-start.17 = (bf16[64,768]{1,0:T(8,128)(2,1)S(1)}, bf16[64,768]{1,0:T(8,128)(2,1)S(1)}, u32[]{:S(2)}, u32[]{:S(2)}) collective-permute-start(bf16[64,768]{1,0:T(8,128)(2,1)S(1)} %pad_maximum_fusion.3), channel_id=1, source_target_pairs={{0,1},{1,0},{2,3},{3,2},{4,5},{5,4},{6,7},{7,6},{8,9},{9,8},{10,11... | collective-permute-start | bytes 294920 | tf_op jit(solution)/shard_map/ppermute | solution.py:417
  210.1 11.6 %collective-permute-start.30 = (bf16[32,4096]{1,0:T(8,128)(2,1)S(1)}, bf16[32,4096]{1,0:T(8,128)(2,1)S(1)}, u32[]{:S(2)}, u32[]{:S(2)}) collective-permute-start(bf16[32,4096]{1,0:T(8,128)(2,1)S(1)} %combine.51.refs_3_), channel_id=1, source_target_pairs={{0,8},{10,2},{4,12},{14,6},{8,16},{18,10},{12,20},{22,14},{16,24},... | collective-permute-start | bytes 786440 | tf_op jit(solution)/shard_map/ppermute | solution.py:372
  218.5 15.3 %collective-permute-start.31 = (bf16[32,4096]{1,0:T(8,128)(2,1)S(1)}, bf16[32,4096]{1,0:T(8,128)(2,1)S(1)}, u32[]{:S(2)}, u32[]{:S(2)}) collective-permute-start(bf16[32,4096]{1,0:T(8,128)(2,1)S(1)} %combine.52.refs_5_.refs_0_), channel_id=1, source_target_pairs={{8,0},{2,10},{12,4},{6,14},{16,8},{10,18},{20,12},{14,22},{24,16},... | collective-permute-start | bytes 786440 | tf_op jit(solution)/shard_map/ppermute | solution.py:372
  219.9 6.8 %collective-permute-start.22 = (bf16[128,768]{1,0:T(8,128)(2,1)S(1)}, bf16[128,768]{1,0:T(8,128)(2,1)S(1)}, u32[]{:S(2)}, u32[]{:S(2)}) collective-permute-start(bf16[128,768]{1,0:T(8,128)(2,1)S(1)} %pad_maximum_fusion), channel_id=1, source_target_pairs={{0,1},{1,0},{2,3},{3,2},{4,5},{5,4},{6,7},{7,6},{8,9},{9,8},{10,11... | collective-permute-start | bytes 589832 | tf_op jit(solution)/shard_map/ppermute | solution.py:417
  221.8 16.6 %collective-permute-start.32 = (bf16[32,4096]{1,0:T(8,128)(2,1)S(1)}, bf16[32,4096]{1,0:T(8,128)(2,1)S(1)}, u32[]{:S(2)}, u32[]{:S(2)}) collective-permute-start(bf16[32,4096]{1,0:T(8,128)(2,1)S(1)} %combine.53.refs_1_), channel_id=1, source_target_pairs={{0,8},{10,2},{4,12},{14,6},{8,16},{18,10},{12,20},{22,14},{16,24},... | collective-permute-start | bytes 786440 | tf_op jit(solution)/shard_map/ppermute | solution.py:372
  226.4 5.7 %collective-permute-start.28 = (bf16[128,768]{1,0:T(8,128)(2,1)S(1)}, bf16[128,768]{1,0:T(8,128)(2,1)S(1)}, u32[]{:S(2)}, u32[]{:S(2)}) collective-permute-start(bf16[128,768]{1,0:T(8,128)(2,1)S(1)} %pad_maximum_fusion.1), channel_id=1, source_target_pairs={{0,1},{1,0},{2,3},{3,2},{4,5},{5,4},{6,7},{7,6},{8,9},{9,8},{10,11... | collective-permute-start | bytes 589832 | tf_op jit(solution)/shard_map/ppermute | solution.py:417
  226.8 16.6 %collective-permute-start.23 = (bf16[128,768]{1,0:T(8,128)(2,1)S(1)}, bf16[128,768]{1,0:T(8,128)(2,1)S(1)}, u32[]{:S(2)}, u32[]{:S(2)}) collective-permute-start(bf16[128,768]{1,0:T(8,128)(2,1)S(1)} %add_convert_fusion.2), channel_id=1, source_target_pairs={{0,2},{2,0},{4,6},{6,4},{1,3},{3,1},{5,7},{7,5},{8,10},{10,8},{12,... | collective-permute-start | bytes 589832 | tf_op jit(solution)/shard_map/ppermute | solution.py:422
  232.2 11.9 %collective-permute-start.29 = (bf16[128,768]{1,0:T(8,128)(2,1)S(1)}, bf16[128,768]{1,0:T(8,128)(2,1)S(1)}, u32[]{:S(2)}, u32[]{:S(2)}) collective-permute-start(bf16[128,768]{1,0:T(8,128)(2,1)S(1)} %add_convert_fusion.1), channel_id=1, source_target_pairs={{0,4},{2,6},{4,0},{6,2},{1,5},{3,7},{5,1},{7,3},{8,12},{10,14},{12... | collective-permute-start | bytes 589832 | tf_op jit(solution)/shard_map/ppermute | solution.py:422
  237.2 8.6 %collective-permute-start.33 = (bf16[32,4096]{1,0:T(8,128)(2,1)S(1)}, bf16[32,4096]{1,0:T(8,128)(2,1)S(1)}, u32[]{:S(2)}, u32[]{:S(2)}) collective-permute-start(bf16[32,4096]{1,0:T(8,128)(2,1)S(1)} %combine.54.refs_3_.refs_0_), channel_id=1, source_target_pairs={{8,0},{2,10},{12,4},{6,14},{16,8},{10,18},{20,12},{14,22},{24,16},... | collective-permute-start | bytes 786440 | tf_op jit(solution)/shard_map/ppermute | solution.py:372
  238.5 10.6 %collective-permute-start.36 = (bf16[32,4096]{1,0:T(8,128)(2,1)S(1)}, bf16[32,4096]{1,0:T(8,128)(2,1)S(1)}, u32[]{:S(2)}, u32[]{:S(2)}) collective-permute-start(bf16[32,4096]{1,0:T(8,128)(2,1)S(1)} %combine.55.refs_1_), channel_id=1, source_target_pairs={{0,8},{10,2},{4,12},{14,6},{8,16},{18,10},{12,20},{22,14},{16,24},... | collective-permute-start | bytes 786440 | tf_op jit(solution)/shard_map/ppermute | solution.py:372
  252.6 4.7 %collective-permute-start.37 = (bf16[64,768]{1,0:T(8,128)(2,1)S(1)}, bf16[64,768]{1,0:T(8,128)(2,1)S(1)}, u32[]{:S(2)}, u32[]{:S(2)}) collective-permute-start(bf16[64,768]{1,0:T(8,128)(2,1)S(1)} %pad_maximum_fusion.4), channel_id=1, source_target_pairs={{0,1},{1,0},{2,3},{3,2},{4,5},{5,4},{6,7},{7,6},{8,9},{9,8},{10,11... | collective-permute-start | bytes 294920 | tf_op jit(solution)/shard_map/ppermute | solution.py:417
  254.1 5.7 %collective-permute-start.34 = (bf16[128,768]{1,0:T(8,128)(2,1)S(1)}, bf16[128,768]{1,0:T(8,128)(2,1)S(1)}, u32[]{:S(2)}, u32[]{:S(2)}) collective-permute-start(bf16[128,768]{1,0:T(8,128)(2,1)S(1)} %pad_maximum_fusion.2), channel_id=1, source_target_pairs={{0,1},{1,0},{2,3},{3,2},{4,5},{5,4},{6,7},{7,6},{8,9},{9,8},{10,11... | collective-permute-start | bytes 589832 | tf_op jit(solution)/shard_map/ppermute | solution.py:417
  259.9 6.3 %collective-permute-start.35 = (bf16[128,768]{1,0:T(8,128)(2,1)S(1)}, bf16[128,768]{1,0:T(8,128)(2,1)S(1)}, u32[]{:S(2)}, u32[]{:S(2)}) collective-permute-start(bf16[128,768]{1,0:T(8,128)(2,1)S(1)} %add_convert_fusion), channel_id=1, source_target_pairs={{0,6},{2,4},{4,2},{6,0},{1,7},{3,5},{5,3},{7,1},{8,14},{10,12},{12... | collective-permute-start | bytes 589832 | tf_op jit(solution)/shard_map/ppermute | solution.py:422

commit v3 on v2

--- a/solution.py
+++ b/solution.py
@@ -1,5 +1,6 @@
 import jax
 import jax.numpy as jnp
+import numpy as np
 from jax import lax
 from jax.experimental import pallas as pl
 from jax.experimental.pallas import tpu as pltpu
@@ -73,16 +74,16 @@
     return run
 
 
-def begin(m, experts, capacity, e, ids, tokens, wg, wu):
+def begin(m, experts, capacity, e, spot, ids, tokens, wg, wu):
     n, width = tokens.shape
     units = wg.shape[1]
     half = capacity // 2
     cuts = tiles_of(units, 512)
     names = (experts + 15) // 16 * 16
 
-    def body(e_ref, ids_hbm, tok_hbm, wg_hbm, wu_hbm, place_ref, *rest):
+    def body(e_ref, spot0_ref, spot1_ref, ids_hbm, tok_hbm, wg_hbm, wu_hbm, place_ref, *rest):
         rows = rest[:experts]
-        g_ref, u_ref, x_ref, ids_ref, tok_ref, buffers, sems, small = rest[experts:]
+        mark_ref, g_ref, u_ref, x_ref, ids_ref, tok_ref, buffers, sems, small = rest[experts:]
         ids_copy = pltpu.make_async_copy(ids_hbm, ids_ref, small.at[0])
         tok_copy = pltpu.make_async_copy(tok_hbm, tok_ref, small.at[1])
         ids_copy.start()
@@ -97,7 +98,9 @@
         run = streamed(pieces, buffers, sems, use)
         ids_copy.wait()
         index = lax.broadcasted_iota(I32, (names, n), 0)
-        ids = [ids_ref[k : k + 1, :] for k in range(2)]
+        ids = [ids_ref[k : k + 1, :] ^ e_ref[0] for k in range(2)]
+        mark_ref[:8] = jnp.full((8, 128), spot0_ref[0], I32)
+        mark_ref[8:] = jnp.full((8, 128), spot1_ref[0], I32)
         hits = [index == ids[k] for k in range(2)]
         earlier = lax.broadcasted_iota(I32, (n, n), 0) < lax.broadcasted_iota(I32, (n, n), 1)
         before = jnp.dot(one_hot(hits[0] | hits[1]), one_hot(earlier), preferred_element_type=F32)
@@ -109,7 +112,7 @@
         lines = lax.broadcasted_iota(I32, (capacity, n), 0) * experts
         tok_copy.wait()
         for j in range(experts):
-            mine = lines + (e_ref[0] ^ j)
+            mine = lines + j
             chosen = one_hot((mine == places[0]) | (mine == places[1]))
             picked = jnp.dot(chosen, tok_ref[...], preferred_element_type=F32).astype(BF16)
             rows[j][...] = picked
@@ -120,14 +123,14 @@
             run(i)
 
     shapes = [array(2, n, dtype=I32)] + [array(capacity, width)] * experts
-    shapes += [array(2 * m, units)] * 2
+    shapes += [array(16, 128, dtype=I32)] + [array(2 * m, units)] * 2
     slots = 2 * len(cuts)
     out = call(
         body,
         "begin",
         shapes,
-        (e, ids, tokens, wg, wu),
-        [SCALAR, FAR, FAR, FAR, FAR],
+        (e, *spot, ids, tokens, wg, wu),
+        [SCALAR] * 3 + [FAR] * 4,
         [
             pltpu.VMEM((2 * m, width), BF16),
             pltpu.VMEM((2, n), I32),
@@ -138,10 +141,10 @@
         ],
         grant=48,
     )
-    return out[0], out[1 : 1 + experts], out[1 + experts :]
-
-
-def project(m, spot, rows, plans, weights, tie):
+    return out[0], out[1 : 1 + experts], out[1 + experts], out[2 + experts :]
+
+
+def project(m, spot, rows, plans, weights, ties):
     used = sorted({c[0] for plan in plans for per_flow in plan for c in per_flow if c})
     width, units = weights[0].shape
     total = 2 * m * len(plans)
@@ -170,14 +173,14 @@
         for i in range(len(pieces)):
             run(i)
 
-    args = (*spot, *(rows[j] for j in used), *weights, tie)
+    args = (*spot, *(rows[j] for j in used), *weights, *ties)
     slots = min(8, 2 * len(cuts))
     return call(
         body,
         "project",
         [array(total, units)] * 2,
         args,
-        [SCALAR] * 2 + [WHOLE] * len(used) + [FAR] * 2 + [WHOLE],
+        [SCALAR] * 2 + [WHOLE] * len(used) + [FAR] * 2 + [WHOLE] * len(ties),
         [
             pltpu.VMEM((total, width), BF16),
             pltpu.VMEM((slots, width, units // len(cuts)), BF16),
@@ -187,7 +190,7 @@
     )
 
 
-def combine(m, units, f, first, came, partial, act, summing, sending, fresh, spot, ties, relay):
+def combine(m, units, f, first, came, partial, act, summing, sending, fresh, spot, ties, relay=()):
     args, use = [], {}
 
     def take(key, value):
@@ -202,7 +205,8 @@
         take("u", partial[1])
         base = partial[2] + f * m
     take("act", act)
-    take("relay", relay)
+    for k, value in enumerate(relay):
+        take(k, value)
     taken = len(args)
     args += ties
     sums = 2 * m if summing and sending else 0
@@ -211,14 +215,14 @@
     shapes = [array(rows, units)] if rows else []
     if fresh:
         shapes.append(array(m, units))
-    if relay is not None:
-        shapes.append(array(*relay.shape))
+    for value in relay:
+        shapes.append(array(*value.shape))
 
     def body(*refs):
         ins, outs = refs[:taken], refs[len(args) :]
         ref = {key: ins[at] for key, at in use.items()}
-        if relay is not None:
-            outs[-1][...] = ref["relay"][...]
+        for k in range(len(relay)):
+            outs[len(shapes) - len(relay) + k][...] = ref[k][...]
 
         def step(cols):
             if summing:
@@ -251,7 +255,7 @@
         lax.fori_loop(0, units // wide, loop, 0)
 
     out = list(call(body, "combine", shapes, args))
-    relayed = out.pop() if relay is not None else None
+    relayed = [out.pop() for _ in relay][::-1]
     activated = out.pop() if fresh else None
     return (out[0] if rows else None), activated, relayed
 
@@ -320,11 +324,11 @@
     flows = [[(a, c) if a % experts % 2 == f else (c, a) for a, c in climb] for f in range(2)]
 
     weights = (w_gate[0], w_up[0])
-    places, picked, opening = begin(
-        m, experts, capacity, e.astype(I32).reshape(1), route_ids.T, tokens, *weights
+    wd = w_down[0]
+    places, picked, marks, opening = begin(
+        m, experts, capacity, e.astype(I32).reshape(1), spot, route_ids.T, tokens, *weights
     )
-    rows = [picked[0]] + [None] * (experts - 1)
-    due = {max(0, order.index((j, 0)) - 2): j for j in range(1, experts)}
+    rows = [picked[0]]
 
     def sources(s):
         found = [[None] * depth for _ in range(2)]
@@ -335,18 +339,61 @@
                     found[f][a] = (j, f * half + i * m)
         return found
 
-    wd = w_down[0]
+    def across(part):
+        if tensors == 2:
+            other = lax.ppermute(part, "tensor", [(0, 1), (1, 0)])
+            return (part.astype(F32) + other.astype(F32)).astype(BF16)
+        return lax.psum(part, "tensor")
+
     sums_end = chunks + last
     ticks = chunks + 2 * last + 1
+    ends = chunks + last
     partial = {0: (*opening, 0)}
     got = [None, None]
     act = [None, None]
     held = [{}, {}]
     outs = {}
     ties = []
+    spans = []
+    for index, (j, i) in enumerate(order):
+        if spans and spans[-1][0] == j:
+            spans[-1][2] = index + 1
+        else:
+            spans.append([j, index, index + 1, i])
+    def rounds_of(start, stop):
+        return range(start, stop + last)
+
+    def own_copy(start, stop):
+        return lax.optimization_barrier([outs[q] for q in rounds_of(start, stop)])
+
+    def finished(start, stop):
+        outs = dict(zip(rounds_of(start, stop), own_copy(start, stop)))
+        return [
+            jnp.concatenate(
+                [
+                    pick(
+                        [outs[c + a][f * m : (f + 1) * m] for a in range(depth)],
+                        marks[8 * (1 - f) : 8 * (1 - f) + 1, :1],
+                    )
+                    for c in range(start, stop)
+                ]
+            )
+            for f in range(2)
+        ]
+
+    parts = []
+
+    def deliver():
+        for j, start, stop, i in spans[len(parts) :]:
+            if all(q in outs for q in rounds_of(start, stop)):
+                part = lax.optimization_barrier(jnp.concatenate(finished(start, stop)))
+                if j:
+                    part = lax.ppermute(part, "expert", [(a, a ^ j) for a in range(experts)])
+                parts.append(part)
+
     for s in range(ticks):
         summing = s < sums_end
-        for f in (0, 1):
+        for f in range(2):
             o = 1 - f
             first = last + 1 if f == 0 else last
             carries = first <= s < first + chunks + last
@@ -365,64 +412,38 @@
                 summing and s >= last,
                 spot[f],
                 ties,
-                picked[due[s]] if f == 1 and s in due else None,
+                picked[1:] if s == 0 and f == 1 else (),
             )
             ties = []
             if s < sums_end - 1 or (carries and s < first + chunks + last - 1):
                 got[f] = lax.ppermute(message, ("dp", "expert"), flows[f])
-            if relayed is not None:
-                j = due[s]
-                rows[j] = lax.ppermute(relayed, "expert", [(a, a ^ j) for a in range(experts)])
+            for j, value in enumerate(relayed, 1):
+                rows.append(lax.ppermute(value, "expert", [(a, a ^ j) for a in range(experts)]))
             if carries:
                 held[o][s - first] = message
-            if f == 1 and s + 1 < sums_end and s + 1 not in partial:
+            if f == (0 if s else 1) and s + 1 < sums_end and s + 1 not in partial:
                 rounds = [r for r in (s + 1, s + 2) if r < sums_end]
-                g, u = project(m, spot, rows, [sources(r) for r in rounds], weights, message)
+                wait = [message] if s else [message, *rows[1:]]
+                g, u = project(m, spot, rows, [sources(r) for r in rounds], weights, wait)
                 for k, r in enumerate(rounds):
                     partial[r] = (g, u, 2 * m * k)
-                ties = [g]
-            if f == 1 or s == ticks - 1:
-                ready = [q for q in range(chunks + last) if q in held[0] and q in held[1]]
-                ready = [q for q in ready if q not in outs]
-                if len(ready) == 2 or (ready and ready[0] >= chunks):
-                    tie = () if s == ticks - 1 else (message,)
-                    pairs = [(held[0][q], held[1][q]) for q in ready]
-                    result = lower(m, pairs, wd, tie)
-                    for k, q in enumerate(ready):
-                        outs[q] = result[2 * m * k : 2 * m * (k + 1)]
-                    ties = ties + [result]
-
-    def finished(start, stop):
-        return [
-            jnp.concatenate(
-                [
-                    pick([outs[c + a][f * m : (f + 1) * m] for a in range(depth)], spot[1 - f][0])
-                    for c in range(start, stop)
-                ]
-            )
-            for f in range(2)
-        ]
+                ties.append(g)
+            ready = [q for q in range(ends) if q in held[0] and q in held[1] and q not in outs]
+            if len(ready) == 2 or (ready and ready[0] == ends - 1):
+                pairs = [(held[0][q], held[1][q]) for q in ready]
+                if ready[0] == ends - 1:
+                    deliver()
+                result = lower(m, pairs, wd, [message] + (parts if ready[0] == ends - 1 else []))
+                ties.append(result)
+                result = across(result)
+                for k, q in enumerate(ready):
+                    outs[q] = result[2 * m * k : 2 * m * (k + 1)]
 
     yields = [jnp.zeros((n, width), F32), jnp.zeros((n, width), F32)]
-    spans = []
-    for index, (j, i) in enumerate(order):
-        if spans and spans[-1][0] == j:
-            spans[-1][2] = index + 1
-        else:
-            spans.append([j, index, index + 1, i])
-    for j, start, stop, i in spans:
-        size = (stop - start) * m
-        part = jnp.concatenate(finished(start, stop))
-        if tensors == 2:
-            other = lax.ppermute(part, "tensor", [(0, 1), (1, 0)])
-            part = (part.astype(F32) + other.astype(F32)).astype(BF16)
-        else:
-            part = lax.psum(part, "tensor")
-        if j:
-            part = lax.ppermute(part, "expert", [(a, a ^ j) for a in range(experts)])
-        ranks = jnp.arange(size, dtype=I32) + i * m
-        ranks = jnp.concatenate([ranks, ranks + half])
-        label = ranks * experts + (e ^ j)
+    deliver()
+    for (j, start, stop, i), part in zip(spans, parts):
+        ranks = np.arange((stop - start) * m, dtype=np.int32) + i * m
+        label = jnp.asarray(np.concatenate([ranks, ranks + half]) * experts + j)
         for k in range(2):
             chosen = (label[:, None] == places[k][None, :]).astype(BF16)
             yields[k] += lax.dot_general(

time: 270 us -> 261 us (0.967)
  waiting for transfers between devices: 101 us -> 95.2 us
  Pallas kernels: 65.4 us -> 59.8 us
  between operations: 0.92 us -> 4.79 us
    pallas_call x42 -> x41, Pallas kernels: 65.4 us -> 59.8 us  [call(): pl.pallas_call(body, name=name, out_shape=shapes, in_specs=specs, out_spe...]
    ppermute x11 -> x12, waiting for transfers between devices: 26.5 us -> 22.7 us  [the longest x6 11.5 us: across(): other = lax.ppermute(part, 'tensor', [(0, 1), (1, 0)])]
    ppermute x11 -> x12, starting transfers between devices: 12.5 us -> 10.3 us  [the longest x6 6.66 us: across(): other = lax.ppermute(part, 'tensor', [(0, 1), (1, 0)])]
  transfers between devices with their start and end apart: 38 -> 39, of which waited for: 18 -> 24; matrix products, arithmetic and copies ran while one was open for 1% -> 1% of each run, Pallas kernels for 22% -> 18%
where the time goes in v3:
time: 261 us; the launch traced here: 260 us
  waiting for transfers between devices  95.2 us (36%)
  starting transfers between devices  92.5 us (35%)
  Pallas kernels  59.8 us (23%)
  between operations  4.79 us (2%)
  matrix products  4.5 us (2%)
    ppermute x27, starting transfers between devices, local(): got[f] = lax.ppermute(message, ('dp', 'expert'), flows[f])  82.2 us
    ppermute x27, waiting for transfers between devices, local(): got[f] = lax.ppermute(message, ('dp', 'expert'), flows[f])  72.5 us
    pallas_call x41, Pallas kernels, call(): pl.pallas_call(body, name=name, out_shape=shapes, in_specs=specs, out_spe...  59.8 us
    ppermute x6, waiting for transfers between devices, across(): other = lax.ppermute(part, 'tensor', [(0, 1), (1, 0)])  11.5 us
    ppermute x3, waiting for transfers between devices, local(): lax.ppermute(value, 'expert', [(a, a ^ j) for a in range(experts)])  9.04 us
    ppermute x6, starting transfers between devices, across(): other = lax.ppermute(part, 'tensor', [(0, 1), (1, 0)])  6.66 us
  transfers between devices with their start and end apart: 39, of which 24 were waited for; matrix products, arithmetic and copies ran while one was open for 1% of the time, Pallas kernels for 18%

profile of v3, /device:TPU:0, one launch (start us, length us, event | category | flops | bytes accessed | tf_op | source)
XLA Modules:
  0.0 259.7 jit_solution(16867514754752910953)
XLA Ops:
  1.7 5.7 %begin.1 = (s32[2,256]{1,0:T(2,128)S(1)}, bf16[128,768]{1,0:T(8,128)(2,1)S(1)}, bf16[128,768]{1,0:T(8,128)(2,1)S(1)}, bf16[128,768]{1,0:T(8,128)(2,1)S(1)}, bf16...) custom-call(s32[1]{0:T(128)} %bitcast.1.e_ref, ...), custom_call_target="tpu_custom_call" | custom-call | tf_op jit(solution)/shard_map/begin/pallas_call | solution.py:38
  7.4 5.0 %collective-permute-start.5 = (bf16[64,4096]{1,0:T(8,128)(2,1)S(1)}, bf16[64,4096]{1,0:T(8,128)(2,1)S(1)}, u32[]{:S(2)}, u32[]{:S(2)}) collective-permute-start(bf16[64,4096]{1,0:T(8,128)(2,1)S(1)} %combine.31), channel_id=1, source_target_pairs={{0,8},{10,2},{4,12},{14,6},{8,16},{18,10},{12,20},{22,14},{16,24},... | collective-permute-start | bytes 1572872 | tf_op jit(solution)/shard_map/ppermute | solution.py:419
  12.5 1.3 collective-permute-start
  14.1 1.7 collective-permute-start.2
  15.8 6.0 %collective-permute-done.2.refs_6_.refs_2_.refs_1_ = bf16[128,768]{1,0:T(8,128)(2,1)S(1)} collective-permute-done((bf16[128,768]{1,0:T(8,128)(2,1)S(1)}, bf16[128,768]{1,0:T(8,128)(2,1)S(1)}, u32[]{:S(2)}, u32[]{:S(2)}) %collective-permute-start.2) | collective-permute-done | bytes 196640 | tf_op jit(solution)/shard_map/ppermute | solution.py:421
  21.8 3.0 %collective-permute-done.3.refs_7_.refs_2_.refs_1_ = bf16[128,768]{1,0:T(8,128)(2,1)S(1)} collective-permute-done((bf16[128,768]{1,0:T(8,128)(2,1)S(1)}, bf16[128,768]{1,0:T(8,128)(2,1)S(1)}, u32[]{:S(2)}, u32[]{:S(2)}) %collective-permute-start.3) | collective-permute-done | bytes 196640 | tf_op jit(solution)/shard_map/ppermute | solution.py:421
  24.8 5.6 %project.5 = (bf16[128,4096]{1,0:T(8,128)(2,1)S(1)}, bf16[128,4096]{1,0:T(8,128)(2,1)S(1)}) custom-call(s32[1]{0:T(128)} %bitcast.2.spot0_ref.refs_0_, s32[1]{0:T(128)} %bitcast.3.spot1_ref.refs_0_, bf16[128,768]{1,0:T(8,128)(2,1)S(1)} %get-tuple-element.90.refs_0_, bf16[128,768]{1,0:T(8,128)(2,1)S(1)} %collective-permute-done.1.refs_1_.refs_5_.refs_0_, ...), custom_call_target="tpu_custom_call" | custom-call | tf_op jit(solution)/shard_map/project/pallas_call | solution.py:38
  30.6 4.7 %collective-permute-start.6 = (bf16[64,4096]{1,0:T(8,128)(2,1)S(1)}, bf16[64,4096]{1,0:T(8,128)(2,1)S(1)}, u32[]{:S(2)}, u32[]{:S(2)}) collective-permute-start(bf16[64,4096]{1,0:T(8,128)(2,1)S(1)} %combine.32), channel_id=1, source_target_pairs={{0,8},{10,2},{4,12},{14,6},{8,16},{18,10},{12,20},{22,14},{16,24},... | collective-permute-start | bytes 1572872 | tf_op jit(solution)/shard_map/ppermute | solution.py:419
  35.5 1.3 collective-permute-start.4
  36.8 9.3 %collective-permute-done.6.refs_0_ = bf16[64,4096]{1,0:T(8,128)(2,1)S(1)} collective-permute-done((bf16[64,4096]{1,0:T(8,128)(2,1)S(1)}, bf16[64,4096]{1,0:T(8,128)(2,1)S(1)}, u32[]{:S(2)}, u32[]{:S(2)}) %collective-permute-start.6) | collective-permute-done | bytes 524320 | tf_op jit(solution)/shard_map/ppermute | solution.py:419
  46.3 4.4 %collective-permute-start.8 = (bf16[64,4096]{1,0:T(8,128)(2,1)S(1)}, bf16[64,4096]{1,0:T(8,128)(2,1)S(1)}, u32[]{:S(2)}, u32[]{:S(2)}) collective-permute-start(bf16[64,4096]{1,0:T(8,128)(2,1)S(1)} %combine.33.refs_5_), channel_id=1, source_target_pairs={{0,8},{10,2},{4,12},{14,6},{8,16},{18,10},{12,20},{22,14},{16,24},... | collective-permute-start | bytes 1572872 | tf_op jit(solution)/shard_map/ppermute | solution.py:419
  50.7 5.6 %project.6 = (bf16[128,4096]{1,0:T(8,128)(2,1)S(1)}, bf16[128,4096]{1,0:T(8,128)(2,1)S(1)}) custom-call(s32[1]{0:T(128)} %bitcast.2.spot0_ref.refs_0_, s32[1]{0:T(128)} %bitcast.3.spot1_ref.refs_0_, bf16[128,768]{1,0:T(8,128)(2,1)S(1)} %get-tuple-element.90.refs_0_, bf16[128,768]{1,0:T(8,128)(2,1)S(1)} %collective-permute-done.1.refs_1_.refs_5_.refs_0_, ...), custom_call_target="tpu_custom_call" | custom-call | tf_op jit(solution)/shard_map/project/pallas_call | solution.py:38
  56.5 1.3 collective-permute-start.7
  57.8 1.9 collective-permute-done.8.refs_0_
  60.0 4.4 %collective-permute-start.9 = (bf16[64,4096]{1,0:T(8,128)(2,1)S(1)}, bf16[64,4096]{1,0:T(8,128)(2,1)S(1)}, u32[]{:S(2)}, u32[]{:S(2)}) collective-permute-start(bf16[64,4096]{1,0:T(8,128)(2,1)S(1)} %get-tuple-element.100), channel_id=1, source_target_pairs={{0,8},{10,2},{4,12},{14,6},{8,16},{18,10},{12,20},{22,14},{16,24},... | collective-permute-start | bytes 1572872 | tf_op jit(solution)/shard_map/ppermute | solution.py:419
  64.4 6.3 %collective-permute-done.7.refs_1_ = bf16[64,4096]{1,0:T(8,128)(2,1)S(1)} collective-permute-done((bf16[64,4096]{1,0:T(8,128)(2,1)S(1)}, bf16[64,4096]{1,0:T(8,128)(2,1)S(1)}, u32[]{:S(2)}, u32[]{:S(2)}) %collective-permute-start.7) | collective-permute-done | bytes 524320 | tf_op jit(solution)/shard_map/ppermute | solution.py:419
  71.0 1.3 collective-permute-start.10
  72.3 1.8 collective-permute-done.9.refs_1_
  74.5 4.4 %collective-permute-start.11 = (bf16[96,4096]{1,0:T(8,128)(2,1)S(1)}, bf16[96,4096]{1,0:T(8,128)(2,1)S(1)}, u32[]{:S(2)}, u32[]{:S(2)}) collective-permute-start(bf16[96,4096]{1,0:T(8,128)(2,1)S(1)} %get-tuple-element.102.refs_5_.refs_1_), channel_id=1, source_target_pairs={{0,8},{10,2},{4,12},{14,6},{8,16},{18,10},{12,20},{22,14},{16,24},... | collective-permute-start | bytes 2359304 | tf_op jit(solution)/shard_map/ppermute | solution.py:419
  78.9 5.6 %project.7 = (bf16[128,4096]{1,0:T(8,128)(2,1)S(1)}, bf16[128,4096]{1,0:T(8,128)(2,1)S(1)}) custom-call(s32[1]{0:T(128)} %bitcast.2.spot0_ref.refs_0_, s32[1]{0:T(128)} %bitcast.3.spot1_ref.refs_0_, bf16[128,768]{1,0:T(8,128)(2,1)S(1)} %collective-permute-done.1.refs_1_.refs_5_.refs_0_, bf16[128,768]{1,0:T(8,128)(2,1)S(1)} %collective-permute-done.2.refs_6_.refs_2_.refs_1_, ...), custom_call_target="tpu_custom_call" | custom-call | tf_op jit(solution)/shard_map/project/pallas_call | solution.py:38
  84.5 5.7 %collective-permute-done.10.refs_1_ = bf16[96,4096]{1,0:T(8,128)(2,1)S(1)} collective-permute-done((bf16[96,4096]{1,0:T(8,128)(2,1)S(1)}, bf16[96,4096]{1,0:T(8,128)(2,1)S(1)}, u32[]{:S(2)}, u32[]{:S(2)}) %collective-permute-start.10) | collective-permute-done | bytes 786464 | tf_op jit(solution)/shard_map/ppermute | solution.py:419
  90.6 1.3 collective-permute-start.13
  92.5 4.4 %collective-permute-start.14 = (bf16[96,4096]{1,0:T(8,128)(2,1)S(1)}, bf16[96,4096]{1,0:T(8,128)(2,1)S(1)}, u32[]{:S(2)}, u32[]{:S(2)}) collective-permute-start(bf16[96,4096]{1,0:T(8,128)(2,1)S(1)} %get-tuple-element.108.refs_3_.refs_5_), channel_id=1, source_target_pairs={{0,8},{10,2},{4,12},{14,6},{8,16},{18,10},{12,20},{22,14},{16,24},... | collective-permute-start | bytes 2359304 | tf_op jit(solution)/shard_map/ppermute | solution.py:419
  97.0 3.3 %lower.6.refs_5_ = bf16[128,768]{1,0:T(8,128)(2,1)S(1)} custom-call(bf16[96,4096]{1,0:T(8,128)(2,1)S(1)} %get-tuple-element.99.refs_0_, bf16[96,4096]{1,0:T(8,128)(2,1)S(1)} %get-tuple-element.102.refs_5_.refs_1_, bf16[96,4096]{1,0:T(8,128)(2,1)S(1)} %get-tuple-element.105.refs_2_, bf16[96,4096]{1,0:T(8,128)(2,1)S(1)} %get-tuple-element.108.refs_3_.refs_5_, ...), custom_call_target="tpu_custom_call" | custom-call | tf_op jit(solution)/shard_map/lower/pallas_call | solution.py:38
  100.3 8.6 %collective-permute-done.13.refs_1_ = bf16[96,4096]{1,0:T(8,128)(2,1)S(1)} collective-permute-done((bf16[96,4096]{1,0:T(8,128)(2,1)S(1)}, bf16[96,4096]{1,0:T(8,128)(2,1)S(1)}, u32[]{:S(2)}, u32[]{:S(2)}) %collective-permute-start.13) | collective-permute-done | bytes 786464 | tf_op jit(solution)/shard_map/ppermute | solution.py:419
  109.2 1.3 collective-permute-start.15
  111.4 4.6 %collective-permute-start.16 = (bf16[96,4096]{1,0:T(8,128)(2,1)S(1)}, bf16[96,4096]{1,0:T(8,128)(2,1)S(1)}, u32[]{:S(2)}, u32[]{:S(2)}) collective-permute-start(bf16[96,4096]{1,0:T(8,128)(2,1)S(1)} %get-tuple-element.112.refs_5_.refs_1_), channel_id=1, source_target_pairs={{0,8},{10,2},{4,12},{14,6},{8,16},{18,10},{12,20},{22,14},{16,24},... | collective-permute-start | bytes 2359304 | tf_op jit(solution)/shard_map/ppermute | solution.py:419
  116.0 5.6 %project.8 = (bf16[128,4096]{1,0:T(8,128)(2,1)S(1)}, bf16[128,4096]{1,0:T(8,128)(2,1)S(1)}) custom-call(s32[1]{0:T(128)} %bitcast.2.spot0_ref.refs_0_, s32[1]{0:T(128)} %bitcast.3.spot1_ref.refs_0_, bf16[128,768]{1,0:T(8,128)(2,1)S(1)} %get-tuple-element.90.refs_0_, bf16[128,768]{1,0:T(8,128)(2,1)S(1)} %collective-permute-done.2.refs_6_.refs_2_.refs_1_, ...), custom_call_target="tpu_custom_call" | custom-call | tf_op jit(solution)/shard_map/project/pallas_call | solution.py:38
  121.7 5.0 %collective-permute-done.15.refs_1_ = bf16[96,4096]{1,0:T(8,128)(2,1)S(1)} collective-permute-done((bf16[96,4096]{1,0:T(8,128)(2,1)S(1)}, bf16[96,4096]{1,0:T(8,128)(2,1)S(1)}, u32[]{:S(2)}, u32[]{:S(2)}) %collective-permute-start.15) | collective-permute-done | bytes 786464 | tf_op jit(solution)/shard_map/ppermute | solution.py:419
  126.9 1.3 collective-permute-start.18
  128.2 2.5 collective-permute-done.16.refs_1_
  131.1 5.4 %collective-permute-start.19 = (bf16[96,4096]{1,0:T(8,128)(2,1)S(1)}, bf16[96,4096]{1,0:T(8,128)(2,1)S(1)}, u32[]{:S(2)}, u32[]{:S(2)}) collective-permute-start(bf16[96,4096]{1,0:T(8,128)(2,1)S(1)} %get-tuple-element.118.refs_3_.refs_5_), channel_id=1, source_target_pairs={{0,8},{10,2},{4,12},{14,6},{8,16},{18,10},{12,20},{22,14},{16,24},... | collective-permute-start | bytes 2359304 | tf_op jit(solution)/shard_map/ppermute | solution.py:419
  140.8 1.6 collective-permute-start.12
  142.4 4.2 %collective-permute-done.12 = bf16[128,768]{1,0:T(8,128)(2,1)S(1)} collective-permute-done((bf16[128,768]{1,0:T(8,128)(2,1)S(1)}, bf16[128,768]{1,0:T(8,128)(2,1)S(1)}, u32[]{:S(2)}, u32[]{:S(2)}) %collective-permute-start.12) | collective-permute-done | bytes 196640 | tf_op jit(solution)/shard_map/ppermute | solution.py:344
  146.6 3.3 %lower.7.refs_5_ = bf16[128,768]{1,0:T(8,128)(2,1)S(1)} custom-call(bf16[96,4096]{1,0:T(8,128)(2,1)S(1)} %get-tuple-element.110.refs_0_, bf16[96,4096]{1,0:T(8,128)(2,1)S(1)} %get-tuple-element.112.refs_5_.refs_1_, bf16[96,4096]{1,0:T(8,128)(2,1)S(1)} %get-tuple-element.115.refs_2_, bf16[96,4096]{1,0:T(8,128)(2,1)S(1)} %get-tuple-element.118.refs_3_.refs_5_, ...), custom_call_target="tpu_custom_call" | custom-call | tf_op jit(solution)/shard_map/lower/pallas_call | solution.py:38
  150.0 1.6 collective-permute-start.17
  151.8 1.3 collective-permute-start.20
  153.5 5.0 %collective-permute-start.21 = (bf16[96,4096]{1,0:T(8,128)(2,1)S(1)}, bf16[96,4096]{1,0:T(8,128)(2,1)S(1)}, u32[]{:S(2)}, u32[]{:S(2)}) collective-permute-start(bf16[96,4096]{1,0:T(8,128)(2,1)S(1)} %get-tuple-element.126.refs_4_.refs_1_), channel_id=1, source_target_pairs={{0,8},{10,2},{4,12},{14,6},{8,16},{18,10},{12,20},{22,14},{16,24},... | collective-permute-start | bytes 2359304 | tf_op jit(solution)/shard_map/ppermute | solution.py:419
  158.6 5.6 %project.9 = (bf16[128,4096]{1,0:T(8,128)(2,1)S(1)}, bf16[128,4096]{1,0:T(8,128)(2,1)S(1)}) custom-call(s32[1]{0:T(128)} %bitcast.2.spot0_ref.refs_0_, s32[1]{0:T(128)} %bitcast.3.spot1_ref.refs_0_, bf16[128,768]{1,0:T(8,128)(2,1)S(1)} %get-tuple-element.90.refs_0_, bf16[128,768]{1,0:T(8,128)(2,1)S(1)} %collective-permute-done.3.refs_7_.refs_2_.refs_1_, ...), custom_call_target="tpu_custom_call" | custom-call | tf_op jit(solution)/shard_map/project/pallas_call | solution.py:38
  164.3 1.9 collective-permute-done.20.refs_1_
  166.5 1.3 collective-permute-start.24
  167.8 8.3 %collective-permute-done.21.refs_1_ = bf16[96,4096]{1,0:T(8,128)(2,1)S(1)} collective-permute-done((bf16[96,4096]{1,0:T(8,128)(2,1)S(1)}, bf16[96,4096]{1,0:T(8,128)(2,1)S(1)}, u32[]{:S(2)}, u32[]{:S(2)}) %collective-permute-start.21) | collective-permute-done | bytes 786464 | tf_op jit(solution)/shard_map/ppermute | solution.py:419
  176.4 3.3 %lower.8.refs_5_ = bf16[128,768]{1,0:T(8,128)(2,1)S(1)} custom-call(bf16[96,4096]{1,0:T(8,128)(2,1)S(1)} %get-tuple-element.124.refs_0_, bf16[96,4096]{1,0:T(8,128)(2,1)S(1)} %get-tuple-element.126.refs_4_.refs_1_, bf16[96,4096]{1,0:T(8,128)(2,1)S(1)} %get-tuple-element.129.refs_2_, bf16[96,4096]{1,0:T(8,128)(2,1)S(1)} %get-tuple-element.132.refs_3_.refs_5_, ...), custom_call_target="tpu_custom_call" | custom-call | tf_op jit(solution)/shard_map/lower/pallas_call | solution.py:38
  180.5 4.4 %collective-permute-start.25 = (bf16[96,4096]{1,0:T(8,128)(2,1)S(1)}, bf16[96,4096]{1,0:T(8,128)(2,1)S(1)}, u32[]{:S(2)}, u32[]{:S(2)}) collective-permute-start(bf16[96,4096]{1,0:T(8,128)(2,1)S(1)} %get-tuple-element.132.refs_3_.refs_5_), channel_id=1, source_target_pairs={{0,8},{10,2},{4,12},{14,6},{8,16},{18,10},{12,20},{22,14},{16,24},... | collective-permute-start | bytes 2359304 | tf_op jit(solution)/shard_map/ppermute | solution.py:419
  186.6 1.3 collective-permute-start.26
  188.0 9.8 %collective-permute-done.25.refs_1_ = bf16[96,4096]{1,0:T(8,128)(2,1)S(1)} collective-permute-done((bf16[96,4096]{1,0:T(8,128)(2,1)S(1)}, bf16[96,4096]{1,0:T(8,128)(2,1)S(1)}, u32[]{:S(2)}, u32[]{:S(2)}) %collective-permute-start.25) | collective-permute-done | bytes 786464 | tf_op jit(solution)/shard_map/ppermute | solution.py:419
  198.1 4.4 %collective-permute-start.27 = (bf16[32,4096]{1,0:T(8,128)(2,1)S(1)}, bf16[32,4096]{1,0:T(8,128)(2,1)S(1)}, u32[]{:S(2)}, u32[]{:S(2)}) collective-permute-start(bf16[32,4096]{1,0:T(8,128)(2,1)S(1)} %get-tuple-element.141.refs_1_), channel_id=1, source_target_pairs={{0,8},{10,2},{4,12},{14,6},{8,16},{18,10},{12,20},{22,14},{16,24},... | collective-permute-start | bytes 786440 | tf_op jit(solution)/shard_map/ppermute | solution.py:419
  203.3 1.3 collective-permute-start.30
  204.6 1.7 collective-permute-done.27.refs_1_
  206.4 3.3 %lower.9.refs_1_ = bf16[128,768]{1,0:T(8,128)(2,1)S(1)} custom-call(bf16[96,4096]{1,0:T(8,128)(2,1)S(1)} %get-tuple-element.139.refs_0_, bf16[32,4096]{1,0:T(8,128)(2,1)S(1)} %get-tuple-element.141.refs_1_, bf16[32,4096]{1,0:T(8,128)(2,1)S(1)} %get-tuple-element.143.refs_2_, bf16[32,4096]{1,0:T(8,128)(2,1)S(1)} %combine.51.refs_3_.refs_5_, ...), custom_call_target="tpu_custom_call" | custom-call | tf_op jit(solution)/shard_map/lower/pallas_call | solution.py:38
  209.7 4.4 %collective-permute-start.31 = (bf16[32,4096]{1,0:T(8,128)(2,1)S(1)}, bf16[32,4096]{1,0:T(8,128)(2,1)S(1)}, u32[]{:S(2)}, u32[]{:S(2)}) collective-permute-start(bf16[32,4096]{1,0:T(8,128)(2,1)S(1)} %combine.51.refs_3_.refs_5_), channel_id=1, source_target_pairs={{0,8},{10,2},{4,12},{14,6},{8,16},{18,10},{12,20},{22,14},{16,24},... | collective-permute-start | bytes 786440 | tf_op jit(solution)/shard_map/ppermute | solution.py:419
  215.6 4.3 %collective-permute-done.28 = bf16[128,768]{1,0:T(8,128)(2,1)S(1)} collective-permute-done((bf16[128,768]{1,0:T(8,128)(2,1)S(1)}, bf16[128,768]{1,0:T(8,128)(2,1)S(1)}, u32[]{:S(2)}, u32[]{:S(2)}) %collective-permute-start.28) | collective-permute-done | bytes 196640 | tf_op jit(solution)/shard_map/ppermute | solution.py:344
  220.0 1.3 collective-permute-start.32
  221.4 5.2 %collective-permute-start.33 = (bf16[32,4096]{1,0:T(8,128)(2,1)S(1)}, bf16[32,4096]{1,0:T(8,128)(2,1)S(1)}, u32[]{:S(2)}, u32[]{:S(2)}) collective-permute-start(bf16[32,4096]{1,0:T(8,128)(2,1)S(1)} %combine.53.refs_1_), channel_id=1, source_target_pairs={{0,8},{10,2},{4,12},{14,6},{8,16},{18,10},{12,20},{22,14},{16,24},... | collective-permute-start | bytes 786440 | tf_op jit(solution)/shard_map/ppermute | solution.py:419
  226.7 4.5 %collective-permute-done.32.refs_0_ = bf16[32,4096]{1,0:T(8,128)(2,1)S(1)} collective-permute-done((bf16[32,4096]{1,0:T(8,128)(2,1)S(1)}, bf16[32,4096]{1,0:T(8,128)(2,1)S(1)}, u32[]{:S(2)}, u32[]{:S(2)}) %collective-permute-start.32) | collective-permute-done | bytes 262176 | tf_op jit(solution)/shard_map/ppermute | solution.py:419
  231.3 3.3 %lower.10.refs_1_ = bf16[128,768]{1,0:T(8,128)(2,1)S(1)} custom-call(bf16[32,4096]{1,0:T(8,128)(2,1)S(1)} %combine.52.refs_0_, bf16[32,4096]{1,0:T(8,128)(2,1)S(1)} %combine.53.refs_1_, bf16[32,4096]{1,0:T(8,128)(2,1)S(1)} %combine.54.refs_2_, bf16[32,4096]{1,0:T(8,128)(2,1)S(1)} %combine.55.refs_3_.refs_5_, bf16[4096,768]{1,0:T(8,128)(2,1)} %bitcast.44, ...), custom_call_target="tpu_custom_call" | custom-call | tf_op jit(solution)/shard_map/lower/pallas_call | solution.py:38
  235.3 1.6 collective-permute-start.29
  236.9 1.3 collective-permute-start.36
  238.2 4.6 %collective-permute-start.37 = (bf16[32,4096]{1,0:T(8,128)(2,1)S(1)}, bf16[32,4096]{1,0:T(8,128)(2,1)S(1)}, u32[]{:S(2)}, u32[]{:S(2)}) collective-permute-start(bf16[32,4096]{1,0:T(8,128)(2,1)S(1)} %combine.55.refs_3_.refs_5_), channel_id=1, source_target_pairs={{0,8},{10,2},{4,12},{14,6},{8,16},{18,10},{12,20},{22,14},{16,24},... | collective-permute-start | bytes 786440 | tf_op jit(solution)/shard_map/ppermute | solution.py:419
  243.4 3.6 %collective-permute-done.36.refs_0_ = bf16[32,4096]{1,0:T(8,128)(2,1)S(1)} collective-permute-done((bf16[32,4096]{1,0:T(8,128)(2,1)S(1)}, bf16[32,4096]{1,0:T(8,128)(2,1)S(1)}, u32[]{:S(2)}, u32[]{:S(2)}) %collective-permute-start.36) | collective-permute-done | bytes 262176 | tf_op jit(solution)/shard_map/ppermute | solution.py:419
  247.1 2.2 collective-permute-done.35.refs_7_
  249.3 3.3 %lower.11 = bf16[64,768]{1,0:T(8,128)(2,1)S(1)} custom-call(bf16[32,4096]{1,0:T(8,128)(2,1)S(1)} %combine.56.refs_0_, bf16[32,4096]{1,0:T(8,128)(2,1)S(1)} %combine.57.refs_1_.refs_3_, bf16[4096,768]{1,0:T(8,128)(2,1)} %bitcast.45, bf16[32,4096]{1,0:T(8,128)(2,1)S(1)} %combine.57.refs_1_.refs_3_, bf16[64,768]{1,0:T(8,128)(2,1)S(1)} %pad_maximum_fusion.3.refs_4_, ...), custom_call_target="tpu_custom_call" | custom-call | tf_op jit(solution)/shard_map/lower/pallas_call | solution.py:38
  252.6 1.5 collective-permute-start.38
  254.9 2.4 collective-permute-done.38
  (108 shorter events, 18.2 us)
Async XLA Ops:
  0.0 1.0 copy-start
  1.0 0.7 copy-start.1
  7.4 23.0 %collective-permute-start.5 = (bf16[64,4096]{1,0:T(8,128)(2,1)S(1)}, bf16[64,4096]{1,0:T(8,128)(2,1)S(1)}, u32[]{:S(2)}, u32[]{:S(2)}) collective-permute-start(bf16[64,4096]{1,0:T(8,128)(2,1)S(1)} %combine.31), channel_id=1, source_target_pairs={{0,8},{10,2},{4,12},{14,6},{8,16},{18,10},{12,20},{22,14},{16,24},... | collective-permute-start | bytes 1572872 | tf_op jit(solution)/shard_map/ppermute | solution.py:419
  12.5 22.8 %collective-permute-start = (bf16[64,4096]{1,0:T(8,128)(2,1)S(1)}, bf16[64,4096]{1,0:T(8,128)(2,1)S(1)}, u32[]{:S(2)}, u32[]{:S(2)}) collective-permute-start(bf16[64,4096]{1,0:T(8,128)(2,1)S(1)} %get-tuple-element.89.refs_4_), channel_id=1, source_target_pairs={{8,0},{2,10},{12,4},{6,14},{16,8},{10,18},{20,12},{14,22},{24,16},... | collective-permute-start | bytes 1572872 | tf_op jit(solution)/shard_map/ppermute | solution.py:419
  13.8 2.0 collective-permute-start.1
  14.1 7.7 %collective-permute-start.2 = (bf16[128,768]{1,0:T(8,128)(2,1)S(1)}, bf16[128,768]{1,0:T(8,128)(2,1)S(1)}, u32[]{:S(2)}, u32[]{:S(2)}) collective-permute-start(bf16[128,768]{1,0:T(8,128)(2,1)S(1)} %get-tuple-element.92), channel_id=1, source_target_pairs={{0,4},{2,6},{4,0},{6,2},{1,5},{3,7},{5,1},{7,3},{8,12},{10,14},{12... | collective-permute-start | bytes 589832 | tf_op jit(solution)/shard_map/ppermute | solution.py:421
  15.7 9.1 %collective-permute-start.3 = (bf16[128,768]{1,0:T(8,128)(2,1)S(1)}, bf16[128,768]{1,0:T(8,128)(2,1)S(1)}, u32[]{:S(2)}, u32[]{:S(2)}) collective-permute-start(bf16[128,768]{1,0:T(8,128)(2,1)S(1)} %get-tuple-element.93), channel_id=1, source_target_pairs={{0,6},{2,4},{4,2},{6,0},{1,7},{3,5},{5,3},{7,1},{8,14},{10,12},{12... | collective-permute-start | bytes 589832 | tf_op jit(solution)/shard_map/ppermute | solution.py:421
  30.6 15.5 %collective-permute-start.6 = (bf16[64,4096]{1,0:T(8,128)(2,1)S(1)}, bf16[64,4096]{1,0:T(8,128)(2,1)S(1)}, u32[]{:S(2)}, u32[]{:S(2)}) collective-permute-start(bf16[64,4096]{1,0:T(8,128)(2,1)S(1)} %combine.32), channel_id=1, source_target_pairs={{0,8},{10,2},{4,12},{14,6},{8,16},{18,10},{12,20},{22,14},{16,24},... | collective-permute-start | bytes 1572872 | tf_op jit(solution)/shard_map/ppermute | solution.py:419
  35.5 20.8 %collective-permute-start.4 = (bf16[64,4096]{1,0:T(8,128)(2,1)S(1)}, bf16[64,4096]{1,0:T(8,128)(2,1)S(1)}, u32[]{:S(2)}, u32[]{:S(2)}) collective-permute-start(bf16[64,4096]{1,0:T(8,128)(2,1)S(1)} %combine.30), channel_id=1, source_target_pairs={{8,0},{2,10},{12,4},{6,14},{16,8},{10,18},{20,12},{14,22},{24,16},... | collective-permute-start | bytes 1572872 | tf_op jit(solution)/shard_map/ppermute | solution.py:419
  46.3 13.4 %collective-permute-start.8 = (bf16[64,4096]{1,0:T(8,128)(2,1)S(1)}, bf16[64,4096]{1,0:T(8,128)(2,1)S(1)}, u32[]{:S(2)}, u32[]{:S(2)}) collective-permute-start(bf16[64,4096]{1,0:T(8,128)(2,1)S(1)} %combine.33.refs_5_), channel_id=1, source_target_pairs={{0,8},{10,2},{4,12},{14,6},{8,16},{18,10},{12,20},{22,14},{16,24},... | collective-permute-start | bytes 1572872 | tf_op jit(solution)/shard_map/ppermute | solution.py:419
  56.5 14.2 %collective-permute-start.7 = (bf16[64,4096]{1,0:T(8,128)(2,1)S(1)}, bf16[64,4096]{1,0:T(8,128)(2,1)S(1)}, u32[]{:S(2)}, u32[]{:S(2)}) collective-permute-start(bf16[64,4096]{1,0:T(8,128)(2,1)S(1)} %combine.34), channel_id=1, source_target_pairs={{8,0},{2,10},{12,4},{6,14},{16,8},{10,18},{20,12},{14,22},{24,16},... | collective-permute-start | bytes 1572872 | tf_op jit(solution)/shard_map/ppermute | solution.py:419
  60.0 14.2 %collective-permute-start.9 = (bf16[64,4096]{1,0:T(8,128)(2,1)S(1)}, bf16[64,4096]{1,0:T(8,128)(2,1)S(1)}, u32[]{:S(2)}, u32[]{:S(2)}) collective-permute-start(bf16[64,4096]{1,0:T(8,128)(2,1)S(1)} %get-tuple-element.100), channel_id=1, source_target_pairs={{0,8},{10,2},{4,12},{14,6},{8,16},{18,10},{12,20},{22,14},{16,24},... | collective-permute-start | bytes 1572872 | tf_op jit(solution)/shard_map/ppermute | solution.py:419
  71.0 19.2 %collective-permute-start.10 = (bf16[96,4096]{1,0:T(8,128)(2,1)S(1)}, bf16[96,4096]{1,0:T(8,128)(2,1)S(1)}, u32[]{:S(2)}, u32[]{:S(2)}) collective-permute-start(bf16[96,4096]{1,0:T(8,128)(2,1)S(1)} %get-tuple-element.99.refs_0_), channel_id=1, source_target_pairs={{8,0},{2,10},{12,4},{6,14},{16,8},{10,18},{20,12},{14,22},{24,16},... | collective-permute-start | bytes 2359304 | tf_op jit(solution)/shard_map/ppermute | solution.py:419
  74.5 17.8 %collective-permute-start.11 = (bf16[96,4096]{1,0:T(8,128)(2,1)S(1)}, bf16[96,4096]{1,0:T(8,128)(2,1)S(1)}, u32[]{:S(2)}, u32[]{:S(2)}) collective-permute-start(bf16[96,4096]{1,0:T(8,128)(2,1)S(1)} %get-tuple-element.102.refs_5_.refs_1_), channel_id=1, source_target_pairs={{0,8},{10,2},{4,12},{14,6},{8,16},{18,10},{12,20},{22,14},{16,24},... | collective-permute-start | bytes 2359304 | tf_op jit(solution)/shard_map/ppermute | solution.py:419
  90.6 18.3 %collective-permute-start.13 = (bf16[96,4096]{1,0:T(8,128)(2,1)S(1)}, bf16[96,4096]{1,0:T(8,128)(2,1)S(1)}, u32[]{:S(2)}, u32[]{:S(2)}) collective-permute-start(bf16[96,4096]{1,0:T(8,128)(2,1)S(1)} %get-tuple-element.105.refs_2_), channel_id=1, source_target_pairs={{8,0},{2,10},{12,4},{6,14},{16,8},{10,18},{20,12},{14,22},{24,16},... | collective-permute-start | bytes 2359304 | tf_op jit(solution)/shard_map/ppermute | solution.py:419
  92.5 18.5 %collective-permute-start.14 = (bf16[96,4096]{1,0:T(8,128)(2,1)S(1)}, bf16[96,4096]{1,0:T(8,128)(2,1)S(1)}, u32[]{:S(2)}, u32[]{:S(2)}) collective-permute-start(bf16[96,4096]{1,0:T(8,128)(2,1)S(1)} %get-tuple-element.108.refs_3_.refs_5_), channel_id=1, source_target_pairs={{0,8},{10,2},{4,12},{14,6},{8,16},{18,10},{12,20},{22,14},{16,24},... | collective-permute-start | bytes 2359304 | tf_op jit(solution)/shard_map/ppermute | solution.py:419
  109.2 17.4 %collective-permute-start.15 = (bf16[96,4096]{1,0:T(8,128)(2,1)S(1)}, bf16[96,4096]{1,0:T(8,128)(2,1)S(1)}, u32[]{:S(2)}, u32[]{:S(2)}) collective-permute-start(bf16[96,4096]{1,0:T(8,128)(2,1)S(1)} %get-tuple-element.110.refs_0_), channel_id=1, source_target_pairs={{8,0},{2,10},{12,4},{6,14},{16,8},{10,18},{20,12},{14,22},{24,16},... | collective-permute-start | bytes 2359304 | tf_op jit(solution)/shard_map/ppermute | solution.py:419
  111.4 19.4 %collective-permute-start.16 = (bf16[96,4096]{1,0:T(8,128)(2,1)S(1)}, bf16[96,4096]{1,0:T(8,128)(2,1)S(1)}, u32[]{:S(2)}, u32[]{:S(2)}) collective-permute-start(bf16[96,4096]{1,0:T(8,128)(2,1)S(1)} %get-tuple-element.112.refs_5_.refs_1_), channel_id=1, source_target_pairs={{0,8},{10,2},{4,12},{14,6},{8,16},{18,10},{12,20},{22,14},{16,24},... | collective-permute-start | bytes 2359304 | tf_op jit(solution)/shard_map/ppermute | solution.py:419
  121.6 20.7 %copy-start.7 = (f32[256,2]{0,1:T(2,128)S(1)}, f32[256,2]{0,1:T(2,128)}, u32[]{:S(2)}) copy-start(f32[256,2]{0,1:T(2,128)} %param.13) | copy-start | bytes 6148
  126.9 24.6 %collective-permute-start.18 = (bf16[96,4096]{1,0:T(8,128)(2,1)S(1)}, bf16[96,4096]{1,0:T(8,128)(2,1)S(1)}, u32[]{:S(2)}, u32[]{:S(2)}) collective-permute-start(bf16[96,4096]{1,0:T(8,128)(2,1)S(1)} %get-tuple-element.115.refs_2_), channel_id=1, source_target_pairs={{8,0},{2,10},{12,4},{6,14},{16,8},{10,18},{20,12},{14,22},{24,16},... | collective-permute-start | bytes 2359304 | tf_op jit(solution)/shard_map/ppermute | solution.py:419
  131.1 22.1 %collective-permute-start.19 = (bf16[96,4096]{1,0:T(8,128)(2,1)S(1)}, bf16[96,4096]{1,0:T(8,128)(2,1)S(1)}, u32[]{:S(2)}, u32[]{:S(2)}) collective-permute-start(bf16[96,4096]{1,0:T(8,128)(2,1)S(1)} %get-tuple-element.118.refs_3_.refs_5_), channel_id=1, source_target_pairs={{0,8},{10,2},{4,12},{14,6},{8,16},{18,10},{12,20},{22,14},{16,24},... | collective-permute-start | bytes 2359304 | tf_op jit(solution)/shard_map/ppermute | solution.py:419
  140.8 5.7 %collective-permute-start.12 = (bf16[128,768]{1,0:T(8,128)(2,1)S(1)}, bf16[128,768]{1,0:T(8,128)(2,1)S(1)}, u32[]{:S(2)}, u32[]{:S(2)}) collective-permute-start(bf16[128,768]{1,0:T(8,128)(2,1)S(1)} %lower.6.refs_5_), channel_id=1, source_target_pairs={{0,1},{1,0},{2,3},{3,2},{4,5},{5,4},{6,7},{7,6},{8,9},{9,8},{10,11... | collective-permute-start | bytes 589832 | tf_op jit(solution)/shard_map/ppermute | solution.py:344
  150.0 8.6 %collective-permute-start.17 = (bf16[128,768]{1,0:T(8,128)(2,1)S(1)}, bf16[128,768]{1,0:T(8,128)(2,1)S(1)}, u32[]{:S(2)}, u32[]{:S(2)}) collective-permute-start(bf16[128,768]{1,0:T(8,128)(2,1)S(1)} %lower.7.refs_5_), channel_id=1, source_target_pairs={{0,1},{1,0},{2,3},{3,2},{4,5},{5,4},{6,7},{7,6},{8,9},{9,8},{10,11... | collective-permute-start | bytes 589832 | tf_op jit(solution)/shard_map/ppermute | solution.py:344
  151.8 14.3 %collective-permute-start.20 = (bf16[96,4096]{1,0:T(8,128)(2,1)S(1)}, bf16[96,4096]{1,0:T(8,128)(2,1)S(1)}, u32[]{:S(2)}, u32[]{:S(2)}) collective-permute-start(bf16[96,4096]{1,0:T(8,128)(2,1)S(1)} %get-tuple-element.124.refs_0_), channel_id=1, source_target_pairs={{8,0},{2,10},{12,4},{6,14},{16,8},{10,18},{20,12},{14,22},{24,16},... | collective-permute-start | bytes 2359304 | tf_op jit(solution)/shard_map/ppermute | solution.py:419
  153.5 22.6 %collective-permute-start.21 = (bf16[96,4096]{1,0:T(8,128)(2,1)S(1)}, bf16[96,4096]{1,0:T(8,128)(2,1)S(1)}, u32[]{:S(2)}, u32[]{:S(2)}) collective-permute-start(bf16[96,4096]{1,0:T(8,128)(2,1)S(1)} %get-tuple-element.126.refs_4_.refs_1_), channel_id=1, source_target_pairs={{0,8},{10,2},{4,12},{14,6},{8,16},{18,10},{12,20},{22,14},{16,24},... | collective-permute-start | bytes 2359304 | tf_op jit(solution)/shard_map/ppermute | solution.py:419
  166.5 19.8 %collective-permute-start.24 = (bf16[96,4096]{1,0:T(8,128)(2,1)S(1)}, bf16[96,4096]{1,0:T(8,128)(2,1)S(1)}, u32[]{:S(2)}, u32[]{:S(2)}) collective-permute-start(bf16[96,4096]{1,0:T(8,128)(2,1)S(1)} %get-tuple-element.129.refs_2_), channel_id=1, source_target_pairs={{8,0},{2,10},{12,4},{6,14},{16,8},{10,18},{20,12},{14,22},{24,16},... | collective-permute-start | bytes 2359304 | tf_op jit(solution)/shard_map/ppermute | solution.py:419
  176.1 4.0 %copy-start.6 = (s32[64]{0:T(128)S(1)}, s32[64]{0:T(128)}, u32[]{:S(2)}) copy-start(s32[64]{0:T(128)} %constant.41.clone) | copy-start | bytes 772
  179.7 5.7 %collective-permute-start.22 = (bf16[128,768]{1,0:T(8,128)(2,1)S(1)}, bf16[128,768]{1,0:T(8,128)(2,1)S(1)}, u32[]{:S(2)}, u32[]{:S(2)}) collective-permute-start(bf16[128,768]{1,0:T(8,128)(2,1)S(1)} %lower.8.refs_5_), channel_id=1, source_target_pairs={{0,1},{1,0},{2,3},{3,2},{4,5},{5,4},{6,7},{7,6},{8,9},{9,8},{10,11... | collective-permute-start | bytes 589832 | tf_op jit(solution)/shard_map/ppermute | solution.py:344
  180.5 17.3 %collective-permute-start.25 = (bf16[96,4096]{1,0:T(8,128)(2,1)S(1)}, bf16[96,4096]{1,0:T(8,128)(2,1)S(1)}, u32[]{:S(2)}, u32[]{:S(2)}) collective-permute-start(bf16[96,4096]{1,0:T(8,128)(2,1)S(1)} %get-tuple-element.132.refs_3_.refs_5_), channel_id=1, source_target_pairs={{0,8},{10,2},{4,12},{14,6},{8,16},{18,10},{12,20},{22,14},{16,24},... | collective-permute-start | bytes 2359304 | tf_op jit(solution)/shard_map/ppermute | solution.py:419
  186.6 16.4 %collective-permute-start.26 = (bf16[96,4096]{1,0:T(8,128)(2,1)S(1)}, bf16[96,4096]{1,0:T(8,128)(2,1)S(1)}, u32[]{:S(2)}, u32[]{:S(2)}) collective-permute-start(bf16[96,4096]{1,0:T(8,128)(2,1)S(1)} %get-tuple-element.139.refs_0_), channel_id=1, source_target_pairs={{8,0},{2,10},{12,4},{6,14},{16,8},{10,18},{20,12},{14,22},{24,16},... | collective-permute-start | bytes 2359304 | tf_op jit(solution)/shard_map/ppermute | solution.py:419
  198.1 8.3 %collective-permute-start.27 = (bf16[32,4096]{1,0:T(8,128)(2,1)S(1)}, bf16[32,4096]{1,0:T(8,128)(2,1)S(1)}, u32[]{:S(2)}, u32[]{:S(2)}) collective-permute-start(bf16[32,4096]{1,0:T(8,128)(2,1)S(1)} %get-tuple-element.141.refs_1_), channel_id=1, source_target_pairs={{0,8},{10,2},{4,12},{14,6},{8,16},{18,10},{12,20},{22,14},{16,24},... | collective-permute-start | bytes 786440 | tf_op jit(solution)/shard_map/ppermute | solution.py:419
  202.5 12.7 %collective-permute-start.23 = (bf16[128,768]{1,0:T(8,128)(2,1)S(1)}, bf16[128,768]{1,0:T(8,128)(2,1)S(1)}, u32[]{:S(2)}, u32[]{:S(2)}) collective-permute-start(bf16[128,768]{1,0:T(8,128)(2,1)S(1)} %pad_maximum_fusion), channel_id=1, source_target_pairs={{0,2},{2,0},{4,6},{6,4},{1,3},{3,1},{5,7},{7,5},{8,10},{10,8},{12,... | collective-permute-start | bytes 589832 | tf_op jit(solution)/shard_map/ppermute | solution.py:391
  202.9 12.3 %copy-start.5 = (s32[128]{0:T(128)S(1)}, s32[128]{0:T(128)}, u32[]{:S(2)}) copy-start(s32[128]{0:T(128)} %constant.42.clone) | copy-start | bytes 1540
  203.3 16.6 %collective-permute-start.30 = (bf16[32,4096]{1,0:T(8,128)(2,1)S(1)}, bf16[32,4096]{1,0:T(8,128)(2,1)S(1)}, u32[]{:S(2)}, u32[]{:S(2)}) collective-permute-start(bf16[32,4096]{1,0:T(8,128)(2,1)S(1)} %get-tuple-element.143.refs_2_), channel_id=1, source_target_pairs={{8,0},{2,10},{12,4},{6,14},{16,8},{10,18},{20,12},{14,22},{24,16},... | collective-permute-start | bytes 786440 | tf_op jit(solution)/shard_map/ppermute | solution.py:419
  209.7 11.6 %collective-permute-start.31 = (bf16[32,4096]{1,0:T(8,128)(2,1)S(1)}, bf16[32,4096]{1,0:T(8,128)(2,1)S(1)}, u32[]{:S(2)}, u32[]{:S(2)}) collective-permute-start(bf16[32,4096]{1,0:T(8,128)(2,1)S(1)} %combine.51.refs_3_.refs_5_), channel_id=1, source_target_pairs={{0,8},{10,2},{4,12},{14,6},{8,16},{18,10},{12,20},{22,14},{16,24},... | collective-permute-start | bytes 786440 | tf_op jit(solution)/shard_map/ppermute | solution.py:419
  214.2 5.7 %collective-permute-start.28 = (bf16[128,768]{1,0:T(8,128)(2,1)S(1)}, bf16[128,768]{1,0:T(8,128)(2,1)S(1)}, u32[]{:S(2)}, u32[]{:S(2)}) collective-permute-start(bf16[128,768]{1,0:T(8,128)(2,1)S(1)} %lower.9.refs_1_), channel_id=1, source_target_pairs={{0,1},{1,0},{2,3},{3,2},{4,5},{5,4},{6,7},{7,6},{8,9},{9,8},{10,11... | collective-permute-start | bytes 589832 | tf_op jit(solution)/shard_map/ppermute | solution.py:344
  220.0 11.2 %collective-permute-start.32 = (bf16[32,4096]{1,0:T(8,128)(2,1)S(1)}, bf16[32,4096]{1,0:T(8,128)(2,1)S(1)}, u32[]{:S(2)}, u32[]{:S(2)}) collective-permute-start(bf16[32,4096]{1,0:T(8,128)(2,1)S(1)} %combine.52.refs_0_), channel_id=1, source_target_pairs={{8,0},{2,10},{12,4},{6,14},{16,8},{10,18},{20,12},{14,22},{24,16},... | collective-permute-start | bytes 786440 | tf_op jit(solution)/shard_map/ppermute | solution.py:419
  221.4 9.9 %collective-permute-start.33 = (bf16[32,4096]{1,0:T(8,128)(2,1)S(1)}, bf16[32,4096]{1,0:T(8,128)(2,1)S(1)}, u32[]{:S(2)}, u32[]{:S(2)}) collective-permute-start(bf16[32,4096]{1,0:T(8,128)(2,1)S(1)} %combine.53.refs_1_), channel_id=1, source_target_pairs={{0,8},{10,2},{4,12},{14,6},{8,16},{18,10},{12,20},{22,14},{16,24},... | collective-permute-start | bytes 786440 | tf_op jit(solution)/shard_map/ppermute | solution.py:419
  234.6 8.1 %collective-permute-start.34 = (bf16[128,768]{1,0:T(8,128)(2,1)S(1)}, bf16[128,768]{1,0:T(8,128)(2,1)S(1)}, u32[]{:S(2)}, u32[]{:S(2)}) collective-permute-start(bf16[128,768]{1,0:T(8,128)(2,1)S(1)} %lower.10.refs_1_), channel_id=1, source_target_pairs={{0,1},{1,0},{2,3},{3,2},{4,5},{5,4},{6,7},{7,6},{8,9},{9,8},{10,11... | collective-permute-start | bytes 589832 | tf_op jit(solution)/shard_map/ppermute | solution.py:344
  235.3 11.8 %collective-permute-start.29 = (bf16[128,768]{1,0:T(8,128)(2,1)S(1)}, bf16[128,768]{1,0:T(8,128)(2,1)S(1)}, u32[]{:S(2)}, u32[]{:S(2)}) collective-permute-start(bf16[128,768]{1,0:T(8,128)(2,1)S(1)} %pad_maximum_fusion.1), channel_id=1, source_target_pairs={{0,4},{2,6},{4,0},{6,2},{1,5},{3,7},{5,1},{7,3},{8,12},{10,14},{12... | collective-permute-start | bytes 589832 | tf_op jit(solution)/shard_map/ppermute | solution.py:391
  236.9 10.1 %collective-permute-start.36 = (bf16[32,4096]{1,0:T(8,128)(2,1)S(1)}, bf16[32,4096]{1,0:T(8,128)(2,1)S(1)}, u32[]{:S(2)}, u32[]{:S(2)}) collective-permute-start(bf16[32,4096]{1,0:T(8,128)(2,1)S(1)} %combine.54.refs_2_), channel_id=1, source_target_pairs={{8,0},{2,10},{12,4},{6,14},{16,8},{10,18},{20,12},{14,22},{24,16},... | collective-permute-start | bytes 786440 | tf_op jit(solution)/shard_map/ppermute | solution.py:419
  238.2 8.8 %collective-permute-start.37 = (bf16[32,4096]{1,0:T(8,128)(2,1)S(1)}, bf16[32,4096]{1,0:T(8,128)(2,1)S(1)}, u32[]{:S(2)}, u32[]{:S(2)}) collective-permute-start(bf16[32,4096]{1,0:T(8,128)(2,1)S(1)} %combine.55.refs_3_.refs_5_), channel_id=1, source_target_pairs={{0,8},{10,2},{4,12},{14,6},{8,16},{18,10},{12,20},{22,14},{16,24},... | collective-permute-start | bytes 786440 | tf_op jit(solution)/shard_map/ppermute | solution.py:419
  242.8 11.3 %copy-start.4 = (s32[128]{0:T(128)S(1)}, s32[128]{0:T(128)}, u32[]{:S(2)}) copy-start(s32[128]{0:T(128)} %constant.44.clone) | copy-start | bytes 1540
  243.0 6.3 %collective-permute-start.35 = (bf16[128,768]{1,0:T(8,128)(2,1)S(1)}, bf16[128,768]{1,0:T(8,128)(2,1)S(1)}, u32[]{:S(2)}, u32[]{:S(2)}) collective-permute-start(bf16[128,768]{1,0:T(8,128)(2,1)S(1)} %pad_maximum_fusion.2), channel_id=1, source_target_pairs={{0,6},{2,4},{4,2},{6,0},{1,7},{3,5},{5,3},{7,1},{8,14},{10,12},{12... | collective-permute-start | bytes 589832 | tf_op jit(solution)/shard_map/ppermute | solution.py:391
  243.4 14.0 %copy-start.3 = (s32[64]{0:T(128)S(1)}, s32[64]{0:T(128)}, u32[]{:S(2)}) copy-start(s32[64]{0:T(128)} %constant.45.clone) | copy-start | bytes 772
  247.1 11.0 %copy-start.2 = (s32[128]{0:T(128)S(1)}, s32[128]{0:T(128)}, u32[]{:S(2)}) copy-start(s32[128]{0:T(128)} %constant.43.clone) | copy-start | bytes 1540
  252.6 4.7 %collective-permute-start.38 = (bf16[64,768]{1,0:T(8,128)(2,1)S(1)}, bf16[64,768]{1,0:T(8,128)(2,1)S(1)}, u32[]{:S(2)}, u32[]{:S(2)}) collective-permute-start(bf16[64,768]{1,0:T(8,128)(2,1)S(1)} %lower.11), channel_id=1, source_target_pairs={{0,1},{1,0},{2,3},{3,2},{4,5},{5,4},{6,7},{7,6},{8,9},{9,8},{10,11... | collective-permute-start | bytes 294920 | tf_op jit(solution)/shard_map/ppermute | solution.py:344

commit v4 on v3

--- a/solution.py
+++ b/solution.py
@@ -300,6 +300,31 @@
     )[0]
 
 
+def mix(m, experts, half, places, gates, spans, parts):
+    n, width = gates.shape[0], parts[0].shape[1]
+
+    def body(place_ref, gate_ref, *refs):
+        total = jnp.zeros((n, width), F32)
+        for k in range(2):
+            y = jnp.zeros((n, width), F32)
+            for (j, start, stop, i), part_ref in zip(spans, refs):
+                rows = (stop - start) * m
+                for f in range(2):
+                    rank = lax.broadcasted_iota(I32, (rows, n), 0) + (i * m + f * half)
+                    chosen = one_hot(rank * experts + j == place_ref[k : k + 1, :])
+                    y += lax.dot_general(
+                        chosen,
+                        part_ref[f * rows : (f + 1) * rows, :],
+                        (((0,), (0,)), ((), ())),
+                        preferred_element_type=F32,
+                    )
+            total += gate_ref[:, k : k + 1] * y
+        refs[-1][...] = total.astype(BF16)
+
+    specs = [WHOLE] * (2 + len(parts))
+    return call(body, "mix", [array(n, width)], (places, gates, *parts), specs)[0]
+
+
 def local(tokens, route_ids, gates, w_gate, w_up, w_down):
     experts = lax.axis_size("expert")
     depth = lax.axis_size("dp")
@@ -381,16 +406,31 @@
             for f in range(2)
         ]
 
-    parts = []
+    parts, sent = [None] * len(spans), set()
+
+    def ready_spans():
+        fresh = []
+        for index, (j, start, stop, i) in enumerate(spans):
+            if index not in sent and all(q in outs for q in rounds_of(start, stop)):
+                sent.add(index)
+                fresh.append((index, lax.optimization_barrier(jnp.concatenate(finished(start, stop)))))
+        return fresh
+
+    def forward(index, part):
+        j = spans[index][0]
+        if j:
+            part = lax.ppermute(part, "expert", [(a, a ^ j) for a in range(experts)])
+        parts[index] = part
 
     def deliver():
-        for j, start, stop, i in spans[len(parts) :]:
-            if all(q in outs for q in rounds_of(start, stop)):
-                part = lax.optimization_barrier(jnp.concatenate(finished(start, stop)))
-                if j:
-                    part = lax.ppermute(part, "expert", [(a, a ^ j) for a in range(experts)])
-                parts.append(part)
-
+        for index, part in ready_spans():
+            forward(index, part)
+
+    def settle(ready, result):
+        for k, q in enumerate(ready):
+            outs[q] = result[2 * m * k : 2 * m * (k + 1)]
+
+    lowered = None
     for s in range(ticks):
         summing = s < sums_end
         for f in range(2):
@@ -399,6 +439,11 @@
             carries = first <= s < first + chunks + last
             if not (summing or carries):
                 continue
+            relay, moving = (), ()
+            if f == 1:
+                moving = ready_spans() if s < ticks - 2 else ()
+                relay = list(picked[1:]) if s == 0 else [part for _, part in moving]
+                relay += [lowered[1]] if lowered else []
             message, act[f], relayed = combine(
                 m,
                 units,
@@ -412,18 +457,29 @@
                 summing and s >= last,
                 spot[f],
                 ties,
-                picked[1:] if s == 0 and f == 1 else (),
+                relay,
             )
             ties = []
             if s < sums_end - 1 or (carries and s < first + chunks + last - 1):
                 got[f] = lax.ppermute(message, ("dp", "expert"), flows[f])
-            for j, value in enumerate(relayed, 1):
-                rows.append(lax.ppermute(value, "expert", [(a, a ^ j) for a in range(experts)]))
+            if s == 0:
+                for j, value in enumerate(relayed, 1):
+                    rows.append(lax.ppermute(value, "expert", [(a, a ^ j) for a in range(experts)]))
+            elif relayed:
+                for (index, _), part in zip(moving, relayed):
+                    forward(index, part)
+                    ties.append(parts[index])
+                if lowered:
+                    settle(lowered[0], across(relayed[-1]))
+                    ties.append(outs[lowered[0][0]])
+                    lowered = None
+            if s == 1 and f == 1:
+                ties += rows[2:]
             if carries:
                 held[o][s - first] = message
             if f == (0 if s else 1) and s + 1 < sums_end and s + 1 not in partial:
                 rounds = [r for r in (s + 1, s + 2) if r < sums_end]
-                wait = [message] if s else [message, *rows[1:]]
+                wait = [message]
                 g, u = project(m, spot, rows, [sources(r) for r in rounds], weights, wait)
                 for k, r in enumerate(rounds):
                     partial[r] = (g, u, 2 * m * k)
@@ -433,24 +489,16 @@
                 pairs = [(held[0][q], held[1][q]) for q in ready]
                 if ready[0] == ends - 1:
                     deliver()
-                result = lower(m, pairs, wd, [message] + (parts if ready[0] == ends - 1 else []))
-                ties.append(result)
-                result = across(result)
-                for k, q in enumerate(ready):
-                    outs[q] = result[2 * m * k : 2 * m * (k + 1)]
-
-    yields = [jnp.zeros((n, width), F32), jnp.zeros((n, width), F32)]
+                arrived = [p for p in parts if p is not None] if ready[0] == ends - 1 else []
+                result = lower(m, pairs, wd, [message] + arrived)
+                if f == 0 and s < ticks - 1:
+                    lowered = (ready, result)
+                else:
+                    ties.append(result)
+                    settle(ready, across(result))
+
     deliver()
-    for (j, start, stop, i), part in zip(spans, parts):
-        ranks = np.arange((stop - start) * m, dtype=np.int32) + i * m
-        label = jnp.asarray(np.concatenate([ranks, ranks + half]) * experts + j)
-        for k in range(2):
-            chosen = (label[:, None] == places[k][None, :]).astype(BF16)
-            yields[k] += lax.dot_general(
-                chosen, part, (((0,), (0,)), ((), ())), preferred_element_type=F32
-            )
-    mixed = gates[:, 0:1] * yields[0] + gates[:, 1:2] * yields[1]
-    return mixed.astype(BF16)
+    return mix(m, experts, half, places, gates, spans, parts)
 
 
 def solution(mesh):

time: 261 us -> 274 us (1.050)
  waiting for transfers between devices: 95.2 us -> 114 us
  matrix products: 4.5 us -> 0 us
  starting transfers between devices: 92.5 us -> 88.4 us
  Pallas kernels: 59.8 us -> 62.9 us
    ppermute x27, waiting for transfers between devices: 72.5 us -> 92.3 us  [local(): got[f] = lax.ppermute(message, ('dp', 'expert'), flows[f])]
    dot_general x10 -> x0, matrix products: 4.5 us -> none  [local(): lax.dot_general(chosen, part, (((0,), (0,)), ((), ())), preferred_element...]
    ppermute x27, starting transfers between devices: 82.2 us -> 78.2 us  [local(): got[f] = lax.ppermute(message, ('dp', 'expert'), flows[f])]
    ppermute x6, waiting for transfers between devices: 11.5 us -> 7.7 us  [across(): other = lax.ppermute(part, 'tensor', [(0, 1), (1, 0)])]
    ppermute x3, waiting for transfers between devices: 2.17 us -> 5.45 us  [forward(): part = lax.ppermute(part, 'expert', [(a, a ^ j) for a in range(experts)])]
    pallas_call x41 -> x42, Pallas kernels: 59.8 us -> 62.9 us  [call(): pl.pallas_call(body, name=name, out_shape=shapes, in_specs=specs, out_spe...]
  transfers between devices with their start and end apart: 39 -> 39, of which waited for: 24 -> 26; matrix products, arithmetic and copies ran while one was open for 1% -> 0% of each run, Pallas kernels for 18% -> 18%
where the time goes in v4:
time: 274 us; the launch traced here: 273 us
  waiting for transfers between devices  114 us (42%)
  starting transfers between devices  88.4 us (32%)
  Pallas kernels  62.9 us (23%)
  between operations  4.66 us (2%)
    ppermute x27, waiting for transfers between devices, local(): got[f] = lax.ppermute(message, ('dp', 'expert'), flows[f])  92.3 us
    ppermute x27, starting transfers between devices, local(): got[f] = lax.ppermute(message, ('dp', 'expert'), flows[f])  78.2 us
    pallas_call x42, Pallas kernels, call(): pl.pallas_call(body, name=name, out_shape=shapes, in_specs=specs, out_spe...  62.9 us
    ppermute x3, waiting for transfers between devices, local(): lax.ppermute(value, 'expert', [(a, a ^ j) for a in range(experts)])  8.92 us
    ppermute x6, waiting for transfers between devices, across(): other = lax.ppermute(part, 'tensor', [(0, 1), (1, 0)])  7.7 us
    ppermute x6, starting transfers between devices, across(): other = lax.ppermute(part, 'tensor', [(0, 1), (1, 0)])  7.2 us
  transfers between devices with their start and end apart: 39, of which 26 were waited for; matrix products, arithmetic and copies ran while one was open for 0% of the time, Pallas kernels for 18%

profile of v4, /device:TPU:0, one launch (start us, length us, event | category | flops | bytes accessed | tf_op | source)
XLA Modules:
  0.0 273.4 jit_solution(11904567927815131721)
XLA Ops:
  1.7 5.7 %begin.1 = (s32[2,256]{1,0:T(2,128)S(1)}, bf16[128,768]{1,0:T(8,128)(2,1)S(1)}, bf16[128,768]{1,0:T(8,128)(2,1)S(1)}, bf16[128,768]{1,0:T(8,128)(2,1)S(1)}, bf16...) custom-call(s32[1]{0:T(128)} %bitcast.e_ref, ...), custom_call_target="tpu_custom_call" | custom-call | tf_op jit(solution)/shard_map/begin/pallas_call | solution.py:38
  7.4 5.0 %collective-permute-start.4 = (bf16[64,4096]{1,0:T(8,128)(2,1)S(1)}, bf16[64,4096]{1,0:T(8,128)(2,1)S(1)}, u32[]{:S(2)}, u32[]{:S(2)}) collective-permute-start(bf16[64,4096]{1,0:T(8,128)(2,1)S(1)} %combine.31), channel_id=1, source_target_pairs={{0,8},{10,2},{4,12},{14,6},{8,16},{18,10},{12,20},{22,14},{16,24},... | collective-permute-start | bytes 1572872 | tf_op jit(solution)/shard_map/ppermute | solution.py:464
  12.5 1.3 collective-permute-start
  15.3 5.6 %project.5 = (bf16[128,4096]{1,0:T(8,128)(2,1)S(1)}, bf16[128,4096]{1,0:T(8,128)(2,1)S(1)}) custom-call(s32[1]{0:T(128)} %bitcast.1.spot0_ref.refs_0_, s32[1]{0:T(128)} %bitcast.2.spot1_ref.refs_0_, bf16[128,768]{1,0:T(8,128)(2,1)S(1)} %get-tuple-element.100.refs_0_, bf16[128,768]{1,0:T(8,128)(2,1)S(1)} %collective-permute-done.1.refs_1_.refs_0_, ...), custom_call_target="tpu_custom_call" | custom-call | tf_op jit(solution)/shard_map/project/pallas_call | solution.py:38
  20.9 2.9 %collective-permute-done.4.refs_0_ = bf16[64,4096]{1,0:T(8,128)(2,1)S(1)} collective-permute-done((bf16[64,4096]{1,0:T(8,128)(2,1)S(1)}, bf16[64,4096]{1,0:T(8,128)(2,1)S(1)}, u32[]{:S(2)}, u32[]{:S(2)}) %collective-permute-start.4) | collective-permute-done | bytes 524320 | tf_op jit(solution)/shard_map/ppermute | solution.py:464
  23.9 4.4 %collective-permute-start.5 = (bf16[64,4096]{1,0:T(8,128)(2,1)S(1)}, bf16[64,4096]{1,0:T(8,128)(2,1)S(1)}, u32[]{:S(2)}, u32[]{:S(2)}) collective-permute-start(bf16[64,4096]{1,0:T(8,128)(2,1)S(1)} %combine.32), channel_id=1, source_target_pairs={{0,8},{10,2},{4,12},{14,6},{8,16},{18,10},{12,20},{22,14},{16,24},... | collective-permute-start | bytes 1572872 | tf_op jit(solution)/shard_map/ppermute | solution.py:464
  28.6 1.3 collective-permute-start.2
  29.9 1.4 collective-permute-start.3
  31.3 5.9 %collective-permute-done.3.refs_3_.refs_2_.refs_1_ = bf16[128,768]{1,0:T(8,128)(2,1)S(1)} collective-permute-done((bf16[128,768]{1,0:T(8,128)(2,1)S(1)}, bf16[128,768]{1,0:T(8,128)(2,1)S(1)}, u32[]{:S(2)}, u32[]{:S(2)}) %collective-permute-start.3) | collective-permute-done | bytes 196640 | tf_op jit(solution)/shard_map/ppermute | solution.py:467
  37.1 1.8 collective-permute-done.6.refs_4_.refs_2_.refs_1_
  38.9 1.5 collective-permute-done.5.refs_0_
  40.5 4.4 %collective-permute-start.8 = (bf16[64,4096]{1,0:T(8,128)(2,1)S(1)}, bf16[64,4096]{1,0:T(8,128)(2,1)S(1)}, u32[]{:S(2)}, u32[]{:S(2)}) collective-permute-start(bf16[64,4096]{1,0:T(8,128)(2,1)S(1)} %combine.33.refs_5_), channel_id=1, source_target_pairs={{0,8},{10,2},{4,12},{14,6},{8,16},{18,10},{12,20},{22,14},{16,24},... | collective-permute-start | bytes 1572872 | tf_op jit(solution)/shard_map/ppermute | solution.py:464
  45.0 5.6 %project.6 = (bf16[128,4096]{1,0:T(8,128)(2,1)S(1)}, bf16[128,4096]{1,0:T(8,128)(2,1)S(1)}) custom-call(s32[1]{0:T(128)} %bitcast.1.spot0_ref.refs_0_, s32[1]{0:T(128)} %bitcast.2.spot1_ref.refs_0_, bf16[128,768]{1,0:T(8,128)(2,1)S(1)} %get-tuple-element.100.refs_0_, bf16[128,768]{1,0:T(8,128)(2,1)S(1)} %collective-permute-done.1.refs_1_.refs_0_, ...), custom_call_target="tpu_custom_call" | custom-call | tf_op jit(solution)/shard_map/project/pallas_call | solution.py:38
  50.8 1.3 collective-permute-start.7
  52.4 9.4 %collective-permute-done.7.refs_1_ = bf16[64,4096]{1,0:T(8,128)(2,1)S(1)} collective-permute-done((bf16[64,4096]{1,0:T(8,128)(2,1)S(1)}, bf16[64,4096]{1,0:T(8,128)(2,1)S(1)}, u32[]{:S(2)}, u32[]{:S(2)}) %collective-permute-start.7) | collective-permute-done | bytes 524320 | tf_op jit(solution)/shard_map/ppermute | solution.py:464
  62.2 1.3 collective-permute-start.9
  63.5 4.6 %collective-permute-start.10 = (bf16[64,4096]{1,0:T(8,128)(2,1)S(1)}, bf16[64,4096]{1,0:T(8,128)(2,1)S(1)}, u32[]{:S(2)}, u32[]{:S(2)}) collective-permute-start(bf16[64,4096]{1,0:T(8,128)(2,1)S(1)} %get-tuple-element.110), channel_id=1, source_target_pairs={{0,8},{10,2},{4,12},{14,6},{8,16},{18,10},{12,20},{22,14},{16,24},... | collective-permute-start | bytes 1572872 | tf_op jit(solution)/shard_map/ppermute | solution.py:464
  68.0 9.0 %collective-permute-done.10.refs_1_ = bf16[64,4096]{1,0:T(8,128)(2,1)S(1)} collective-permute-done((bf16[64,4096]{1,0:T(8,128)(2,1)S(1)}, bf16[64,4096]{1,0:T(8,128)(2,1)S(1)}, u32[]{:S(2)}, u32[]{:S(2)}) %collective-permute-start.10) | collective-permute-done | bytes 524320 | tf_op jit(solution)/shard_map/ppermute | solution.py:464
  77.3 4.4 %collective-permute-start.12 = (bf16[96,4096]{1,0:T(8,128)(2,1)S(1)}, bf16[96,4096]{1,0:T(8,128)(2,1)S(1)}, u32[]{:S(2)}, u32[]{:S(2)}) collective-permute-start(bf16[96,4096]{1,0:T(8,128)(2,1)S(1)} %get-tuple-element.113.refs_5_.refs_1_), channel_id=1, source_target_pairs={{0,8},{10,2},{4,12},{14,6},{8,16},{18,10},{12,20},{22,14},{16,24},... | collective-permute-start | bytes 2359304 | tf_op jit(solution)/shard_map/ppermute | solution.py:464
  81.8 5.6 %project.7 = (bf16[128,4096]{1,0:T(8,128)(2,1)S(1)}, bf16[128,4096]{1,0:T(8,128)(2,1)S(1)}) custom-call(s32[1]{0:T(128)} %bitcast.1.spot0_ref.refs_0_, s32[1]{0:T(128)} %bitcast.2.spot1_ref.refs_0_, bf16[128,768]{1,0:T(8,128)(2,1)S(1)} %collective-permute-done.1.refs_1_.refs_0_, bf16[128,768]{1,0:T(8,128)(2,1)S(1)} %collective-permute-done.3.refs_3_.refs_2_.refs_1_, ...), custom_call_target="tpu_custom_call" | custom-call | tf_op jit(solution)/shard_map/project/pallas_call | solution.py:38
  87.7 1.3 collective-permute-start.11
  89.0 3.3 %collective-permute-done.12.refs_1_ = bf16[96,4096]{1,0:T(8,128)(2,1)S(1)} collective-permute-done((bf16[96,4096]{1,0:T(8,128)(2,1)S(1)}, bf16[96,4096]{1,0:T(8,128)(2,1)S(1)}, u32[]{:S(2)}, u32[]{:S(2)}) %collective-permute-start.12) | collective-permute-done | bytes 786464 | tf_op jit(solution)/shard_map/ppermute | solution.py:464
  92.7 4.4 %collective-permute-start.14 = (bf16[96,4096]{1,0:T(8,128)(2,1)S(1)}, bf16[96,4096]{1,0:T(8,128)(2,1)S(1)}, u32[]{:S(2)}, u32[]{:S(2)}) collective-permute-start(bf16[96,4096]{1,0:T(8,128)(2,1)S(1)} %get-tuple-element.119.refs_3_.refs_5_), channel_id=1, source_target_pairs={{0,8},{10,2},{4,12},{14,6},{8,16},{18,10},{12,20},{22,14},{16,24},... | collective-permute-start | bytes 2359304 | tf_op jit(solution)/shard_map/ppermute | solution.py:464
  97.1 3.3 %lower.6.refs_5_ = bf16[128,768]{1,0:T(8,128)(2,1)S(1)} custom-call(bf16[96,4096]{1,0:T(8,128)(2,1)S(1)} %get-tuple-element.109.refs_0_, bf16[96,4096]{1,0:T(8,128)(2,1)S(1)} %get-tuple-element.113.refs_5_.refs_1_, bf16[96,4096]{1,0:T(8,128)(2,1)S(1)} %get-tuple-element.115.refs_2_, bf16[96,4096]{1,0:T(8,128)(2,1)S(1)} %get-tuple-element.119.refs_3_.refs_5_, ...), custom_call_target="tpu_custom_call" | custom-call | tf_op jit(solution)/shard_map/lower/pallas_call | solution.py:38
  100.4 6.5 %collective-permute-done.11.refs_1_ = bf16[96,4096]{1,0:T(8,128)(2,1)S(1)} collective-permute-done((bf16[96,4096]{1,0:T(8,128)(2,1)S(1)}, bf16[96,4096]{1,0:T(8,128)(2,1)S(1)}, u32[]{:S(2)}, u32[]{:S(2)}) %collective-permute-start.11) | collective-permute-done | bytes 786464 | tf_op jit(solution)/shard_map/ppermute | solution.py:464
  107.2 1.3 collective-permute-start.13
  108.5 1.5 collective-permute-start.15
  110.0 4.3 %collective-permute-done.15 = bf16[128,768]{1,0:T(8,128)(2,1)S(1)} collective-permute-done((bf16[128,768]{1,0:T(8,128)(2,1)S(1)}, bf16[128,768]{1,0:T(8,128)(2,1)S(1)}, u32[]{:S(2)}, u32[]{:S(2)}) %collective-permute-start.15) | collective-permute-done | bytes 196640 | tf_op jit(solution)/shard_map/ppermute | solution.py:369
  114.7 4.8 %collective-permute-start.17 = (bf16[96,4096]{1,0:T(8,128)(2,1)S(1)}, bf16[96,4096]{1,0:T(8,128)(2,1)S(1)}, u32[]{:S(2)}, u32[]{:S(2)}) collective-permute-start(bf16[96,4096]{1,0:T(8,128)(2,1)S(1)} %get-tuple-element.124.refs_5_.refs_1_), channel_id=1, source_target_pairs={{0,8},{10,2},{4,12},{14,6},{8,16},{18,10},{12,20},{22,14},{16,24},... | collective-permute-start | bytes 2359304 | tf_op jit(solution)/shard_map/ppermute | solution.py:464
  119.5 5.6 %project.8 = (bf16[128,4096]{1,0:T(8,128)(2,1)S(1)}, bf16[128,4096]{1,0:T(8,128)(2,1)S(1)}) custom-call(s32[1]{0:T(128)} %bitcast.1.spot0_ref.refs_0_, s32[1]{0:T(128)} %bitcast.2.spot1_ref.refs_0_, bf16[128,768]{1,0:T(8,128)(2,1)S(1)} %get-tuple-element.100.refs_0_, bf16[128,768]{1,0:T(8,128)(2,1)S(1)} %collective-permute-done.3.refs_3_.refs_2_.refs_1_, ...), custom_call_target="tpu_custom_call" | custom-call | tf_op jit(solution)/shard_map/project/pallas_call | solution.py:38
  125.1 1.6 collective-permute-done.13.refs_1_
  127.0 1.3 collective-permute-start.16
  128.3 6.3 %collective-permute-done.17.refs_1_ = bf16[96,4096]{1,0:T(8,128)(2,1)S(1)} collective-permute-done((bf16[96,4096]{1,0:T(8,128)(2,1)S(1)}, bf16[96,4096]{1,0:T(8,128)(2,1)S(1)}, u32[]{:S(2)}, u32[]{:S(2)}) %collective-permute-start.17) | collective-permute-done | bytes 786464 | tf_op jit(solution)/shard_map/ppermute | solution.py:464
  134.9 3.3 %lower.7.refs_5_ = bf16[128,768]{1,0:T(8,128)(2,1)S(1)} custom-call(bf16[96,4096]{1,0:T(8,128)(2,1)S(1)} %get-tuple-element.120.refs_0_, bf16[96,4096]{1,0:T(8,128)(2,1)S(1)} %get-tuple-element.124.refs_5_.refs_1_, bf16[96,4096]{1,0:T(8,128)(2,1)S(1)} %get-tuple-element.126.refs_2_, bf16[96,4096]{1,0:T(8,128)(2,1)S(1)} %get-tuple-element.130.refs_3_.refs_5_, ...), custom_call_target="tpu_custom_call" | custom-call | tf_op jit(solution)/shard_map/lower/pallas_call | solution.py:38
  138.3 2.6 collective-permute-done.16.refs_1_
  141.2 1.7 collective-permute-start.20
  147.3 3.7 %collective-permute-start.19 = (bf16[96,4096]{1,0:T(8,128)(2,1)S(1)}, bf16[96,4096]{1,0:T(8,128)(2,1)S(1)}, u32[]{:S(2)}, u32[]{:S(2)}) collective-permute-start(bf16[96,4096]{1,0:T(8,128)(2,1)S(1)} %get-tuple-element.130.refs_3_.refs_5_), channel_id=1, source_target_pairs={{0,8},{10,2},{4,12},{14,6},{8,16},{18,10},{12,20},{22,14},{16,24},... | collective-permute-start | bytes 2359304 | tf_op jit(solution)/shard_map/ppermute | solution.py:464
  151.1 1.3 collective-permute-start.18
  152.5 14.0 %collective-permute-done.19.refs_1_ = bf16[96,4096]{1,0:T(8,128)(2,1)S(1)} collective-permute-done((bf16[96,4096]{1,0:T(8,128)(2,1)S(1)}, bf16[96,4096]{1,0:T(8,128)(2,1)S(1)}, u32[]{:S(2)}, u32[]{:S(2)}) %collective-permute-start.19) | collective-permute-done | bytes 786464 | tf_op jit(solution)/shard_map/ppermute | solution.py:464
  166.8 4.4 %collective-permute-start.22 = (bf16[96,4096]{1,0:T(8,128)(2,1)S(1)}, bf16[96,4096]{1,0:T(8,128)(2,1)S(1)}, u32[]{:S(2)}, u32[]{:S(2)}) collective-permute-start(bf16[96,4096]{1,0:T(8,128)(2,1)S(1)} %get-tuple-element.140.refs_4_.refs_1_), channel_id=1, source_target_pairs={{0,8},{10,2},{4,12},{14,6},{8,16},{18,10},{12,20},{22,14},{16,24},... | collective-permute-start | bytes 2359304 | tf_op jit(solution)/shard_map/ppermute | solution.py:464
  171.2 5.6 %project.9 = (bf16[128,4096]{1,0:T(8,128)(2,1)S(1)}, bf16[128,4096]{1,0:T(8,128)(2,1)S(1)}) custom-call(s32[1]{0:T(128)} %bitcast.1.spot0_ref.refs_0_, s32[1]{0:T(128)} %bitcast.2.spot1_ref.refs_0_, bf16[128,768]{1,0:T(8,128)(2,1)S(1)} %get-tuple-element.100.refs_0_, bf16[128,768]{1,0:T(8,128)(2,1)S(1)} %collective-permute-done.6.refs_4_.refs_2_.refs_1_, ...), custom_call_target="tpu_custom_call" | custom-call | tf_op jit(solution)/shard_map/project/pallas_call | solution.py:38
  178.5 7.6 %collective-permute-done.22.refs_1_ = bf16[96,4096]{1,0:T(8,128)(2,1)S(1)} collective-permute-done((bf16[96,4096]{1,0:T(8,128)(2,1)S(1)}, bf16[96,4096]{1,0:T(8,128)(2,1)S(1)}, u32[]{:S(2)}, u32[]{:S(2)}) %collective-permute-start.22) | collective-permute-done | bytes 786464 | tf_op jit(solution)/shard_map/ppermute | solution.py:464
  186.4 3.3 %lower.8.refs_5_ = bf16[128,768]{1,0:T(8,128)(2,1)S(1)} custom-call(bf16[96,4096]{1,0:T(8,128)(2,1)S(1)} %get-tuple-element.131.refs_0_, bf16[96,4096]{1,0:T(8,128)(2,1)S(1)} %get-tuple-element.140.refs_4_.refs_1_, bf16[96,4096]{1,0:T(8,128)(2,1)S(1)} %get-tuple-element.143.refs_2_, bf16[96,4096]{1,0:T(8,128)(2,1)S(1)} %get-tuple-element.147.refs_3_.refs_5_, ...), custom_call_target="tpu_custom_call" | custom-call | tf_op jit(solution)/shard_map/lower/pallas_call | solution.py:38
  189.8 1.3 collective-permute-done.21.refs_1_
  192.1 3.7 %collective-permute-start.24 = (bf16[96,4096]{1,0:T(8,128)(2,1)S(1)}, bf16[96,4096]{1,0:T(8,128)(2,1)S(1)}, u32[]{:S(2)}, u32[]{:S(2)}) collective-permute-start(bf16[96,4096]{1,0:T(8,128)(2,1)S(1)} %get-tuple-element.147.refs_3_.refs_5_), channel_id=1, source_target_pairs={{0,8},{10,2},{4,12},{14,6},{8,16},{18,10},{12,20},{22,14},{16,24},... | collective-permute-start | bytes 2359304 | tf_op jit(solution)/shard_map/ppermute | solution.py:464
  197.3 11.8 %collective-permute-done.24.refs_1_ = bf16[96,4096]{1,0:T(8,128)(2,1)S(1)} collective-permute-done((bf16[96,4096]{1,0:T(8,128)(2,1)S(1)}, bf16[96,4096]{1,0:T(8,128)(2,1)S(1)}, u32[]{:S(2)}, u32[]{:S(2)}) %collective-permute-start.24) | collective-permute-done | bytes 786464 | tf_op jit(solution)/shard_map/ppermute | solution.py:464
  209.5 4.4 %collective-permute-start.28 = (bf16[32,4096]{1,0:T(8,128)(2,1)S(1)}, bf16[32,4096]{1,0:T(8,128)(2,1)S(1)}, u32[]{:S(2)}, u32[]{:S(2)}) collective-permute-start(bf16[32,4096]{1,0:T(8,128)(2,1)S(1)} %get-tuple-element.159.refs_1_), channel_id=1, source_target_pairs={{0,8},{10,2},{4,12},{14,6},{8,16},{18,10},{12,20},{22,14},{16,24},... | collective-permute-start | bytes 786440 | tf_op jit(solution)/shard_map/ppermute | solution.py:464
  215.6 2.1 collective-permute-done.28.refs_1_
  217.8 3.3 %lower.9.refs_1_ = bf16[128,768]{1,0:T(8,128)(2,1)S(1)} custom-call(bf16[96,4096]{1,0:T(8,128)(2,1)S(1)} %get-tuple-element.148.refs_0_, bf16[32,4096]{1,0:T(8,128)(2,1)S(1)} %get-tuple-element.159.refs_1_, bf16[32,4096]{1,0:T(8,128)(2,1)S(1)} %get-tuple-element.158.refs_2_, bf16[32,4096]{1,0:T(8,128)(2,1)S(1)} %combine.51.refs_3_.refs_5_, ...), custom_call_target="tpu_custom_call" | custom-call | tf_op jit(solution)/shard_map/lower/pallas_call | solution.py:38
  221.1 1.8 collective-permute-done.27.refs_0_
  223.0 1.3 collective-permute-start.30
  224.3 4.0 %collective-permute-start.33 = (bf16[32,4096]{1,0:T(8,128)(2,1)S(1)}, bf16[32,4096]{1,0:T(8,128)(2,1)S(1)}, u32[]{:S(2)}, u32[]{:S(2)}) collective-permute-start(bf16[32,4096]{1,0:T(8,128)(2,1)S(1)} %combine.51.refs_3_.refs_5_), channel_id=1, source_target_pairs={{0,8},{10,2},{4,12},{14,6},{8,16},{18,10},{12,20},{22,14},{16,24},... | collective-permute-start | bytes 786440 | tf_op jit(solution)/shard_map/ppermute | solution.py:464
  229.7 4.7 %collective-permute-done.33.refs_0_ = bf16[32,4096]{1,0:T(8,128)(2,1)S(1)} collective-permute-done((bf16[32,4096]{1,0:T(8,128)(2,1)S(1)}, bf16[32,4096]{1,0:T(8,128)(2,1)S(1)}, u32[]{:S(2)}, u32[]{:S(2)}) %collective-permute-start.33) | collective-permute-done | bytes 262176 | tf_op jit(solution)/shard_map/ppermute | solution.py:464
  234.4 4.4 %collective-permute-start.34 = (bf16[32,4096]{1,0:T(8,128)(2,1)S(1)}, bf16[32,4096]{1,0:T(8,128)(2,1)S(1)}, u32[]{:S(2)}, u32[]{:S(2)}) collective-permute-start(bf16[32,4096]{1,0:T(8,128)(2,1)S(1)} %combine.54.refs_1_), channel_id=1, source_target_pairs={{0,8},{10,2},{4,12},{14,6},{8,16},{18,10},{12,20},{22,14},{16,24},... | collective-permute-start | bytes 786440 | tf_op jit(solution)/shard_map/ppermute | solution.py:464
  239.0 1.3 collective-permute-start.32
  241.4 2.6 collective-permute-done.34.refs_0_
  244.1 1.9 collective-permute-done.31.refs_1_.refs_6_.refs_2_
  246.0 3.3 %lower.10.refs_1_ = bf16[128,768]{1,0:T(8,128)(2,1)S(1)} custom-call(bf16[32,4096]{1,0:T(8,128)(2,1)S(1)} %get-tuple-element.161.refs_0_, bf16[32,4096]{1,0:T(8,128)(2,1)S(1)} %combine.54.refs_1_, bf16[32,4096]{1,0:T(8,128)(2,1)S(1)} %get-tuple-element.169.refs_2_, bf16[32,4096]{1,0:T(8,128)(2,1)S(1)} %combine.55.refs_3_.refs_5_, ...), custom_call_target="tpu_custom_call" | custom-call | tf_op jit(solution)/shard_map/lower/pallas_call | solution.py:38
  250.4 4.8 %collective-permute-start.37 = (bf16[32,4096]{1,0:T(8,128)(2,1)S(1)}, bf16[32,4096]{1,0:T(8,128)(2,1)S(1)}, u32[]{:S(2)}, u32[]{:S(2)}) collective-permute-start(bf16[32,4096]{1,0:T(8,128)(2,1)S(1)} %combine.55.refs_3_.refs_5_), channel_id=1, source_target_pairs={{0,8},{10,2},{4,12},{14,6},{8,16},{18,10},{12,20},{22,14},{16,24},... | collective-permute-start | bytes 786440 | tf_op jit(solution)/shard_map/ppermute | solution.py:464
  255.5 3.3 %collective-permute-done.37.refs_0_ = bf16[32,4096]{1,0:T(8,128)(2,1)S(1)} collective-permute-done((bf16[32,4096]{1,0:T(8,128)(2,1)S(1)}, bf16[32,4096]{1,0:T(8,128)(2,1)S(1)}, u32[]{:S(2)}, u32[]{:S(2)}) %collective-permute-start.37) | collective-permute-done | bytes 262176 | tf_op jit(solution)/shard_map/ppermute | solution.py:464
  258.8 3.5 %collective-permute-done.36.refs_7_.refs_3_ = bf16[128,768]{1,0:T(8,128)(2,1)S(1)} collective-permute-done((bf16[128,768]{1,0:T(8,128)(2,1)S(1)}, bf16[128,768]{1,0:T(8,128)(2,1)S(1)}, u32[]{:S(2)}, u32[]{:S(2)}) %collective-permute-start.36) | collective-permute-done | bytes 196640 | tf_op jit(solution)/shard_map/ppermute | solution.py:422
  262.3 3.3 %lower.11 = bf16[64,768]{1,0:T(8,128)(2,1)S(1)} custom-call(bf16[32,4096]{1,0:T(8,128)(2,1)S(1)} %get-tuple-element.176.refs_0_, bf16[32,4096]{1,0:T(8,128)(2,1)S(1)} %combine.57.refs_1_.refs_3_, bf16[4096,768]{1,0:T(8,128)(2,1)} %bitcast.31, bf16[32,4096]{1,0:T(8,128)(2,1)S(1)} %combine.57.refs_1_.refs_3_, ...), custom_call_target="tpu_custom_call" | custom-call | tf_op jit(solution)/shard_map/lower/pallas_call | solution.py:38
  267.0 3.3 %collective-permute-done.38 = bf16[64,768]{1,0:T(8,128)(2,1)S(1)} collective-permute-done((bf16[64,768]{1,0:T(8,128)(2,1)S(1)}, bf16[64,768]{1,0:T(8,128)(2,1)S(1)}, u32[]{:S(2)}, u32[]{:S(2)}) %collective-permute-start.38) | collective-permute-done | bytes 98336 | tf_op jit(solution)/shard_map/ppermute | solution.py:369
  270.4 3.0 %mix.1 = bf16[256,768]{1,0:T(8,128)(2,1)} custom-call(s32[2,256]{1,0:T(2,128)S(1)} %get-tuple-element.93.place_ref, f32[256,2]{1,0:T(8,128)S(1)} %copy.7.gate_ref, bf16[64,768]{1,0:T(8,128)(2,1)S(1)} %get-tuple-element.142.refs_5_.refs_4_.refs_0_, bf16[128,768]{1,0:T(8,128)(2,1)S(1)} %collective-permute-done.26.refs_3_.refs_5_.refs_1_, ...), custom_call_target="tpu_custom_call" | custom-call | tf_op jit(solution)/shard_map/mix/pallas_call | solution.py:38
  (88 shorter events, 20.1 us)
Async XLA Ops:
  0.0 1.0 copy-start
  1.0 0.7 copy-start.1
  7.4 16.3 %collective-permute-start.4 = (bf16[64,4096]{1,0:T(8,128)(2,1)S(1)}, bf16[64,4096]{1,0:T(8,128)(2,1)S(1)}, u32[]{:S(2)}, u32[]{:S(2)}) collective-permute-start(bf16[64,4096]{1,0:T(8,128)(2,1)S(1)} %combine.31), channel_id=1, source_target_pairs={{0,8},{10,2},{4,12},{14,6},{8,16},{18,10},{12,20},{22,14},{16,24},... | collective-permute-start | bytes 1572872 | tf_op jit(solution)/shard_map/ppermute | solution.py:464
  12.5 15.9 %collective-permute-start = (bf16[64,4096]{1,0:T(8,128)(2,1)S(1)}, bf16[64,4096]{1,0:T(8,128)(2,1)S(1)}, u32[]{:S(2)}, u32[]{:S(2)}) collective-permute-start(bf16[64,4096]{1,0:T(8,128)(2,1)S(1)} %get-tuple-element.99.refs_4_), channel_id=1, source_target_pairs={{8,0},{2,10},{12,4},{6,14},{16,8},{10,18},{20,12},{14,22},{24,16},... | collective-permute-start | bytes 1572872 | tf_op jit(solution)/shard_map/ppermute | solution.py:464
  13.8 1.5 collective-permute-start.1
  23.9 16.4 %collective-permute-start.5 = (bf16[64,4096]{1,0:T(8,128)(2,1)S(1)}, bf16[64,4096]{1,0:T(8,128)(2,1)S(1)}, u32[]{:S(2)}, u32[]{:S(2)}) collective-permute-start(bf16[64,4096]{1,0:T(8,128)(2,1)S(1)} %combine.32), channel_id=1, source_target_pairs={{0,8},{10,2},{4,12},{14,6},{8,16},{18,10},{12,20},{22,14},{16,24},... | collective-permute-start | bytes 1572872 | tf_op jit(solution)/shard_map/ppermute | solution.py:464
  28.6 22.0 %collective-permute-start.2 = (bf16[64,4096]{1,0:T(8,128)(2,1)S(1)}, bf16[64,4096]{1,0:T(8,128)(2,1)S(1)}, u32[]{:S(2)}, u32[]{:S(2)}) collective-permute-start(bf16[64,4096]{1,0:T(8,128)(2,1)S(1)} %combine.30), channel_id=1, source_target_pairs={{8,0},{2,10},{12,4},{6,14},{16,8},{10,18},{20,12},{14,22},{24,16},... | collective-permute-start | bytes 1572872 | tf_op jit(solution)/shard_map/ppermute | solution.py:464
  29.9 7.3 %collective-permute-start.3 = (bf16[128,768]{1,0:T(8,128)(2,1)S(1)}, bf16[128,768]{1,0:T(8,128)(2,1)S(1)}, u32[]{:S(2)}, u32[]{:S(2)}) collective-permute-start(bf16[128,768]{1,0:T(8,128)(2,1)S(1)} %get-tuple-element.104), channel_id=1, source_target_pairs={{0,4},{2,6},{4,0},{6,2},{1,5},{3,7},{5,1},{7,3},{8,12},{10,14},{12... | collective-permute-start | bytes 589832 | tf_op jit(solution)/shard_map/ppermute | solution.py:467
  31.3 7.7 %collective-permute-start.6 = (bf16[128,768]{1,0:T(8,128)(2,1)S(1)}, bf16[128,768]{1,0:T(8,128)(2,1)S(1)}, u32[]{:S(2)}, u32[]{:S(2)}) collective-permute-start(bf16[128,768]{1,0:T(8,128)(2,1)S(1)} %get-tuple-element.105), channel_id=1, source_target_pairs={{0,6},{2,4},{4,2},{6,0},{1,7},{3,5},{5,3},{7,1},{8,14},{10,12},{12... | collective-permute-start | bytes 589832 | tf_op jit(solution)/shard_map/ppermute | solution.py:467
  40.5 11.5 %collective-permute-start.8 = (bf16[64,4096]{1,0:T(8,128)(2,1)S(1)}, bf16[64,4096]{1,0:T(8,128)(2,1)S(1)}, u32[]{:S(2)}, u32[]{:S(2)}) collective-permute-start(bf16[64,4096]{1,0:T(8,128)(2,1)S(1)} %combine.33.refs_5_), channel_id=1, source_target_pairs={{0,8},{10,2},{4,12},{14,6},{8,16},{18,10},{12,20},{22,14},{16,24},... | collective-permute-start | bytes 1572872 | tf_op jit(solution)/shard_map/ppermute | solution.py:464
  50.8 11.1 %collective-permute-start.7 = (bf16[64,4096]{1,0:T(8,128)(2,1)S(1)}, bf16[64,4096]{1,0:T(8,128)(2,1)S(1)}, u32[]{:S(2)}, u32[]{:S(2)}) collective-permute-start(bf16[64,4096]{1,0:T(8,128)(2,1)S(1)} %combine.34), channel_id=1, source_target_pairs={{8,0},{2,10},{12,4},{6,14},{16,8},{10,18},{20,12},{14,22},{24,16},... | collective-permute-start | bytes 1572872 | tf_op jit(solution)/shard_map/ppermute | solution.py:464
  62.2 25.3 %collective-permute-start.9 = (bf16[96,4096]{1,0:T(8,128)(2,1)S(1)}, bf16[96,4096]{1,0:T(8,128)(2,1)S(1)}, u32[]{:S(2)}, u32[]{:S(2)}) collective-permute-start(bf16[96,4096]{1,0:T(8,128)(2,1)S(1)} %get-tuple-element.109.refs_0_), channel_id=1, source_target_pairs={{8,0},{2,10},{12,4},{6,14},{16,8},{10,18},{20,12},{14,22},{24,16},... | collective-permute-start | bytes 2359304 | tf_op jit(solution)/shard_map/ppermute | solution.py:464
  63.5 13.6 %collective-permute-start.10 = (bf16[64,4096]{1,0:T(8,128)(2,1)S(1)}, bf16[64,4096]{1,0:T(8,128)(2,1)S(1)}, u32[]{:S(2)}, u32[]{:S(2)}) collective-permute-start(bf16[64,4096]{1,0:T(8,128)(2,1)S(1)} %get-tuple-element.110), channel_id=1, source_target_pairs={{0,8},{10,2},{4,12},{14,6},{8,16},{18,10},{12,20},{22,14},{16,24},... | collective-permute-start | bytes 1572872 | tf_op jit(solution)/shard_map/ppermute | solution.py:464
  77.3 15.0 %collective-permute-start.12 = (bf16[96,4096]{1,0:T(8,128)(2,1)S(1)}, bf16[96,4096]{1,0:T(8,128)(2,1)S(1)}, u32[]{:S(2)}, u32[]{:S(2)}) collective-permute-start(bf16[96,4096]{1,0:T(8,128)(2,1)S(1)} %get-tuple-element.113.refs_5_.refs_1_), channel_id=1, source_target_pairs={{0,8},{10,2},{4,12},{14,6},{8,16},{18,10},{12,20},{22,14},{16,24},... | collective-permute-start | bytes 2359304 | tf_op jit(solution)/shard_map/ppermute | solution.py:464
  87.7 19.2 %collective-permute-start.11 = (bf16[96,4096]{1,0:T(8,128)(2,1)S(1)}, bf16[96,4096]{1,0:T(8,128)(2,1)S(1)}, u32[]{:S(2)}, u32[]{:S(2)}) collective-permute-start(bf16[96,4096]{1,0:T(8,128)(2,1)S(1)} %get-tuple-element.115.refs_2_), channel_id=1, source_target_pairs={{8,0},{2,10},{12,4},{6,14},{16,8},{10,18},{20,12},{14,22},{24,16},... | collective-permute-start | bytes 2359304 | tf_op jit(solution)/shard_map/ppermute | solution.py:464
  92.7 21.7 %collective-permute-start.14 = (bf16[96,4096]{1,0:T(8,128)(2,1)S(1)}, bf16[96,4096]{1,0:T(8,128)(2,1)S(1)}, u32[]{:S(2)}, u32[]{:S(2)}) collective-permute-start(bf16[96,4096]{1,0:T(8,128)(2,1)S(1)} %get-tuple-element.119.refs_3_.refs_5_), channel_id=1, source_target_pairs={{0,8},{10,2},{4,12},{14,6},{8,16},{18,10},{12,20},{22,14},{16,24},... | collective-permute-start | bytes 2359304 | tf_op jit(solution)/shard_map/ppermute | solution.py:464
  107.2 19.5 %collective-permute-start.13 = (bf16[96,4096]{1,0:T(8,128)(2,1)S(1)}, bf16[96,4096]{1,0:T(8,128)(2,1)S(1)}, u32[]{:S(2)}, u32[]{:S(2)}) collective-permute-start(bf16[96,4096]{1,0:T(8,128)(2,1)S(1)} %get-tuple-element.120.refs_0_), channel_id=1, source_target_pairs={{8,0},{2,10},{12,4},{6,14},{16,8},{10,18},{20,12},{14,22},{24,16},... | collective-permute-start | bytes 2359304 | tf_op jit(solution)/shard_map/ppermute | solution.py:464
  108.5 5.7 %collective-permute-start.15 = (bf16[128,768]{1,0:T(8,128)(2,1)S(1)}, bf16[128,768]{1,0:T(8,128)(2,1)S(1)}, u32[]{:S(2)}, u32[]{:S(2)}) collective-permute-start(bf16[128,768]{1,0:T(8,128)(2,1)S(1)} %get-tuple-element.122), channel_id=1, source_target_pairs={{0,1},{1,0},{2,3},{3,2},{4,5},{5,4},{6,7},{7,6},{8,9},{9,8},{10,11... | collective-permute-start | bytes 589832 | tf_op jit(solution)/shard_map/ppermute | solution.py:369
  114.7 19.9 %collective-permute-start.17 = (bf16[96,4096]{1,0:T(8,128)(2,1)S(1)}, bf16[96,4096]{1,0:T(8,128)(2,1)S(1)}, u32[]{:S(2)}, u32[]{:S(2)}) collective-permute-start(bf16[96,4096]{1,0:T(8,128)(2,1)S(1)} %get-tuple-element.124.refs_5_.refs_1_), channel_id=1, source_target_pairs={{0,8},{10,2},{4,12},{14,6},{8,16},{18,10},{12,20},{22,14},{16,24},... | collective-permute-start | bytes 2359304 | tf_op jit(solution)/shard_map/ppermute | solution.py:464
  127.0 13.9 %collective-permute-start.16 = (bf16[96,4096]{1,0:T(8,128)(2,1)S(1)}, bf16[96,4096]{1,0:T(8,128)(2,1)S(1)}, u32[]{:S(2)}, u32[]{:S(2)}) collective-permute-start(bf16[96,4096]{1,0:T(8,128)(2,1)S(1)} %get-tuple-element.126.refs_2_), channel_id=1, source_target_pairs={{8,0},{2,10},{12,4},{6,14},{16,8},{10,18},{20,12},{14,22},{24,16},... | collective-permute-start | bytes 2359304 | tf_op jit(solution)/shard_map/ppermute | solution.py:464
  141.2 11.1 %collective-permute-start.20 = (bf16[128,768]{1,0:T(8,128)(2,1)S(1)}, bf16[128,768]{1,0:T(8,128)(2,1)S(1)}, u32[]{:S(2)}, u32[]{:S(2)}) collective-permute-start(bf16[128,768]{1,0:T(8,128)(2,1)S(1)} %get-tuple-element.133), channel_id=1, source_target_pairs={{0,1},{1,0},{2,3},{3,2},{4,5},{5,4},{6,7},{7,6},{8,9},{9,8},{10,11... | collective-permute-start | bytes 589832 | tf_op jit(solution)/shard_map/ppermute | solution.py:369
  147.3 19.2 %collective-permute-start.19 = (bf16[96,4096]{1,0:T(8,128)(2,1)S(1)}, bf16[96,4096]{1,0:T(8,128)(2,1)S(1)}, u32[]{:S(2)}, u32[]{:S(2)}) collective-permute-start(bf16[96,4096]{1,0:T(8,128)(2,1)S(1)} %get-tuple-element.130.refs_3_.refs_5_), channel_id=1, source_target_pairs={{0,8},{10,2},{4,12},{14,6},{8,16},{18,10},{12,20},{22,14},{16,24},... | collective-permute-start | bytes 2359304 | tf_op jit(solution)/shard_map/ppermute | solution.py:464
  151.1 25.8 %collective-permute-start.18 = (bf16[96,4096]{1,0:T(8,128)(2,1)S(1)}, bf16[96,4096]{1,0:T(8,128)(2,1)S(1)}, u32[]{:S(2)}, u32[]{:S(2)}) collective-permute-start(bf16[96,4096]{1,0:T(8,128)(2,1)S(1)} %get-tuple-element.131.refs_0_), channel_id=1, source_target_pairs={{8,0},{2,10},{12,4},{6,14},{16,8},{10,18},{20,12},{14,22},{24,16},... | collective-permute-start | bytes 2359304 | tf_op jit(solution)/shard_map/ppermute | solution.py:464
  166.8 19.3 %collective-permute-start.22 = (bf16[96,4096]{1,0:T(8,128)(2,1)S(1)}, bf16[96,4096]{1,0:T(8,128)(2,1)S(1)}, u32[]{:S(2)}, u32[]{:S(2)}) collective-permute-start(bf16[96,4096]{1,0:T(8,128)(2,1)S(1)} %get-tuple-element.140.refs_4_.refs_1_), channel_id=1, source_target_pairs={{0,8},{10,2},{4,12},{14,6},{8,16},{18,10},{12,20},{22,14},{16,24},... | collective-permute-start | bytes 2359304 | tf_op jit(solution)/shard_map/ppermute | solution.py:464
  177.2 13.9 %collective-permute-start.21 = (bf16[96,4096]{1,0:T(8,128)(2,1)S(1)}, bf16[96,4096]{1,0:T(8,128)(2,1)S(1)}, u32[]{:S(2)}, u32[]{:S(2)}) collective-permute-start(bf16[96,4096]{1,0:T(8,128)(2,1)S(1)} %get-tuple-element.143.refs_2_), channel_id=1, source_target_pairs={{8,0},{2,10},{12,4},{6,14},{16,8},{10,18},{20,12},{14,22},{24,16},... | collective-permute-start | bytes 2359304 | tf_op jit(solution)/shard_map/ppermute | solution.py:464
  191.4 5.7 %collective-permute-start.25 = (bf16[128,768]{1,0:T(8,128)(2,1)S(1)}, bf16[128,768]{1,0:T(8,128)(2,1)S(1)}, u32[]{:S(2)}, u32[]{:S(2)}) collective-permute-start(bf16[128,768]{1,0:T(8,128)(2,1)S(1)} %get-tuple-element.150), channel_id=1, source_target_pairs={{0,1},{1,0},{2,3},{3,2},{4,5},{5,4},{6,7},{7,6},{8,9},{9,8},{10,11... | collective-permute-start | bytes 589832 | tf_op jit(solution)/shard_map/ppermute | solution.py:369
  192.1 17.0 %collective-permute-start.24 = (bf16[96,4096]{1,0:T(8,128)(2,1)S(1)}, bf16[96,4096]{1,0:T(8,128)(2,1)S(1)}, u32[]{:S(2)}, u32[]{:S(2)}) collective-permute-start(bf16[96,4096]{1,0:T(8,128)(2,1)S(1)} %get-tuple-element.147.refs_3_.refs_5_), channel_id=1, source_target_pairs={{0,8},{10,2},{4,12},{14,6},{8,16},{18,10},{12,20},{22,14},{16,24},... | collective-permute-start | bytes 2359304 | tf_op jit(solution)/shard_map/ppermute | solution.py:464
  195.8 18.0 %collective-permute-start.23 = (bf16[96,4096]{1,0:T(8,128)(2,1)S(1)}, bf16[96,4096]{1,0:T(8,128)(2,1)S(1)}, u32[]{:S(2)}, u32[]{:S(2)}) collective-permute-start(bf16[96,4096]{1,0:T(8,128)(2,1)S(1)} %get-tuple-element.148.refs_0_), channel_id=1, source_target_pairs={{8,0},{2,10},{12,4},{6,14},{16,8},{10,18},{20,12},{14,22},{24,16},... | collective-permute-start | bytes 2359304 | tf_op jit(solution)/shard_map/ppermute | solution.py:464
  209.5 8.3 %collective-permute-start.28 = (bf16[32,4096]{1,0:T(8,128)(2,1)S(1)}, bf16[32,4096]{1,0:T(8,128)(2,1)S(1)}, u32[]{:S(2)}, u32[]{:S(2)}) collective-permute-start(bf16[32,4096]{1,0:T(8,128)(2,1)S(1)} %get-tuple-element.159.refs_1_), channel_id=1, source_target_pairs={{0,8},{10,2},{4,12},{14,6},{8,16},{18,10},{12,20},{22,14},{16,24},... | collective-permute-start | bytes 786440 | tf_op jit(solution)/shard_map/ppermute | solution.py:464
  214.2 8.7 %collective-permute-start.27 = (bf16[32,4096]{1,0:T(8,128)(2,1)S(1)}, bf16[32,4096]{1,0:T(8,128)(2,1)S(1)}, u32[]{:S(2)}, u32[]{:S(2)}) collective-permute-start(bf16[32,4096]{1,0:T(8,128)(2,1)S(1)} %get-tuple-element.158.refs_2_), channel_id=1, source_target_pairs={{8,0},{2,10},{12,4},{6,14},{16,8},{10,18},{20,12},{14,22},{24,16},... | collective-permute-start | bytes 786440 | tf_op jit(solution)/shard_map/ppermute | solution.py:464
  215.5 2.2 collective-permute-start.26
  223.0 6.6 %collective-permute-start.30 = (bf16[128,768]{1,0:T(8,128)(2,1)S(1)}, bf16[128,768]{1,0:T(8,128)(2,1)S(1)}, u32[]{:S(2)}, u32[]{:S(2)}) collective-permute-start(bf16[128,768]{1,0:T(8,128)(2,1)S(1)} %get-tuple-element.162), channel_id=1, source_target_pairs={{0,1},{1,0},{2,3},{3,2},{4,5},{5,4},{6,7},{7,6},{8,9},{9,8},{10,11... | collective-permute-start | bytes 589832 | tf_op jit(solution)/shard_map/ppermute | solution.py:369
  224.3 10.0 %collective-permute-start.33 = (bf16[32,4096]{1,0:T(8,128)(2,1)S(1)}, bf16[32,4096]{1,0:T(8,128)(2,1)S(1)}, u32[]{:S(2)}, u32[]{:S(2)}) collective-permute-start(bf16[32,4096]{1,0:T(8,128)(2,1)S(1)} %combine.51.refs_3_.refs_5_), channel_id=1, source_target_pairs={{0,8},{10,2},{4,12},{14,6},{8,16},{18,10},{12,20},{22,14},{16,24},... | collective-permute-start | bytes 786440 | tf_op jit(solution)/shard_map/ppermute | solution.py:464
  228.3 10.6 %collective-permute-start.29 = (bf16[32,4096]{1,0:T(8,128)(2,1)S(1)}, bf16[32,4096]{1,0:T(8,128)(2,1)S(1)}, u32[]{:S(2)}, u32[]{:S(2)}) collective-permute-start(bf16[32,4096]{1,0:T(8,128)(2,1)S(1)} %get-tuple-element.161.refs_0_), channel_id=1, source_target_pairs={{8,0},{2,10},{12,4},{6,14},{16,8},{10,18},{20,12},{14,22},{24,16},... | collective-permute-start | bytes 786440 | tf_op jit(solution)/shard_map/ppermute | solution.py:464
  234.4 9.7 %collective-permute-start.34 = (bf16[32,4096]{1,0:T(8,128)(2,1)S(1)}, bf16[32,4096]{1,0:T(8,128)(2,1)S(1)}, u32[]{:S(2)}, u32[]{:S(2)}) collective-permute-start(bf16[32,4096]{1,0:T(8,128)(2,1)S(1)} %combine.54.refs_1_), channel_id=1, source_target_pairs={{0,8},{10,2},{4,12},{14,6},{8,16},{18,10},{12,20},{22,14},{16,24},... | collective-permute-start | bytes 786440 | tf_op jit(solution)/shard_map/ppermute | solution.py:464
  239.0 10.4 %collective-permute-start.32 = (bf16[32,4096]{1,0:T(8,128)(2,1)S(1)}, bf16[32,4096]{1,0:T(8,128)(2,1)S(1)}, u32[]{:S(2)}, u32[]{:S(2)}) collective-permute-start(bf16[32,4096]{1,0:T(8,128)(2,1)S(1)} %get-tuple-element.169.refs_2_), channel_id=1, source_target_pairs={{8,0},{2,10},{12,4},{6,14},{16,8},{10,18},{20,12},{14,22},{24,16},... | collective-permute-start | bytes 786440 | tf_op jit(solution)/shard_map/ppermute | solution.py:464
  240.3 5.7 %collective-permute-start.31 = (bf16[128,768]{1,0:T(8,128)(2,1)S(1)}, bf16[128,768]{1,0:T(8,128)(2,1)S(1)}, u32[]{:S(2)}, u32[]{:S(2)}) collective-permute-start(bf16[128,768]{1,0:T(8,128)(2,1)S(1)} %get-tuple-element.168), channel_id=1, source_target_pairs={{0,4},{2,6},{4,0},{6,2},{1,5},{3,7},{5,1},{7,3},{8,12},{10,14},{12... | collective-permute-start | bytes 589832 | tf_op jit(solution)/shard_map/ppermute | solution.py:422
  249.4 17.5 %copy-start.2 = (f32[256,2]{0,1:T(2,128)S(1)}, f32[256,2]{0,1:T(2,128)}, u32[]{:S(2)}) copy-start(f32[256,2]{0,1:T(2,128)} %param.8) | copy-start | bytes 6148
  249.5 5.7 %collective-permute-start.35 = (bf16[128,768]{1,0:T(8,128)(2,1)S(1)}, bf16[128,768]{1,0:T(8,128)(2,1)S(1)}, u32[]{:S(2)}, u32[]{:S(2)}) collective-permute-start(bf16[128,768]{1,0:T(8,128)(2,1)S(1)} %get-tuple-element.170), channel_id=1, source_target_pairs={{0,1},{1,0},{2,3},{3,2},{4,5},{5,4},{6,7},{7,6},{8,9},{9,8},{10,11... | collective-permute-start | bytes 589832 | tf_op jit(solution)/shard_map/ppermute | solution.py:369
  250.4 8.4 %collective-permute-start.37 = (bf16[32,4096]{1,0:T(8,128)(2,1)S(1)}, bf16[32,4096]{1,0:T(8,128)(2,1)S(1)}, u32[]{:S(2)}, u32[]{:S(2)}) collective-permute-start(bf16[32,4096]{1,0:T(8,128)(2,1)S(1)} %combine.55.refs_3_.refs_5_), channel_id=1, source_target_pairs={{0,8},{10,2},{4,12},{14,6},{8,16},{18,10},{12,20},{22,14},{16,24},... | collective-permute-start | bytes 786440 | tf_op jit(solution)/shard_map/ppermute | solution.py:464
  255.4 6.9 %collective-permute-start.36 = (bf16[128,768]{1,0:T(8,128)(2,1)S(1)}, bf16[128,768]{1,0:T(8,128)(2,1)S(1)}, u32[]{:S(2)}, u32[]{:S(2)}) collective-permute-start(bf16[128,768]{1,0:T(8,128)(2,1)S(1)} %pad_maximum_fusion.2), channel_id=1, source_target_pairs={{0,6},{2,4},{4,2},{6,0},{1,7},{3,5},{5,3},{7,1},{8,14},{10,12},{12... | collective-permute-start | bytes 589832 | tf_op jit(solution)/shard_map/ppermute | solution.py:422
  265.6 4.7 %collective-permute-start.38 = (bf16[64,768]{1,0:T(8,128)(2,1)S(1)}, bf16[64,768]{1,0:T(8,128)(2,1)S(1)}, u32[]{:S(2)}, u32[]{:S(2)}) collective-permute-start(bf16[64,768]{1,0:T(8,128)(2,1)S(1)} %lower.11), channel_id=1, source_target_pairs={{0,1},{1,0},{2,3},{3,2},{4,5},{5,4},{6,7},{7,6},{8,9},{9,8},{10,11... | collective-permute-start | bytes 294920 | tf_op jit(solution)/shard_map/ppermute | solution.py:369

commit v5 on v3

--- a/solution.py
+++ b/solution.py
@@ -298,6 +298,31 @@
         ],
         grant=48,
     )[0]
+
+
+def mix(m, experts, half, places, gates, spans, parts):
+    n, width = gates.shape[0], parts[0].shape[1]
+
+    def body(place_ref, gate_ref, *refs):
+        total = jnp.zeros((n, width), F32)
+        for k in range(2):
+            y = jnp.zeros((n, width), F32)
+            for (j, start, stop, i), part_ref in zip(spans, refs):
+                rows = (stop - start) * m
+                for f in range(2):
+                    rank = lax.broadcasted_iota(I32, (rows, n), 0) + (i * m + f * half)
+                    chosen = one_hot(rank * experts + j == place_ref[k : k + 1, :])
+                    y += lax.dot_general(
+                        chosen,
+                        part_ref[f * rows : (f + 1) * rows, :],
+                        (((0,), (0,)), ((), ())),
+                        preferred_element_type=F32,
+                    )
+            total += gate_ref[:, k : k + 1] * y
+        refs[-1][...] = total.astype(BF16)
+
+    specs = [WHOLE] * (2 + len(parts))
+    return call(body, "mix", [array(n, width)], (places, gates, *parts), specs)[0]
 
 
 def local(tokens, route_ids, gates, w_gate, w_up, w_down):
@@ -419,11 +444,13 @@
                 got[f] = lax.ppermute(message, ("dp", "expert"), flows[f])
             for j, value in enumerate(relayed, 1):
                 rows.append(lax.ppermute(value, "expert", [(a, a ^ j) for a in range(experts)]))
+            if s == 1 and f == 1:
+                ties += rows[2:]
             if carries:
                 held[o][s - first] = message
             if f == (0 if s else 1) and s + 1 < sums_end and s + 1 not in partial:
                 rounds = [r for r in (s + 1, s + 2) if r < sums_end]
-                wait = [message] if s else [message, *rows[1:]]
+                wait = [message]
                 g, u = project(m, spot, rows, [sources(r) for r in rounds], weights, wait)
                 for k, r in enumerate(rounds):
                     partial[r] = (g, u, 2 * m * k)
@@ -439,18 +466,8 @@
                 for k, q in enumerate(ready):
                     outs[q] = result[2 * m * k : 2 * m * (k + 1)]
 
-    yields = [jnp.zeros((n, width), F32), jnp.zeros((n, width), F32)]
     deliver()
-    for (j, start, stop, i), part in zip(spans, parts):
-        ranks = np.arange((stop - start) * m, dtype=np.int32) + i * m
-        label = jnp.asarray(np.concatenate([ranks, ranks + half]) * experts + j)
-        for k in range(2):
-            chosen = (label[:, None] == places[k][None, :]).astype(BF16)
-            yields[k] += lax.dot_general(
-                chosen, part, (((0,), (0,)), ((), ())), preferred_element_type=F32
-            )
-    mixed = gates[:, 0:1] * yields[0] + gates[:, 1:2] * yields[1]
-    return mixed.astype(BF16)
+    return mix(m, experts, half, places, gates, spans, parts)
 
 
 def solution(mesh):

time: 261 us -> 262 us (level)
  matrix products: 4.5 us -> 0 us
  waiting for transfers between devices: 95.2 us -> 98.6 us
  Pallas kernels: 59.8 us -> 62.8 us
    ppermute x27, waiting for transfers between devices: 72.5 us -> 81.5 us  [local(): got[f] = lax.ppermute(message, ('dp', 'expert'), flows[f])]
    ppermute x6, waiting for transfers between devices: 11.5 us -> 5.05 us  [across(): other = lax.ppermute(part, 'tensor', [(0, 1), (1, 0)])]
    dot_general x10 -> x0, matrix products: 4.5 us -> none  [local(): lax.dot_general(chosen, part, (((0,), (0,)), ((), ())), preferred_element...]
    pallas_call x41 -> x42, Pallas kernels: 59.8 us -> 62.8 us  [call(): pl.pallas_call(body, name=name, out_shape=shapes, in_specs=specs, out_spe...]
  transfers between devices with their start and end apart: 39 -> 39, of which waited for: 24 -> 24; matrix products, arithmetic and copies ran while one was open for 1% -> 0% of each run, Pallas kernels for 18% -> 18%
where the time goes in v5:
time: 262 us; the launch traced here: 261 us
  waiting for transfers between devices  98.6 us (38%)
  starting transfers between devices  91.8 us (35%)
  Pallas kernels  62.8 us (24%)
  between operations  4.45 us (2%)
    ppermute x27, starting transfers between devices, local(): got[f] = lax.ppermute(message, ('dp', 'expert'), flows[f])  81.6 us
    ppermute x27, waiting for transfers between devices, local(): got[f] = lax.ppermute(message, ('dp', 'expert'), flows[f])  81.5 us
    pallas_call x42, Pallas kernels, call(): pl.pallas_call(body, name=name, out_shape=shapes, in_specs=specs, out_spe...  62.8 us
    ppermute x3, waiting for transfers between devices, local(): lax.ppermute(value, 'expert', [(a, a ^ j) for a in range(experts)])  8.92 us
    ppermute x6, starting transfers between devices, across(): other = lax.ppermute(part, 'tensor', [(0, 1), (1, 0)])  7.12 us
  transfers between devices with their start and end apart: 39, of which 24 were waited for; matrix products, arithmetic and copies ran while one was open for 0% of the time, Pallas kernels for 18%

profile of v5, /device:TPU:0, one launch (start us, length us, event | category | flops | bytes accessed | tf_op | source)
XLA Modules:
  0.0 260.6 jit_solution(274538326196394085)
XLA Ops:
  1.7 5.7 %begin.1 = (s32[2,256]{1,0:T(2,128)S(1)}, bf16[128,768]{1,0:T(8,128)(2,1)S(1)}, bf16[128,768]{1,0:T(8,128)(2,1)S(1)}, bf16[128,768]{1,0:T(8,128)(2,1)S(1)}, bf16...) custom-call(s32[1]{0:T(128)} %bitcast.e_ref, ...), custom_call_target="tpu_custom_call" | custom-call | tf_op jit(solution)/shard_map/begin/pallas_call | solution.py:38
  7.4 5.0 %collective-permute-start.4 = (bf16[64,4096]{1,0:T(8,128)(2,1)S(1)}, bf16[64,4096]{1,0:T(8,128)(2,1)S(1)}, u32[]{:S(2)}, u32[]{:S(2)}) collective-permute-start(bf16[64,4096]{1,0:T(8,128)(2,1)S(1)} %combine.31), channel_id=1, source_target_pairs={{0,8},{10,2},{4,12},{14,6},{8,16},{18,10},{12,20},{22,14},{16,24},... | collective-permute-start | bytes 1572872 | tf_op jit(solution)/shard_map/ppermute | solution.py:444
  12.5 1.3 collective-permute-start
  15.3 5.6 %project.5 = (bf16[128,4096]{1,0:T(8,128)(2,1)S(1)}, bf16[128,4096]{1,0:T(8,128)(2,1)S(1)}) custom-call(s32[1]{0:T(128)} %bitcast.1.spot0_ref.refs_0_, s32[1]{0:T(128)} %bitcast.2.spot1_ref.refs_0_, bf16[128,768]{1,0:T(8,128)(2,1)S(1)} %get-tuple-element.90.refs_0_, bf16[128,768]{1,0:T(8,128)(2,1)S(1)} %collective-permute-done.1.refs_1_.refs_0_, ...), custom_call_target="tpu_custom_call" | custom-call | tf_op jit(solution)/shard_map/project/pallas_call | solution.py:38
  20.9 2.9 %collective-permute-done.4.refs_0_ = bf16[64,4096]{1,0:T(8,128)(2,1)S(1)} collective-permute-done((bf16[64,4096]{1,0:T(8,128)(2,1)S(1)}, bf16[64,4096]{1,0:T(8,128)(2,1)S(1)}, u32[]{:S(2)}, u32[]{:S(2)}) %collective-permute-start.4) | collective-permute-done | bytes 524320 | tf_op jit(solution)/shard_map/ppermute | solution.py:444
  23.9 4.4 %collective-permute-start.5 = (bf16[64,4096]{1,0:T(8,128)(2,1)S(1)}, bf16[64,4096]{1,0:T(8,128)(2,1)S(1)}, u32[]{:S(2)}, u32[]{:S(2)}) collective-permute-start(bf16[64,4096]{1,0:T(8,128)(2,1)S(1)} %combine.32), channel_id=1, source_target_pairs={{0,8},{10,2},{4,12},{14,6},{8,16},{18,10},{12,20},{22,14},{16,24},... | collective-permute-start | bytes 1572872 | tf_op jit(solution)/shard_map/ppermute | solution.py:444
  28.6 1.3 collective-permute-start.2
  29.9 1.4 collective-permute-start.3
  31.3 5.9 %collective-permute-done.3.refs_3_.refs_2_.refs_1_ = bf16[128,768]{1,0:T(8,128)(2,1)S(1)} collective-permute-done((bf16[128,768]{1,0:T(8,128)(2,1)S(1)}, bf16[128,768]{1,0:T(8,128)(2,1)S(1)}, u32[]{:S(2)}, u32[]{:S(2)}) %collective-permute-start.3) | collective-permute-done | bytes 196640 | tf_op jit(solution)/shard_map/ppermute | solution.py:446
  37.1 1.8 collective-permute-done.6.refs_4_.refs_2_.refs_1_
  38.9 1.5 collective-permute-done.5.refs_0_
  40.5 4.4 %collective-permute-start.8 = (bf16[64,4096]{1,0:T(8,128)(2,1)S(1)}, bf16[64,4096]{1,0:T(8,128)(2,1)S(1)}, u32[]{:S(2)}, u32[]{:S(2)}) collective-permute-start(bf16[64,4096]{1,0:T(8,128)(2,1)S(1)} %combine.33.refs_5_), channel_id=1, source_target_pairs={{0,8},{10,2},{4,12},{14,6},{8,16},{18,10},{12,20},{22,14},{16,24},... | collective-permute-start | bytes 1572872 | tf_op jit(solution)/shard_map/ppermute | solution.py:444
  45.0 5.6 %project.6 = (bf16[128,4096]{1,0:T(8,128)(2,1)S(1)}, bf16[128,4096]{1,0:T(8,128)(2,1)S(1)}) custom-call(s32[1]{0:T(128)} %bitcast.1.spot0_ref.refs_0_, s32[1]{0:T(128)} %bitcast.2.spot1_ref.refs_0_, bf16[128,768]{1,0:T(8,128)(2,1)S(1)} %get-tuple-element.90.refs_0_, bf16[128,768]{1,0:T(8,128)(2,1)S(1)} %collective-permute-done.1.refs_1_.refs_0_, ...), custom_call_target="tpu_custom_call" | custom-call | tf_op jit(solution)/shard_map/project/pallas_call | solution.py:38
  50.8 1.3 collective-permute-start.7
  52.4 4.6 %collective-permute-start.9 = (bf16[64,4096]{1,0:T(8,128)(2,1)S(1)}, bf16[64,4096]{1,0:T(8,128)(2,1)S(1)}, u32[]{:S(2)}, u32[]{:S(2)}) collective-permute-start(bf16[64,4096]{1,0:T(8,128)(2,1)S(1)} %get-tuple-element.100), channel_id=1, source_target_pairs={{0,8},{10,2},{4,12},{14,6},{8,16},{18,10},{12,20},{22,14},{16,24},... | collective-permute-start | bytes 1572872 | tf_op jit(solution)/shard_map/ppermute | solution.py:444
  57.0 9.8 %collective-permute-done.7.refs_1_ = bf16[64,4096]{1,0:T(8,128)(2,1)S(1)} collective-permute-done((bf16[64,4096]{1,0:T(8,128)(2,1)S(1)}, bf16[64,4096]{1,0:T(8,128)(2,1)S(1)}, u32[]{:S(2)}, u32[]{:S(2)}) %collective-permute-start.7) | collective-permute-done | bytes 524320 | tf_op jit(solution)/shard_map/ppermute | solution.py:444
  67.1 1.3 collective-permute-start.10
  68.7 4.6 %collective-permute-start.11 = (bf16[96,4096]{1,0:T(8,128)(2,1)S(1)}, bf16[96,4096]{1,0:T(8,128)(2,1)S(1)}, u32[]{:S(2)}, u32[]{:S(2)}) collective-permute-start(bf16[96,4096]{1,0:T(8,128)(2,1)S(1)} %get-tuple-element.102.refs_5_.refs_1_), channel_id=1, source_target_pairs={{0,8},{10,2},{4,12},{14,6},{8,16},{18,10},{12,20},{22,14},{16,24},... | collective-permute-start | bytes 2359304 | tf_op jit(solution)/shard_map/ppermute | solution.py:444
  73.3 5.6 %project.7 = (bf16[128,4096]{1,0:T(8,128)(2,1)S(1)}, bf16[128,4096]{1,0:T(8,128)(2,1)S(1)}) custom-call(s32[1]{0:T(128)} %bitcast.1.spot0_ref.refs_0_, s32[1]{0:T(128)} %bitcast.2.spot1_ref.refs_0_, bf16[128,768]{1,0:T(8,128)(2,1)S(1)} %collective-permute-done.1.refs_1_.refs_0_, bf16[128,768]{1,0:T(8,128)(2,1)S(1)} %collective-permute-done.3.refs_3_.refs_2_.refs_1_, ...), custom_call_target="tpu_custom_call" | custom-call | tf_op jit(solution)/shard_map/project/pallas_call | solution.py:38
  79.0 10.0 %collective-permute-done.10.refs_1_ = bf16[96,4096]{1,0:T(8,128)(2,1)S(1)} collective-permute-done((bf16[96,4096]{1,0:T(8,128)(2,1)S(1)}, bf16[96,4096]{1,0:T(8,128)(2,1)S(1)}, u32[]{:S(2)}, u32[]{:S(2)}) %collective-permute-start.10) | collective-permute-done | bytes 786464 | tf_op jit(solution)/shard_map/ppermute | solution.py:444
  89.2 1.3 collective-permute-start.13
  90.9 4.6 %collective-permute-start.14 = (bf16[96,4096]{1,0:T(8,128)(2,1)S(1)}, bf16[96,4096]{1,0:T(8,128)(2,1)S(1)}, u32[]{:S(2)}, u32[]{:S(2)}) collective-permute-start(bf16[96,4096]{1,0:T(8,128)(2,1)S(1)} %get-tuple-element.108.refs_3_.refs_5_), channel_id=1, source_target_pairs={{0,8},{10,2},{4,12},{14,6},{8,16},{18,10},{12,20},{22,14},{16,24},... | collective-permute-start | bytes 2359304 | tf_op jit(solution)/shard_map/ppermute | solution.py:444
  95.5 3.3 %lower.6.refs_5_ = bf16[128,768]{1,0:T(8,128)(2,1)S(1)} custom-call(bf16[96,4096]{1,0:T(8,128)(2,1)S(1)} %get-tuple-element.99.refs_0_, bf16[96,4096]{1,0:T(8,128)(2,1)S(1)} %get-tuple-element.102.refs_5_.refs_1_, bf16[96,4096]{1,0:T(8,128)(2,1)S(1)} %get-tuple-element.105.refs_2_, bf16[96,4096]{1,0:T(8,128)(2,1)S(1)} %get-tuple-element.108.refs_3_.refs_5_, ...), custom_call_target="tpu_custom_call" | custom-call | tf_op jit(solution)/shard_map/lower/pallas_call | solution.py:38
  98.8 11.5 %collective-permute-done.13.refs_1_ = bf16[96,4096]{1,0:T(8,128)(2,1)S(1)} collective-permute-done((bf16[96,4096]{1,0:T(8,128)(2,1)S(1)}, bf16[96,4096]{1,0:T(8,128)(2,1)S(1)}, u32[]{:S(2)}, u32[]{:S(2)}) %collective-permute-start.13) | collective-permute-done | bytes 786464 | tf_op jit(solution)/shard_map/ppermute | solution.py:444
  110.6 1.3 collective-permute-start.15
  112.2 4.8 %collective-permute-start.16 = (bf16[96,4096]{1,0:T(8,128)(2,1)S(1)}, bf16[96,4096]{1,0:T(8,128)(2,1)S(1)}, u32[]{:S(2)}, u32[]{:S(2)}) collective-permute-start(bf16[96,4096]{1,0:T(8,128)(2,1)S(1)} %get-tuple-element.112.refs_5_.refs_1_), channel_id=1, source_target_pairs={{0,8},{10,2},{4,12},{14,6},{8,16},{18,10},{12,20},{22,14},{16,24},... | collective-permute-start | bytes 2359304 | tf_op jit(solution)/shard_map/ppermute | solution.py:444
  117.0 5.6 %project.8 = (bf16[128,4096]{1,0:T(8,128)(2,1)S(1)}, bf16[128,4096]{1,0:T(8,128)(2,1)S(1)}) custom-call(s32[1]{0:T(128)} %bitcast.1.spot0_ref.refs_0_, s32[1]{0:T(128)} %bitcast.2.spot1_ref.refs_0_, bf16[128,768]{1,0:T(8,128)(2,1)S(1)} %get-tuple-element.90.refs_0_, bf16[128,768]{1,0:T(8,128)(2,1)S(1)} %collective-permute-done.3.refs_3_.refs_2_.refs_1_, ...), custom_call_target="tpu_custom_call" | custom-call | tf_op jit(solution)/shard_map/project/pallas_call | solution.py:38
  122.6 8.1 %collective-permute-done.15.refs_1_ = bf16[96,4096]{1,0:T(8,128)(2,1)S(1)} collective-permute-done((bf16[96,4096]{1,0:T(8,128)(2,1)S(1)}, bf16[96,4096]{1,0:T(8,128)(2,1)S(1)}, u32[]{:S(2)}, u32[]{:S(2)}) %collective-permute-start.15) | collective-permute-done | bytes 786464 | tf_op jit(solution)/shard_map/ppermute | solution.py:444
  131.1 1.3 collective-permute-start.18
  132.7 4.6 %collective-permute-start.19 = (bf16[96,4096]{1,0:T(8,128)(2,1)S(1)}, bf16[96,4096]{1,0:T(8,128)(2,1)S(1)}, u32[]{:S(2)}, u32[]{:S(2)}) collective-permute-start(bf16[96,4096]{1,0:T(8,128)(2,1)S(1)} %get-tuple-element.118.refs_3_.refs_5_), channel_id=1, source_target_pairs={{0,8},{10,2},{4,12},{14,6},{8,16},{18,10},{12,20},{22,14},{16,24},... | collective-permute-start | bytes 2359304 | tf_op jit(solution)/shard_map/ppermute | solution.py:444
  137.3 3.3 %lower.7.refs_5_ = bf16[128,768]{1,0:T(8,128)(2,1)S(1)} custom-call(bf16[96,4096]{1,0:T(8,128)(2,1)S(1)} %get-tuple-element.110.refs_0_, bf16[96,4096]{1,0:T(8,128)(2,1)S(1)} %get-tuple-element.112.refs_5_.refs_1_, bf16[96,4096]{1,0:T(8,128)(2,1)S(1)} %get-tuple-element.115.refs_2_, bf16[96,4096]{1,0:T(8,128)(2,1)S(1)} %get-tuple-element.118.refs_3_.refs_5_, ...), custom_call_target="tpu_custom_call" | custom-call | tf_op jit(solution)/shard_map/lower/pallas_call | solution.py:38
  140.7 9.8 %collective-permute-done.18.refs_1_ = bf16[96,4096]{1,0:T(8,128)(2,1)S(1)} collective-permute-done((bf16[96,4096]{1,0:T(8,128)(2,1)S(1)}, bf16[96,4096]{1,0:T(8,128)(2,1)S(1)}, u32[]{:S(2)}, u32[]{:S(2)}) %collective-permute-start.18) | collective-permute-done | bytes 786464 | tf_op jit(solution)/shard_map/ppermute | solution.py:444
  150.7 1.3 collective-permute-start.20
  152.0 2.2 collective-permute-done.19.refs_1_
  154.5 4.4 %collective-permute-start.21 = (bf16[96,4096]{1,0:T(8,128)(2,1)S(1)}, bf16[96,4096]{1,0:T(8,128)(2,1)S(1)}, u32[]{:S(2)}, u32[]{:S(2)}) collective-permute-start(bf16[96,4096]{1,0:T(8,128)(2,1)S(1)} %get-tuple-element.126.refs_4_.refs_1_), channel_id=1, source_target_pairs={{0,8},{10,2},{4,12},{14,6},{8,16},{18,10},{12,20},{22,14},{16,24},... | collective-permute-start | bytes 2359304 | tf_op jit(solution)/shard_map/ppermute | solution.py:444
  160.2 5.6 %project.9 = (bf16[128,4096]{1,0:T(8,128)(2,1)S(1)}, bf16[128,4096]{1,0:T(8,128)(2,1)S(1)}) custom-call(s32[1]{0:T(128)} %bitcast.1.spot0_ref.refs_0_, s32[1]{0:T(128)} %bitcast.2.spot1_ref.refs_0_, bf16[128,768]{1,0:T(8,128)(2,1)S(1)} %get-tuple-element.90.refs_0_, bf16[128,768]{1,0:T(8,128)(2,1)S(1)} %collective-permute-done.6.refs_4_.refs_2_.refs_1_, ...), custom_call_target="tpu_custom_call" | custom-call | tf_op jit(solution)/shard_map/project/pallas_call | solution.py:38
  165.8 3.4 %collective-permute-done.20.refs_1_ = bf16[96,4096]{1,0:T(8,128)(2,1)S(1)} collective-permute-done((bf16[96,4096]{1,0:T(8,128)(2,1)S(1)}, bf16[96,4096]{1,0:T(8,128)(2,1)S(1)}, u32[]{:S(2)}, u32[]{:S(2)}) %collective-permute-start.20) | collective-permute-done | bytes 786464 | tf_op jit(solution)/shard_map/ppermute | solution.py:444
  169.5 1.3 collective-permute-start.24
  176.9 4.4 %collective-permute-start.25 = (bf16[96,4096]{1,0:T(8,128)(2,1)S(1)}, bf16[96,4096]{1,0:T(8,128)(2,1)S(1)}, u32[]{:S(2)}, u32[]{:S(2)}) collective-permute-start(bf16[96,4096]{1,0:T(8,128)(2,1)S(1)} %get-tuple-element.132.refs_3_.refs_5_), channel_id=1, source_target_pairs={{0,8},{10,2},{4,12},{14,6},{8,16},{18,10},{12,20},{22,14},{16,24},... | collective-permute-start | bytes 2359304 | tf_op jit(solution)/shard_map/ppermute | solution.py:444
  181.5 3.3 %lower.8.refs_5_ = bf16[128,768]{1,0:T(8,128)(2,1)S(1)} custom-call(bf16[96,4096]{1,0:T(8,128)(2,1)S(1)} %get-tuple-element.124.refs_0_, bf16[96,4096]{1,0:T(8,128)(2,1)S(1)} %get-tuple-element.126.refs_4_.refs_1_, bf16[96,4096]{1,0:T(8,128)(2,1)S(1)} %get-tuple-element.129.refs_2_, bf16[96,4096]{1,0:T(8,128)(2,1)S(1)} %get-tuple-element.132.refs_3_.refs_5_, ...), custom_call_target="tpu_custom_call" | custom-call | tf_op jit(solution)/shard_map/lower/pallas_call | solution.py:38
  184.8 1.4 collective-permute-start.22
  187.3 1.3 collective-permute-start.26
  188.6 2.0 collective-permute-done.22
  190.6 8.0 %collective-permute-done.25.refs_1_ = bf16[96,4096]{1,0:T(8,128)(2,1)S(1)} collective-permute-done((bf16[96,4096]{1,0:T(8,128)(2,1)S(1)}, bf16[96,4096]{1,0:T(8,128)(2,1)S(1)}, u32[]{:S(2)}, u32[]{:S(2)}) %collective-permute-start.25) | collective-permute-done | bytes 786464 | tf_op jit(solution)/shard_map/ppermute | solution.py:444
  198.9 4.4 %collective-permute-start.27 = (bf16[32,4096]{1,0:T(8,128)(2,1)S(1)}, bf16[32,4096]{1,0:T(8,128)(2,1)S(1)}, u32[]{:S(2)}, u32[]{:S(2)}) collective-permute-start(bf16[32,4096]{1,0:T(8,128)(2,1)S(1)} %get-tuple-element.141.refs_1_), channel_id=1, source_target_pairs={{0,8},{10,2},{4,12},{14,6},{8,16},{18,10},{12,20},{22,14},{16,24},... | collective-permute-start | bytes 786440 | tf_op jit(solution)/shard_map/ppermute | solution.py:444
  203.8 3.4 %collective-permute-done.27.refs_1_ = bf16[32,4096]{1,0:T(8,128)(2,1)S(1)} collective-permute-done((bf16[32,4096]{1,0:T(8,128)(2,1)S(1)}, bf16[32,4096]{1,0:T(8,128)(2,1)S(1)}, u32[]{:S(2)}, u32[]{:S(2)}) %collective-permute-start.27) | collective-permute-done | bytes 262176 | tf_op jit(solution)/shard_map/ppermute | solution.py:444
  207.3 3.3 %lower.9.refs_1_ = bf16[128,768]{1,0:T(8,128)(2,1)S(1)} custom-call(bf16[96,4096]{1,0:T(8,128)(2,1)S(1)} %get-tuple-element.139.refs_0_, bf16[32,4096]{1,0:T(8,128)(2,1)S(1)} %get-tuple-element.141.refs_1_, bf16[32,4096]{1,0:T(8,128)(2,1)S(1)} %get-tuple-element.143.refs_2_, bf16[32,4096]{1,0:T(8,128)(2,1)S(1)} %combine.51.refs_3_.refs_5_, ...), custom_call_target="tpu_custom_call" | custom-call | tf_op jit(solution)/shard_map/lower/pallas_call | solution.py:38
  210.6 1.3 collective-permute-start.28
  212.0 1.3 collective-permute-start.30
  213.3 5.0 %collective-permute-start.31 = (bf16[32,4096]{1,0:T(8,128)(2,1)S(1)}, bf16[32,4096]{1,0:T(8,128)(2,1)S(1)}, u32[]{:S(2)}, u32[]{:S(2)}) collective-permute-start(bf16[32,4096]{1,0:T(8,128)(2,1)S(1)} %combine.51.refs_3_.refs_5_), channel_id=1, source_target_pairs={{0,8},{10,2},{4,12},{14,6},{8,16},{18,10},{12,20},{22,14},{16,24},... | collective-permute-start | bytes 786440 | tf_op jit(solution)/shard_map/ppermute | solution.py:444
  218.5 2.2 collective-permute-done.30.refs_0_
  220.8 1.3 collective-permute-start.32
  222.2 4.5 %collective-permute-start.33 = (bf16[32,4096]{1,0:T(8,128)(2,1)S(1)}, bf16[32,4096]{1,0:T(8,128)(2,1)S(1)}, u32[]{:S(2)}, u32[]{:S(2)}) collective-permute-start(bf16[32,4096]{1,0:T(8,128)(2,1)S(1)} %combine.53.refs_1_), channel_id=1, source_target_pairs={{0,8},{10,2},{4,12},{14,6},{8,16},{18,10},{12,20},{22,14},{16,24},... | collective-permute-start | bytes 786440 | tf_op jit(solution)/shard_map/ppermute | solution.py:444
  226.8 4.0 %collective-permute-done.32.refs_0_ = bf16[32,4096]{1,0:T(8,128)(2,1)S(1)} collective-permute-done((bf16[32,4096]{1,0:T(8,128)(2,1)S(1)}, bf16[32,4096]{1,0:T(8,128)(2,1)S(1)}, u32[]{:S(2)}, u32[]{:S(2)}) %collective-permute-start.32) | collective-permute-done | bytes 262176 | tf_op jit(solution)/shard_map/ppermute | solution.py:444
  230.9 3.3 %lower.10.refs_1_ = bf16[128,768]{1,0:T(8,128)(2,1)S(1)} custom-call(bf16[32,4096]{1,0:T(8,128)(2,1)S(1)} %combine.52.refs_0_, bf16[32,4096]{1,0:T(8,128)(2,1)S(1)} %combine.53.refs_1_, bf16[32,4096]{1,0:T(8,128)(2,1)S(1)} %combine.54.refs_2_, bf16[32,4096]{1,0:T(8,128)(2,1)S(1)} %combine.55.refs_3_.refs_5_, bf16[4096,768]{1,0:T(8,128)(2,1)} %bitcast.30, ...), custom_call_target="tpu_custom_call" | custom-call | tf_op jit(solution)/shard_map/lower/pallas_call | solution.py:38
  235.0 1.3 collective-permute-start.29
  237.6 5.1 %collective-permute-start.37 = (bf16[32,4096]{1,0:T(8,128)(2,1)S(1)}, bf16[32,4096]{1,0:T(8,128)(2,1)S(1)}, u32[]{:S(2)}, u32[]{:S(2)}) collective-permute-start(bf16[32,4096]{1,0:T(8,128)(2,1)S(1)} %combine.55.refs_3_.refs_5_), channel_id=1, source_target_pairs={{0,8},{10,2},{4,12},{14,6},{8,16},{18,10},{12,20},{22,14},{16,24},... | collective-permute-start | bytes 786440 | tf_op jit(solution)/shard_map/ppermute | solution.py:444
  243.0 2.0 collective-permute-done.36.refs_0_
  245.0 1.3 collective-permute-done.37.refs_0_
  246.4 3.1 %collective-permute-done.35.refs_7_.refs_3_ = bf16[128,768]{1,0:T(8,128)(2,1)S(1)} collective-permute-done((bf16[128,768]{1,0:T(8,128)(2,1)S(1)}, bf16[128,768]{1,0:T(8,128)(2,1)S(1)}, u32[]{:S(2)}, u32[]{:S(2)}) %collective-permute-start.35) | collective-permute-done | bytes 196640 | tf_op jit(solution)/shard_map/ppermute | solution.py:416
  249.5 3.3 %lower.11 = bf16[64,768]{1,0:T(8,128)(2,1)S(1)} custom-call(bf16[32,4096]{1,0:T(8,128)(2,1)S(1)} %combine.56.refs_0_, bf16[32,4096]{1,0:T(8,128)(2,1)S(1)} %combine.57.refs_1_.refs_3_, bf16[4096,768]{1,0:T(8,128)(2,1)} %bitcast.31, bf16[32,4096]{1,0:T(8,128)(2,1)S(1)} %combine.57.refs_1_.refs_3_, bf16[64,768]{1,0:T(8,128)(2,1)S(1)} %pad_maximum_fusion.3.refs_4_.refs_0_, ...), custom_call_target="tpu_custom_call" | custom-call | tf_op jit(solution)/shard_map/lower/pallas_call | solution.py:38
  252.8 1.4 collective-permute-start.38
  254.4 3.1 %collective-permute-done.38 = bf16[64,768]{1,0:T(8,128)(2,1)S(1)} collective-permute-done((bf16[64,768]{1,0:T(8,128)(2,1)S(1)}, bf16[64,768]{1,0:T(8,128)(2,1)S(1)}, u32[]{:S(2)}, u32[]{:S(2)}) %collective-permute-start.38) | collective-permute-done | bytes 98336 | tf_op jit(solution)/shard_map/ppermute | solution.py:369
  257.6 3.0 %mix.1 = bf16[256,768]{1,0:T(8,128)(2,1)} custom-call(s32[2,256]{1,0:T(2,128)S(1)} %get-tuple-element.82.place_ref, f32[256,2]{1,0:T(8,128)S(1)} %copy.7.gate_ref, bf16[64,768]{1,0:T(8,128)(2,1)S(1)} %pad_maximum_fusion.3.refs_4_.refs_0_, bf16[128,768]{1,0:T(8,128)(2,1)S(1)} %collective-permute-done.23.refs_5_.refs_1_, ...), custom_call_target="tpu_custom_call" | custom-call | tf_op jit(solution)/shard_map/mix/pallas_call | solution.py:38
  (88 shorter events, 16.5 us)
Async XLA Ops:
  0.0 1.0 copy-start
  1.0 0.7 copy-start.1
  7.4 16.3 %collective-permute-start.4 = (bf16[64,4096]{1,0:T(8,128)(2,1)S(1)}, bf16[64,4096]{1,0:T(8,128)(2,1)S(1)}, u32[]{:S(2)}, u32[]{:S(2)}) collective-permute-start(bf16[64,4096]{1,0:T(8,128)(2,1)S(1)} %combine.31), channel_id=1, source_target_pairs={{0,8},{10,2},{4,12},{14,6},{8,16},{18,10},{12,20},{22,14},{16,24},... | collective-permute-start | bytes 1572872 | tf_op jit(solution)/shard_map/ppermute | solution.py:444
  12.5 15.9 %collective-permute-start = (bf16[64,4096]{1,0:T(8,128)(2,1)S(1)}, bf16[64,4096]{1,0:T(8,128)(2,1)S(1)}, u32[]{:S(2)}, u32[]{:S(2)}) collective-permute-start(bf16[64,4096]{1,0:T(8,128)(2,1)S(1)} %get-tuple-element.89.refs_4_), channel_id=1, source_target_pairs={{8,0},{2,10},{12,4},{6,14},{16,8},{10,18},{20,12},{14,22},{24,16},... | collective-permute-start | bytes 1572872 | tf_op jit(solution)/shard_map/ppermute | solution.py:444
  13.8 1.5 collective-permute-start.1
  23.9 16.4 %collective-permute-start.5 = (bf16[64,4096]{1,0:T(8,128)(2,1)S(1)}, bf16[64,4096]{1,0:T(8,128)(2,1)S(1)}, u32[]{:S(2)}, u32[]{:S(2)}) collective-permute-start(bf16[64,4096]{1,0:T(8,128)(2,1)S(1)} %combine.32), channel_id=1, source_target_pairs={{0,8},{10,2},{4,12},{14,6},{8,16},{18,10},{12,20},{22,14},{16,24},... | collective-permute-start | bytes 1572872 | tf_op jit(solution)/shard_map/ppermute | solution.py:444
  28.6 22.0 %collective-permute-start.2 = (bf16[64,4096]{1,0:T(8,128)(2,1)S(1)}, bf16[64,4096]{1,0:T(8,128)(2,1)S(1)}, u32[]{:S(2)}, u32[]{:S(2)}) collective-permute-start(bf16[64,4096]{1,0:T(8,128)(2,1)S(1)} %combine.30), channel_id=1, source_target_pairs={{8,0},{2,10},{12,4},{6,14},{16,8},{10,18},{20,12},{14,22},{24,16},... | collective-permute-start | bytes 1572872 | tf_op jit(solution)/shard_map/ppermute | solution.py:444
  29.9 7.3 %collective-permute-start.3 = (bf16[128,768]{1,0:T(8,128)(2,1)S(1)}, bf16[128,768]{1,0:T(8,128)(2,1)S(1)}, u32[]{:S(2)}, u32[]{:S(2)}) collective-permute-start(bf16[128,768]{1,0:T(8,128)(2,1)S(1)} %get-tuple-element.94), channel_id=1, source_target_pairs={{0,4},{2,6},{4,0},{6,2},{1,5},{3,7},{5,1},{7,3},{8,12},{10,14},{12... | collective-permute-start | bytes 589832 | tf_op jit(solution)/shard_map/ppermute | solution.py:446
  31.3 7.7 %collective-permute-start.6 = (bf16[128,768]{1,0:T(8,128)(2,1)S(1)}, bf16[128,768]{1,0:T(8,128)(2,1)S(1)}, u32[]{:S(2)}, u32[]{:S(2)}) collective-permute-start(bf16[128,768]{1,0:T(8,128)(2,1)S(1)} %get-tuple-element.95), channel_id=1, source_target_pairs={{0,6},{2,4},{4,2},{6,0},{1,7},{3,5},{5,3},{7,1},{8,14},{10,12},{12... | collective-permute-start | bytes 589832 | tf_op jit(solution)/shard_map/ppermute | solution.py:446
  40.5 11.5 %collective-permute-start.8 = (bf16[64,4096]{1,0:T(8,128)(2,1)S(1)}, bf16[64,4096]{1,0:T(8,128)(2,1)S(1)}, u32[]{:S(2)}, u32[]{:S(2)}) collective-permute-start(bf16[64,4096]{1,0:T(8,128)(2,1)S(1)} %combine.33.refs_5_), channel_id=1, source_target_pairs={{0,8},{10,2},{4,12},{14,6},{8,16},{18,10},{12,20},{22,14},{16,24},... | collective-permute-start | bytes 1572872 | tf_op jit(solution)/shard_map/ppermute | solution.py:444
  50.8 16.0 %collective-permute-start.7 = (bf16[64,4096]{1,0:T(8,128)(2,1)S(1)}, bf16[64,4096]{1,0:T(8,128)(2,1)S(1)}, u32[]{:S(2)}, u32[]{:S(2)}) collective-permute-start(bf16[64,4096]{1,0:T(8,128)(2,1)S(1)} %combine.34), channel_id=1, source_target_pairs={{8,0},{2,10},{12,4},{6,14},{16,8},{10,18},{20,12},{14,22},{24,16},... | collective-permute-start | bytes 1572872 | tf_op jit(solution)/shard_map/ppermute | solution.py:444
  52.4 16.0 %collective-permute-start.9 = (bf16[64,4096]{1,0:T(8,128)(2,1)S(1)}, bf16[64,4096]{1,0:T(8,128)(2,1)S(1)}, u32[]{:S(2)}, u32[]{:S(2)}) collective-permute-start(bf16[64,4096]{1,0:T(8,128)(2,1)S(1)} %get-tuple-element.100), channel_id=1, source_target_pairs={{0,8},{10,2},{4,12},{14,6},{8,16},{18,10},{12,20},{22,14},{16,24},... | collective-permute-start | bytes 1572872 | tf_op jit(solution)/shard_map/ppermute | solution.py:444
  67.1 21.8 %collective-permute-start.10 = (bf16[96,4096]{1,0:T(8,128)(2,1)S(1)}, bf16[96,4096]{1,0:T(8,128)(2,1)S(1)}, u32[]{:S(2)}, u32[]{:S(2)}) collective-permute-start(bf16[96,4096]{1,0:T(8,128)(2,1)S(1)} %get-tuple-element.99.refs_0_), channel_id=1, source_target_pairs={{8,0},{2,10},{12,4},{6,14},{16,8},{10,18},{20,12},{14,22},{24,16},... | collective-permute-start | bytes 2359304 | tf_op jit(solution)/shard_map/ppermute | solution.py:444
  68.7 21.8 %collective-permute-start.11 = (bf16[96,4096]{1,0:T(8,128)(2,1)S(1)}, bf16[96,4096]{1,0:T(8,128)(2,1)S(1)}, u32[]{:S(2)}, u32[]{:S(2)}) collective-permute-start(bf16[96,4096]{1,0:T(8,128)(2,1)S(1)} %get-tuple-element.102.refs_5_.refs_1_), channel_id=1, source_target_pairs={{0,8},{10,2},{4,12},{14,6},{8,16},{18,10},{12,20},{22,14},{16,24},... | collective-permute-start | bytes 2359304 | tf_op jit(solution)/shard_map/ppermute | solution.py:444
  89.2 21.0 %collective-permute-start.13 = (bf16[96,4096]{1,0:T(8,128)(2,1)S(1)}, bf16[96,4096]{1,0:T(8,128)(2,1)S(1)}, u32[]{:S(2)}, u32[]{:S(2)}) collective-permute-start(bf16[96,4096]{1,0:T(8,128)(2,1)S(1)} %get-tuple-element.105.refs_2_), channel_id=1, source_target_pairs={{8,0},{2,10},{12,4},{6,14},{16,8},{10,18},{20,12},{14,22},{24,16},... | collective-permute-start | bytes 2359304 | tf_op jit(solution)/shard_map/ppermute | solution.py:444
  90.9 21.0 %collective-permute-start.14 = (bf16[96,4096]{1,0:T(8,128)(2,1)S(1)}, bf16[96,4096]{1,0:T(8,128)(2,1)S(1)}, u32[]{:S(2)}, u32[]{:S(2)}) collective-permute-start(bf16[96,4096]{1,0:T(8,128)(2,1)S(1)} %get-tuple-element.108.refs_3_.refs_5_), channel_id=1, source_target_pairs={{0,8},{10,2},{4,12},{14,6},{8,16},{18,10},{12,20},{22,14},{16,24},... | collective-permute-start | bytes 2359304 | tf_op jit(solution)/shard_map/ppermute | solution.py:444
  110.6 20.2 %collective-permute-start.15 = (bf16[96,4096]{1,0:T(8,128)(2,1)S(1)}, bf16[96,4096]{1,0:T(8,128)(2,1)S(1)}, u32[]{:S(2)}, u32[]{:S(2)}) collective-permute-start(bf16[96,4096]{1,0:T(8,128)(2,1)S(1)} %get-tuple-element.110.refs_0_), channel_id=1, source_target_pairs={{8,0},{2,10},{12,4},{6,14},{16,8},{10,18},{20,12},{14,22},{24,16},... | collective-permute-start | bytes 2359304 | tf_op jit(solution)/shard_map/ppermute | solution.py:444
  112.2 20.2 %collective-permute-start.16 = (bf16[96,4096]{1,0:T(8,128)(2,1)S(1)}, bf16[96,4096]{1,0:T(8,128)(2,1)S(1)}, u32[]{:S(2)}, u32[]{:S(2)}) collective-permute-start(bf16[96,4096]{1,0:T(8,128)(2,1)S(1)} %get-tuple-element.112.refs_5_.refs_1_), channel_id=1, source_target_pairs={{0,8},{10,2},{4,12},{14,6},{8,16},{18,10},{12,20},{22,14},{16,24},... | collective-permute-start | bytes 2359304 | tf_op jit(solution)/shard_map/ppermute | solution.py:444
  131.1 19.3 %collective-permute-start.18 = (bf16[96,4096]{1,0:T(8,128)(2,1)S(1)}, bf16[96,4096]{1,0:T(8,128)(2,1)S(1)}, u32[]{:S(2)}, u32[]{:S(2)}) collective-permute-start(bf16[96,4096]{1,0:T(8,128)(2,1)S(1)} %get-tuple-element.115.refs_2_), channel_id=1, source_target_pairs={{8,0},{2,10},{12,4},{6,14},{16,8},{10,18},{20,12},{14,22},{24,16},... | collective-permute-start | bytes 2359304 | tf_op jit(solution)/shard_map/ppermute | solution.py:444
  132.7 21.5 %collective-permute-start.19 = (bf16[96,4096]{1,0:T(8,128)(2,1)S(1)}, bf16[96,4096]{1,0:T(8,128)(2,1)S(1)}, u32[]{:S(2)}, u32[]{:S(2)}) collective-permute-start(bf16[96,4096]{1,0:T(8,128)(2,1)S(1)} %get-tuple-element.118.refs_3_.refs_5_), channel_id=1, source_target_pairs={{0,8},{10,2},{4,12},{14,6},{8,16},{18,10},{12,20},{22,14},{16,24},... | collective-permute-start | bytes 2359304 | tf_op jit(solution)/shard_map/ppermute | solution.py:444
  150.7 18.4 %collective-permute-start.20 = (bf16[96,4096]{1,0:T(8,128)(2,1)S(1)}, bf16[96,4096]{1,0:T(8,128)(2,1)S(1)}, u32[]{:S(2)}, u32[]{:S(2)}) collective-permute-start(bf16[96,4096]{1,0:T(8,128)(2,1)S(1)} %get-tuple-element.124.refs_0_), channel_id=1, source_target_pairs={{8,0},{2,10},{12,4},{6,14},{16,8},{10,18},{20,12},{14,22},{24,16},... | collective-permute-start | bytes 2359304 | tf_op jit(solution)/shard_map/ppermute | solution.py:444
  154.5 22.1 %collective-permute-start.21 = (bf16[96,4096]{1,0:T(8,128)(2,1)S(1)}, bf16[96,4096]{1,0:T(8,128)(2,1)S(1)}, u32[]{:S(2)}, u32[]{:S(2)}) collective-permute-start(bf16[96,4096]{1,0:T(8,128)(2,1)S(1)} %get-tuple-element.126.refs_4_.refs_1_), channel_id=1, source_target_pairs={{0,8},{10,2},{4,12},{14,6},{8,16},{18,10},{12,20},{22,14},{16,24},... | collective-permute-start | bytes 2359304 | tf_op jit(solution)/shard_map/ppermute | solution.py:444
  159.0 15.9 %collective-permute-start.12 = (bf16[128,768]{1,0:T(8,128)(2,1)S(1)}, bf16[128,768]{1,0:T(8,128)(2,1)S(1)}, u32[]{:S(2)}, u32[]{:S(2)}) collective-permute-start(bf16[128,768]{1,0:T(8,128)(2,1)S(1)} %lower.6.refs_5_), channel_id=1, source_target_pairs={{0,1},{1,0},{2,3},{3,2},{4,5},{5,4},{6,7},{7,6},{8,9},{9,8},{10,11... | collective-permute-start | bytes 589832 | tf_op jit(solution)/shard_map/ppermute | solution.py:369
  169.5 17.5 %collective-permute-start.24 = (bf16[96,4096]{1,0:T(8,128)(2,1)S(1)}, bf16[96,4096]{1,0:T(8,128)(2,1)S(1)}, u32[]{:S(2)}, u32[]{:S(2)}) collective-permute-start(bf16[96,4096]{1,0:T(8,128)(2,1)S(1)} %get-tuple-element.129.refs_2_), channel_id=1, source_target_pairs={{8,0},{2,10},{12,4},{6,14},{16,8},{10,18},{20,12},{14,22},{24,16},... | collective-permute-start | bytes 2359304 | tf_op jit(solution)/shard_map/ppermute | solution.py:444
  174.9 6.5 %collective-permute-start.17 = (bf16[128,768]{1,0:T(8,128)(2,1)S(1)}, bf16[128,768]{1,0:T(8,128)(2,1)S(1)}, u32[]{:S(2)}, u32[]{:S(2)}) collective-permute-start(bf16[128,768]{1,0:T(8,128)(2,1)S(1)} %lower.7.refs_5_), channel_id=1, source_target_pairs={{0,1},{1,0},{2,3},{3,2},{4,5},{5,4},{6,7},{7,6},{8,9},{9,8},{10,11... | collective-permute-start | bytes 589832 | tf_op jit(solution)/shard_map/ppermute | solution.py:369
  176.9 21.7 %collective-permute-start.25 = (bf16[96,4096]{1,0:T(8,128)(2,1)S(1)}, bf16[96,4096]{1,0:T(8,128)(2,1)S(1)}, u32[]{:S(2)}, u32[]{:S(2)}) collective-permute-start(bf16[96,4096]{1,0:T(8,128)(2,1)S(1)} %get-tuple-element.132.refs_3_.refs_5_), channel_id=1, source_target_pairs={{0,8},{10,2},{4,12},{14,6},{8,16},{18,10},{12,20},{22,14},{16,24},... | collective-permute-start | bytes 2359304 | tf_op jit(solution)/shard_map/ppermute | solution.py:444
  184.8 5.7 %collective-permute-start.22 = (bf16[128,768]{1,0:T(8,128)(2,1)S(1)}, bf16[128,768]{1,0:T(8,128)(2,1)S(1)}, u32[]{:S(2)}, u32[]{:S(2)}) collective-permute-start(bf16[128,768]{1,0:T(8,128)(2,1)S(1)} %lower.8.refs_5_), channel_id=1, source_target_pairs={{0,1},{1,0},{2,3},{3,2},{4,5},{5,4},{6,7},{7,6},{8,9},{9,8},{10,11... | collective-permute-start | bytes 589832 | tf_op jit(solution)/shard_map/ppermute | solution.py:369
  187.3 16.1 %collective-permute-start.26 = (bf16[96,4096]{1,0:T(8,128)(2,1)S(1)}, bf16[96,4096]{1,0:T(8,128)(2,1)S(1)}, u32[]{:S(2)}, u32[]{:S(2)}) collective-permute-start(bf16[96,4096]{1,0:T(8,128)(2,1)S(1)} %get-tuple-element.139.refs_0_), channel_id=1, source_target_pairs={{8,0},{2,10},{12,4},{6,14},{16,8},{10,18},{20,12},{14,22},{24,16},... | collective-permute-start | bytes 2359304 | tf_op jit(solution)/shard_map/ppermute | solution.py:444
  198.9 8.3 %collective-permute-start.27 = (bf16[32,4096]{1,0:T(8,128)(2,1)S(1)}, bf16[32,4096]{1,0:T(8,128)(2,1)S(1)}, u32[]{:S(2)}, u32[]{:S(2)}) collective-permute-start(bf16[32,4096]{1,0:T(8,128)(2,1)S(1)} %get-tuple-element.141.refs_1_), channel_id=1, source_target_pairs={{0,8},{10,2},{4,12},{14,6},{8,16},{18,10},{12,20},{22,14},{16,24},... | collective-permute-start | bytes 786440 | tf_op jit(solution)/shard_map/ppermute | solution.py:444
  210.6 7.8 %collective-permute-start.28 = (bf16[128,768]{1,0:T(8,128)(2,1)S(1)}, bf16[128,768]{1,0:T(8,128)(2,1)S(1)}, u32[]{:S(2)}, u32[]{:S(2)}) collective-permute-start(bf16[128,768]{1,0:T(8,128)(2,1)S(1)} %lower.9.refs_1_), channel_id=1, source_target_pairs={{0,1},{1,0},{2,3},{3,2},{4,5},{5,4},{6,7},{7,6},{8,9},{9,8},{10,11... | collective-permute-start | bytes 589832 | tf_op jit(solution)/shard_map/ppermute | solution.py:369
  212.0 8.7 %collective-permute-start.30 = (bf16[32,4096]{1,0:T(8,128)(2,1)S(1)}, bf16[32,4096]{1,0:T(8,128)(2,1)S(1)}, u32[]{:S(2)}, u32[]{:S(2)}) collective-permute-start(bf16[32,4096]{1,0:T(8,128)(2,1)S(1)} %get-tuple-element.143.refs_2_), channel_id=1, source_target_pairs={{8,0},{2,10},{12,4},{6,14},{16,8},{10,18},{20,12},{14,22},{24,16},... | collective-permute-start | bytes 786440 | tf_op jit(solution)/shard_map/ppermute | solution.py:444
  213.3 8.9 %collective-permute-start.31 = (bf16[32,4096]{1,0:T(8,128)(2,1)S(1)}, bf16[32,4096]{1,0:T(8,128)(2,1)S(1)}, u32[]{:S(2)}, u32[]{:S(2)}) collective-permute-start(bf16[32,4096]{1,0:T(8,128)(2,1)S(1)} %combine.51.refs_3_.refs_5_), channel_id=1, source_target_pairs={{0,8},{10,2},{4,12},{14,6},{8,16},{18,10},{12,20},{22,14},{16,24},... | collective-permute-start | bytes 786440 | tf_op jit(solution)/shard_map/ppermute | solution.py:444
  218.4 28.1 %collective-permute-start.23 = (bf16[128,768]{1,0:T(8,128)(2,1)S(1)}, bf16[128,768]{1,0:T(8,128)(2,1)S(1)}, u32[]{:S(2)}, u32[]{:S(2)}) collective-permute-start(bf16[128,768]{1,0:T(8,128)(2,1)S(1)} %pad_maximum_fusion), channel_id=1, source_target_pairs={{0,2},{2,0},{4,6},{6,4},{1,3},{3,1},{5,7},{7,5},{8,10},{10,8},{12,... | collective-permute-start | bytes 589832 | tf_op jit(solution)/shard_map/ppermute | solution.py:416
  220.8 10.0 %collective-permute-start.32 = (bf16[32,4096]{1,0:T(8,128)(2,1)S(1)}, bf16[32,4096]{1,0:T(8,128)(2,1)S(1)}, u32[]{:S(2)}, u32[]{:S(2)}) collective-permute-start(bf16[32,4096]{1,0:T(8,128)(2,1)S(1)} %combine.52.refs_0_), channel_id=1, source_target_pairs={{8,0},{2,10},{12,4},{6,14},{16,8},{10,18},{20,12},{14,22},{24,16},... | collective-permute-start | bytes 786440 | tf_op jit(solution)/shard_map/ppermute | solution.py:444
  222.2 8.6 %collective-permute-start.33 = (bf16[32,4096]{1,0:T(8,128)(2,1)S(1)}, bf16[32,4096]{1,0:T(8,128)(2,1)S(1)}, u32[]{:S(2)}, u32[]{:S(2)}) collective-permute-start(bf16[32,4096]{1,0:T(8,128)(2,1)S(1)} %combine.53.refs_1_), channel_id=1, source_target_pairs={{0,8},{10,2},{4,12},{14,6},{8,16},{18,10},{12,20},{22,14},{16,24},... | collective-permute-start | bytes 786440 | tf_op jit(solution)/shard_map/ppermute | solution.py:444
  234.3 8.5 %collective-permute-start.34 = (bf16[128,768]{1,0:T(8,128)(2,1)S(1)}, bf16[128,768]{1,0:T(8,128)(2,1)S(1)}, u32[]{:S(2)}, u32[]{:S(2)}) collective-permute-start(bf16[128,768]{1,0:T(8,128)(2,1)S(1)} %lower.10.refs_1_), channel_id=1, source_target_pairs={{0,1},{1,0},{2,3},{3,2},{4,5},{5,4},{6,7},{7,6},{8,9},{9,8},{10,11... | collective-permute-start | bytes 589832 | tf_op jit(solution)/shard_map/ppermute | solution.py:369
  235.0 19.3 %copy-start.2 = (f32[256,2]{0,1:T(2,128)S(1)}, f32[256,2]{0,1:T(2,128)}, u32[]{:S(2)}) copy-start(f32[256,2]{0,1:T(2,128)} %param.8) | copy-start | bytes 6148
  235.0 11.4 %collective-permute-start.29 = (bf16[128,768]{1,0:T(8,128)(2,1)S(1)}, bf16[128,768]{1,0:T(8,128)(2,1)S(1)}, u32[]{:S(2)}, u32[]{:S(2)}) collective-permute-start(bf16[128,768]{1,0:T(8,128)(2,1)S(1)} %pad_maximum_fusion.1), channel_id=1, source_target_pairs={{0,4},{2,6},{4,0},{6,2},{1,5},{3,7},{5,1},{7,3},{8,12},{10,14},{12... | collective-permute-start | bytes 589832 | tf_op jit(solution)/shard_map/ppermute | solution.py:416
  236.3 8.7 %collective-permute-start.36 = (bf16[32,4096]{1,0:T(8,128)(2,1)S(1)}, bf16[32,4096]{1,0:T(8,128)(2,1)S(1)}, u32[]{:S(2)}, u32[]{:S(2)}) collective-permute-start(bf16[32,4096]{1,0:T(8,128)(2,1)S(1)} %combine.54.refs_2_), channel_id=1, source_target_pairs={{8,0},{2,10},{12,4},{6,14},{16,8},{10,18},{20,12},{14,22},{24,16},... | collective-permute-start | bytes 786440 | tf_op jit(solution)/shard_map/ppermute | solution.py:444
  237.6 8.7 %collective-permute-start.37 = (bf16[32,4096]{1,0:T(8,128)(2,1)S(1)}, bf16[32,4096]{1,0:T(8,128)(2,1)S(1)}, u32[]{:S(2)}, u32[]{:S(2)}) collective-permute-start(bf16[32,4096]{1,0:T(8,128)(2,1)S(1)} %combine.55.refs_3_.refs_5_), channel_id=1, source_target_pairs={{0,8},{10,2},{4,12},{14,6},{8,16},{18,10},{12,20},{22,14},{16,24},... | collective-permute-start | bytes 786440 | tf_op jit(solution)/shard_map/ppermute | solution.py:444
  242.9 6.6 %collective-permute-start.35 = (bf16[128,768]{1,0:T(8,128)(2,1)S(1)}, bf16[128,768]{1,0:T(8,128)(2,1)S(1)}, u32[]{:S(2)}, u32[]{:S(2)}) collective-permute-start(bf16[128,768]{1,0:T(8,128)(2,1)S(1)} %pad_maximum_fusion.2), channel_id=1, source_target_pairs={{0,6},{2,4},{4,2},{6,0},{1,7},{3,5},{5,3},{7,1},{8,14},{10,12},{12... | collective-permute-start | bytes 589832 | tf_op jit(solution)/shard_map/ppermute | solution.py:416
  252.8 4.7 %collective-permute-start.38 = (bf16[64,768]{1,0:T(8,128)(2,1)S(1)}, bf16[64,768]{1,0:T(8,128)(2,1)S(1)}, u32[]{:S(2)}, u32[]{:S(2)}) collective-permute-start(bf16[64,768]{1,0:T(8,128)(2,1)S(1)} %lower.11), channel_id=1, source_target_pairs={{0,1},{1,0},{2,3},{3,2},{4,5},{5,4},{6,7},{7,6},{8,9},{9,8},{10,11... | collective-permute-start | bytes 294920 | tf_op jit(solution)/shard_map/ppermute | solution.py:369
